TPU v7x, 256 devices: a whole 4x4x8 slice. The times are simulated.
256 devices in a mesh: view: 4 (over x_lo, core), seq: 64 (over y, z, x_hi).
Axes of the slice: x: 4 (x_hi: 2, x_lo: 2; x = x_hi * 2 + x_lo), y: 4, z: 8, core: 2. Of those that a mesh axis runs over, the one named last changes fastest.
Arguments:
- hidden_in: bfloat16 [4, 8192, 2048], P('view', 'seq'), may hold values from -6 to 6
- queries: bfloat16 [4, 8192, 2048], P('view', 'seq'), may hold values from -100 to 100
- keys: bfloat16 [4, 8192, 2048], P('view', 'seq'), may hold values from -4 to 4
- values: bfloat16 [4, 8192, 2048], P('view', 'seq'), may hold values from -6 to 6
- out_weight: bfloat16 [2048, 2048], replicated, may hold values from -0.125 to 0.125
- gate: bfloat16 [4, 2048], P('view'), may hold values from 0.5 to 1.5
Outputs:
- updated: bfloat16 [4, 8192, 2048], P('view', 'seq')
All inputs are finite; a program needn't handle non-finite values.
Results may differ from a plain program's by a relative error of at most 0.015.
Values may be sent and summed in bfloat16 or wider, within the bound.
No kernel may reach another device: no remote copies, remote signals or barrier semaphores. Data moves between devices by JAX's collectives and lax.ppermute only.
A program may use at most 128 MiB of HBM per device.

v0:
```python
import math

import jax
import jax.numpy as jnp
from jax import lax
from jax.sharding import PartitionSpec as P

HEADS = 16
HEAD_DIM = 128


def key_blocks(rows_array):
    count_rows = rows_array.shape[0]
    block_rows = math.gcd(count_rows, 1024)
    return rows_array.reshape(
        count_rows // block_rows, block_rows, rows_array.shape[1], rows_array.shape[2]
    )


def fold_blocks(query_all, key_rows, value_rows, carried, score_scale):

    def visit_block(state_now, blocks_pair):
        row_peak, row_total, accum = state_now
        key_block, value_block = blocks_pair
        scores = (
            jnp.einsum("qgd,kgd->gqk", query_all, key_block, preferred_element_type=jnp.float32)
            * score_scale
        )
        new_peak = jnp.maximum(row_peak, jnp.max(scores, axis=-1))
        shrink = jnp.exp(row_peak - new_peak)
        expanded = jnp.exp(scores - new_peak[..., None])
        new_total = row_total * shrink + jnp.sum(expanded, axis=-1)
        added = jnp.einsum(
            "gqk,kgd->qgd",
            expanded.astype(jnp.bfloat16),
            value_block,
            preferred_element_type=jnp.float32,
        )
        new_accum = accum * shrink.T[:, :, None] + added
        return ((new_peak, new_total, new_accum), None)

    state_done, unused = lax.scan(
        visit_block, carried, (key_blocks(key_rows), key_blocks(value_rows))
    )
    return state_done


def local(hidden_in, queries, keys, values, out_weight, gate):
    tok_rows = hidden_in.shape[1]
    model_width = hidden_in.shape[2]
    seq_count = lax.axis_size("seq")
    copies = max(1, seq_count // HEADS)
    head_group = max(1, HEADS // seq_count)
    group_count = HEADS // head_group
    query_rows = tok_rows // copies
    group_width = head_group * HEAD_DIM
    score_scale = HEAD_DIM ** (-0.5)
    query_local = queries[0]
    key_local = keys[0]
    value_local = values[0]

    def spread_items(array):
        shaped = array.reshape(tok_rows, group_count, 1, group_width)
        return jnp.broadcast_to(shaped, (tok_rows, group_count, copies, group_width)).reshape(
            tok_rows, seq_count, group_width
        )

    key_views, value_views = (
        lax.all_gather(keys, "view", axis=0, tiled=True),
        lax.all_gather(values, "view", axis=0, tiled=True),
    )
    view_total_count = key_views.shape[0]
    query_split = query_local.reshape(tok_rows, HEADS, HEAD_DIM)
    key_split = key_views.reshape(view_total_count, tok_rows, HEADS, HEAD_DIM)
    value_split = value_views.reshape(view_total_count, tok_rows, HEADS, HEAD_DIM)
    cross_scores = (
        jnp.einsum("thd,bthd->tbh", query_split, key_split, preferred_element_type=jnp.float32)
        * score_scale
    )
    cross_peak = jnp.max(cross_scores, axis=1, keepdims=True)
    expanded = jnp.exp(cross_scores - cross_peak)
    cross_weights = (expanded / jnp.sum(expanded, axis=1, keepdims=True)).astype(jnp.bfloat16)
    cross_out = jnp.einsum(
        "tbh,bthd->thd", cross_weights, value_split, preferred_element_type=jnp.float32
    )
    cross_out = cross_out.reshape(tok_rows, model_width)
    shaped = query_local.reshape(copies, query_rows, group_count, group_width)
    query_got = lax.all_to_all(
        shaped.transpose(1, 2, 0, 3).reshape(query_rows, seq_count, group_width),
        "seq",
        split_axis=1,
        concat_axis=0,
        tiled=True,
    )
    key_got = lax.all_to_all(
        spread_items(key_local), "seq", split_axis=1, concat_axis=0, tiled=True
    )
    value_got = lax.all_to_all(
        spread_items(value_local), "seq", split_axis=1, concat_axis=0, tiled=True
    )
    row_count = query_got.shape[0]
    row_peak, row_total, accum = fold_blocks(
        query_got,
        key_got,
        value_got,
        (
            jnp.full((head_group, row_count), -jnp.inf, jnp.float32),
            jnp.zeros((head_group, row_count), jnp.float32),
            jnp.zeros(query_got.shape, jnp.float32),
        ),
        score_scale,
    )
    self_heads = (accum / row_total.T[:, :, None]).astype(jnp.bfloat16)
    outgoing = self_heads.reshape(seq_count, query_rows, group_width)
    returned = lax.all_to_all(outgoing, "seq", split_axis=0, concat_axis=0, tiled=True)
    self_out = (
        returned.reshape(group_count, copies, query_rows, group_width)
        .transpose(1, 2, 0, 3)
        .reshape(tok_rows, model_width)
    )
    attended = (self_out.astype(jnp.float32) + cross_out).astype(jnp.bfloat16)
    projected = jnp.dot(attended, out_weight, preferred_element_type=jnp.float32)
    updated = hidden_in[0].astype(jnp.float32) + gate[0].astype(jnp.float32)[None, :] * projected
    return updated.astype(jnp.bfloat16)[None]


def solution(mesh):
    return jax.shard_map(
        local,
        mesh=mesh,
        in_specs=(
            P("view", "seq", None),
            P("view", "seq", None),
            P("view", "seq", None),
            P("view", "seq", None),
            P(),
            P("view", None),
        ),
        out_specs=P("view", "seq", None),
        check_vma=False,
    )
```

profile of v0, /device:TPU:1, one launch (start us, length us, event | category | flops | bytes accessed | tf_op | source)
XLA Modules:
  0.0 320.7 jit_solution(2972345431150875333)
XLA Ops:
  6.5 1.1 copy.38
  7.7 0.9 copy.25
  8.6 15.1 %all-to-all-start.1 = ((bf16[32,64,128]{2,0,1:T(8,128)(2,1)}), bf16[32,64,128]{2,0,1:T(8,128)(2,1)S(1)}, u32[]{:S(2)}, u32[]{:S(2)}) async-start(bf16[32,64,128]{2,0,1:T(8,128)(2,1)} %bitcast.8), calls=%async_computation.1 | async-start | bytes 1048576 | tf_op jit(solution)/shard_map/all_to_all | solution.py:88
  23.7 1.1 copy.39
  25.1 15.8 %all-to-all-done.1 = bf16[32,64,128]{2,0,1:T(8,128)(2,1)S(1)} async-done(((bf16[32,64,128]{2,0,1:T(8,128)(2,1)}), bf16[32,64,128]{2,0,1:T(8,128)(2,1)S(1)}, u32[]{:S(2)}, u32[]{:S(2)}) %all-to-all-start.1) | async-done | bytes 524320 | tf_op jit(solution)/shard_map/all_to_all | solution.py:88
  40.8 1.8 broadcast_in_dim.36
  42.7 7.5 %all-to-all-start.2 = ((bf16[128,64,128]{2,0,1:T(8,128)(2,1)}), bf16[128,64,128]{2,0,1:T(8,128)(2,1)S(1)}, u32[]{:S(2)}, u32[]{:S(2)}) async-start(bf16[128,64,128]{2,0,1:T(8,128)(2,1)} %bitcast.12), calls=%async_computation.2 | async-start | bytes 4194304 | tf_op jit(solution)/shard_map/all_to_all | solution.py:98
  50.4 0.9 copy.24
  51.3 49.4 %all-to-all-done.2 = bf16[128,64,128]{2,0,1:T(8,128)(2,1)S(1)} async-done(((bf16[128,64,128]{2,0,1:T(8,128)(2,1)}), bf16[128,64,128]{2,0,1:T(8,128)(2,1)S(1)}, u32[]{:S(2)}, u32[]{:S(2)}) %all-to-all-start.2) | async-done | bytes 2097184 | tf_op jit(solution)/shard_map/all_to_all | solution.py:98
  100.8 3.2 %broadcast_in_dim.34 = bf16[128,16,4,128]{3,0,2,1:T(8,128)(2,1)} broadcast(bf16[128,16,128]{2,0,1:T(8,128)(2,1)} %copy.24), dimensions={0,1,3} | broadcast | bytes 2621440 | tf_op jit(solution)/shard_map/broadcast_in_dim | solution.py:64
  104.0 7.8 %all-to-all-start = ((bf16[128,64,128]{2,0,1:T(8,128)(2,1)}), bf16[128,64,128]{2,0,1:T(8,128)(2,1)}, u32[]{:S(2)}, u32[]{:S(2)}) async-start(bf16[128,64,128]{2,0,1:T(8,128)(2,1)} %bitcast.2), calls=%async_computation | async-start | bytes 4194304 | tf_op jit(solution)/shard_map/all_to_all | solution.py:95
  113.3 2.1 reshape.92
  115.4 46.0 %all-gather.3.cloned.1.call-done = bf16[4,128,2048]{2,1,0:T(8,128)(2,1)} async-done(((bf16[1,128,2048]{2,1,0:T(8,128)(2,1)}), bf16[4,128,2048]{2,1,0:T(8,128)(2,1)}) %all-gather.3.cloned.1.call-update) | async-done | bytes 2097168 | tf_op jit(solution)/shard_map/all_gather | solution.py:69
  161.4 3.5 %copy.41 = bf16[64,8,16,128]{3,2,1,0:T(8,128)(2,1)} copy(bf16[64,8,16,128]{3,1,2,0:T(8,128)(2,1)} %bitcast.143) | data formatting | bytes 4194304
  165.0 112.8 %while.15 = (s32[]{:T(128)}, f32[1,2048]{1,0:T(1,128)S(1)}, f32[1,2048]{1,0:T(1,128)S(1)}, f32[2048,1,128]{0,2,1:T(8,128)S(1)}, bf16[8,1024,1,128]{3,1,2,0:T(8,1...) while((s32[]{:T(128)}, f32[1,2048]{1,0:T(1,128)S(1)}, ...), condition=%wide.region_3.0_spmd.clone, body=%wide.region_0.3_spmd.clone.sunk | while | flops 1091315712 | bytes 61998212 | solution.py:42
  165.0 5.4 %multiply_reduce_fusion.2 = (f32[2048]{0:T(1024)S(1)}, f32[1024,2048]{1,0:T(8,128)}) fusion(bf16[2048,1,128]{2,0,1:T(8,128)(2,1)S(1)} %get-tuple-element.182, bf16[8,1024,1,128]{3,1,2,0:T(8,128)(2,1)} %get-tuple-element.181, s32[]{:T(128)} %get-tuple-element.168), kind=kOutput, calls=%fused_computation.1.clone.1 | convolution fusion | flops 541063168 | bytes 9183744 | tf_op jit(solution)/shard_map/while/body/eval_jaxpr/qgd,kgd->gqk/dot_general | solution.py:26
  170.4 4.9 %fusion.48 = f32[2048]{0:T(1024)S(1)} fusion(f32[1024,2048]{1,0:T(8,128)} %get-tuple-element.156, f32[2048]{0:T(1024)S(1)} %bitcast.136), kind=kLoop, calls=%fused_computation.3.clone.1 | loop fusion | flops 6289408 | bytes 8404992 | tf_op jit(solution)/shard_map/while/body/eval_jaxpr/reduce_sum | solution.py:32
  175.4 1.1 copy-done
  176.5 2.8 fusion.50
  179.4 5.4 %multiply_reduce_fusion.2 = (f32[2048]{0:T(1024)S(1)}, f32[1024,2048]{1,0:T(8,128)}) fusion(bf16[2048,1,128]{2,0,1:T(8,128)(2,1)S(1)} %get-tuple-element.182, bf16[8,1024,1,128]{3,1,2,0:T(8,128)(2,1)} %get-tuple-element.181, s32[]{:T(128)} %get-tuple-element.168), kind=kOutput, calls=%fused_computation.1.clone.1 | convolution fusion | flops 541063168 | bytes 9183744 | tf_op jit(solution)/shard_map/while/body/eval_jaxpr/qgd,kgd->gqk/dot_general | solution.py:26
  184.8 5.0 %fusion.48 = f32[2048]{0:T(1024)S(1)} fusion(f32[1024,2048]{1,0:T(8,128)} %get-tuple-element.156, f32[2048]{0:T(1024)S(1)} %bitcast.136), kind=kLoop, calls=%fused_computation.3.clone.1 | loop fusion | flops 6289408 | bytes 8404992 | tf_op jit(solution)/shard_map/while/body/eval_jaxpr/reduce_sum | solution.py:32
  190.7 2.8 fusion.50
  193.6 5.4 %multiply_reduce_fusion.2 = (f32[2048]{0:T(1024)S(1)}, f32[1024,2048]{1,0:T(8,128)}) fusion(bf16[2048,1,128]{2,0,1:T(8,128)(2,1)S(1)} %get-tuple-element.182, bf16[8,1024,1,128]{3,1,2,0:T(8,128)(2,1)} %get-tuple-element.181, s32[]{:T(128)} %get-tuple-element.168), kind=kOutput, calls=%fused_computation.1.clone.1 | convolution fusion | flops 541063168 | bytes 9183744 | tf_op jit(solution)/shard_map/while/body/eval_jaxpr/qgd,kgd->gqk/dot_general | solution.py:26
  199.0 4.9 %fusion.48 = f32[2048]{0:T(1024)S(1)} fusion(f32[1024,2048]{1,0:T(8,128)} %get-tuple-element.156, f32[2048]{0:T(1024)S(1)} %bitcast.136), kind=kLoop, calls=%fused_computation.3.clone.1 | loop fusion | flops 6289408 | bytes 8404992 | tf_op jit(solution)/shard_map/while/body/eval_jaxpr/reduce_sum | solution.py:32
  204.8 2.8 fusion.50
  207.6 5.4 %multiply_reduce_fusion.2 = (f32[2048]{0:T(1024)S(1)}, f32[1024,2048]{1,0:T(8,128)}) fusion(bf16[2048,1,128]{2,0,1:T(8,128)(2,1)S(1)} %get-tuple-element.182, bf16[8,1024,1,128]{3,1,2,0:T(8,128)(2,1)} %get-tuple-element.181, s32[]{:T(128)} %get-tuple-element.168), kind=kOutput, calls=%fused_computation.1.clone.1 | convolution fusion | flops 541063168 | bytes 9183744 | tf_op jit(solution)/shard_map/while/body/eval_jaxpr/qgd,kgd->gqk/dot_general | solution.py:26
  213.0 4.9 %fusion.48 = f32[2048]{0:T(1024)S(1)} fusion(f32[1024,2048]{1,0:T(8,128)} %get-tuple-element.156, f32[2048]{0:T(1024)S(1)} %bitcast.136), kind=kLoop, calls=%fused_computation.3.clone.1 | loop fusion | flops 6289408 | bytes 8404992 | tf_op jit(solution)/shard_map/while/body/eval_jaxpr/reduce_sum | solution.py:32
  218.8 2.8 fusion.50
  221.6 5.4 %multiply_reduce_fusion.2 = (f32[2048]{0:T(1024)S(1)}, f32[1024,2048]{1,0:T(8,128)}) fusion(bf16[2048,1,128]{2,0,1:T(8,128)(2,1)S(1)} %get-tuple-element.182, bf16[8,1024,1,128]{3,1,2,0:T(8,128)(2,1)} %get-tuple-element.181, s32[]{:T(128)} %get-tuple-element.168), kind=kOutput, calls=%fused_computation.1.clone.1 | convolution fusion | flops 541063168 | bytes 9183744 | tf_op jit(solution)/shard_map/while/body/eval_jaxpr/qgd,kgd->gqk/dot_general | solution.py:26
  227.1 4.9 %fusion.48 = f32[2048]{0:T(1024)S(1)} fusion(f32[1024,2048]{1,0:T(8,128)} %get-tuple-element.156, f32[2048]{0:T(1024)S(1)} %bitcast.136), kind=kLoop, calls=%fused_computation.3.clone.1 | loop fusion | flops 6289408 | bytes 8404992 | tf_op jit(solution)/shard_map/while/body/eval_jaxpr/reduce_sum | solution.py:32
  232.8 2.8 fusion.50
  235.7 5.4 %multiply_reduce_fusion.2 = (f32[2048]{0:T(1024)S(1)}, f32[1024,2048]{1,0:T(8,128)}) fusion(bf16[2048,1,128]{2,0,1:T(8,128)(2,1)S(1)} %get-tuple-element.182, bf16[8,1024,1,128]{3,1,2,0:T(8,128)(2,1)} %get-tuple-element.181, s32[]{:T(128)} %get-tuple-element.168), kind=kOutput, calls=%fused_computation.1.clone.1 | convolution fusion | flops 541063168 | bytes 9183744 | tf_op jit(solution)/shard_map/while/body/eval_jaxpr/qgd,kgd->gqk/dot_general | solution.py:26
  241.1 4.9 %fusion.48 = f32[2048]{0:T(1024)S(1)} fusion(f32[1024,2048]{1,0:T(8,128)} %get-tuple-element.156, f32[2048]{0:T(1024)S(1)} %bitcast.136), kind=kLoop, calls=%fused_computation.3.clone.1 | loop fusion | flops 6289408 | bytes 8404992 | tf_op jit(solution)/shard_map/while/body/eval_jaxpr/reduce_sum | solution.py:32
  246.9 2.8 fusion.50
  249.7 5.4 %multiply_reduce_fusion.2 = (f32[2048]{0:T(1024)S(1)}, f32[1024,2048]{1,0:T(8,128)}) fusion(bf16[2048,1,128]{2,0,1:T(8,128)(2,1)S(1)} %get-tuple-element.182, bf16[8,1024,1,128]{3,1,2,0:T(8,128)(2,1)} %get-tuple-element.181, s32[]{:T(128)} %get-tuple-element.168), kind=kOutput, calls=%fused_computation.1.clone.1 | convolution fusion | flops 541063168 | bytes 9183744 | tf_op jit(solution)/shard_map/while/body/eval_jaxpr/qgd,kgd->gqk/dot_general | solution.py:26
  255.2 4.9 %fusion.48 = f32[2048]{0:T(1024)S(1)} fusion(f32[1024,2048]{1,0:T(8,128)} %get-tuple-element.156, f32[2048]{0:T(1024)S(1)} %bitcast.136), kind=kLoop, calls=%fused_computation.3.clone.1 | loop fusion | flops 6289408 | bytes 8404992 | tf_op jit(solution)/shard_map/while/body/eval_jaxpr/reduce_sum | solution.py:32
  260.9 2.8 fusion.50
  263.8 5.4 %multiply_reduce_fusion.2 = (f32[2048]{0:T(1024)S(1)}, f32[1024,2048]{1,0:T(8,128)}) fusion(bf16[2048,1,128]{2,0,1:T(8,128)(2,1)S(1)} %get-tuple-element.182, bf16[8,1024,1,128]{3,1,2,0:T(8,128)(2,1)} %get-tuple-element.181, s32[]{:T(128)} %get-tuple-element.168), kind=kOutput, calls=%fused_computation.1.clone.1 | convolution fusion | flops 541063168 | bytes 9183744 | tf_op jit(solution)/shard_map/while/body/eval_jaxpr/qgd,kgd->gqk/dot_general | solution.py:26
  269.2 4.9 %fusion.48 = f32[2048]{0:T(1024)S(1)} fusion(f32[1024,2048]{1,0:T(8,128)} %get-tuple-element.156, f32[2048]{0:T(1024)S(1)} %bitcast.136), kind=kLoop, calls=%fused_computation.3.clone.1 | loop fusion | flops 6289408 | bytes 8404992 | tf_op jit(solution)/shard_map/while/body/eval_jaxpr/reduce_sum | solution.py:32
  275.0 2.8 fusion.50
  278.1 1.1 divide_convert_fusion
  279.3 11.1 %all-to-all-start.3 = ((bf16[64,32,128]{2,1,0:T(8,128)(2,1)}), bf16[64,32,128]{2,1,0:T(8,128)(2,1)S(1)}, u32[]{:S(2)}, u32[]{:S(2)}) async-start(bf16[64,32,128]{2,1,0:T(8,128)(2,1)} %bitcast.18), calls=%async_computation.3 | async-start | bytes 1048576 | tf_op jit(solution)/shard_map/all_to_all | solution.py:115
  290.4 4.2 %fusion.29 = f32[128,16,1,4]{3,2,1,0:T(1,128)S(1)} fusion(bf16[128,16,128,1]{2,3,1,0:T(2,128)(2,1)} %reshape.92, bf16[4,128,16,128]{3,2,1,0:T(8,128)(2,1)} %bitcast.142), kind=kOutput, calls=%fused_computation.31 | convolution fusion | flops 2097152 | bytes 2654208 | tf_op jit(solution)/shard_map/thd,bthd->tbh/dot_general | solution.py:77
  295.1 0.9 copy.34
  296.0 2.2 copy.42
  298.2 2.3 fusion.27
  300.5 7.0 %all-to-all-done.3 = bf16[64,32,128]{2,1,0:T(8,128)(2,1)S(1)} async-done(((bf16[64,32,128]{2,1,0:T(8,128)(2,1)}), bf16[64,32,128]{2,1,0:T(8,128)(2,1)S(1)}, u32[]{:S(2)}, u32[]{:S(2)}) %all-to-all-start.3) | async-done | bytes 524320 | tf_op jit(solution)/shard_map/all_to_all | solution.py:115
  307.9 6.0 %fusion.26 = bf16[1,128,2048]{2,1,0:T(8,128)(2,1)} fusion(bf16[2048,2048]{1,0:T(8,128)(2,1)} %param.12, f32[16,8,16,128]{3,2,1,0:T(8,128)S(1)} %bitcast.138, f32[16,8,16,128]{3,2,1,0:T(8,128)S(1)} %bitcast.134, bf16[1,128,2048]{2,1,0:T(8,128)(2,1)S(1)} %copy-done.4, f32[2048]{0:T(1024)S(1)} %bitcast.154), kind=kOutput, calls=%fused_computation.28 | convolution fusion | flops 1075314688 | bytes 11542528 | tf_op jit(solution)/shard_map/dot_general | solution.py:122
  (67 shorter events, 8.9 us)
Async XLA Ops:
  8.6 32.2 %all-to-all-start.1 = ((bf16[32,64,128]{2,0,1:T(8,128)(2,1)}), bf16[32,64,128]{2,0,1:T(8,128)(2,1)S(1)}, u32[]{:S(2)}, u32[]{:S(2)}) async-start(bf16[32,64,128]{2,0,1:T(8,128)(2,1)} %bitcast.8), calls=%async_computation.1 | async-start | bytes 1048576 | tf_op jit(solution)/shard_map/all_to_all | solution.py:88
  24.9 25.3 %copy-start.3 = (bf16[1,128,2048]{2,1,0:T(8,128)(2,1)S(1)}, bf16[1,128,2048]{2,1,0:T(8,128)(2,1)}, u32[]{:S(2)}) copy-start(bf16[1,128,2048]{2,1,0:T(8,128)(2,1)} %param.10) | copy-start | bytes 1572868
  42.7 58.1 %all-to-all-start.2 = ((bf16[128,64,128]{2,0,1:T(8,128)(2,1)}), bf16[128,64,128]{2,0,1:T(8,128)(2,1)S(1)}, u32[]{:S(2)}, u32[]{:S(2)}) async-start(bf16[128,64,128]{2,0,1:T(8,128)(2,1)} %bitcast.12), calls=%async_computation.2 | async-start | bytes 4194304 | tf_op jit(solution)/shard_map/all_to_all | solution.py:98
  51.3 62.0 %copy-start.2 = (bf16[1,128,2048]{2,1,0:T(8,128)(2,1)S(1)}, bf16[1,128,2048]{2,1,0:T(8,128)(2,1)}, u32[]{:S(2)}) copy-start(bf16[1,128,2048]{2,1,0:T(8,128)(2,1)} %param.9) | copy-start | bytes 1572868
  51.3 64.1 %copy-start.5 = (bf16[1,2048]{1,0:T(2,128)(2,1)S(1)}, bf16[1,2048]{1,0:T(2,128)(2,1)}, u32[]{:S(2)}) copy-start(bf16[1,2048]{1,0:T(2,128)(2,1)} %param.13) | copy-start | bytes 12292
  100.7 12.6 %copy-start.1 = (bf16[128,64,128]{2,0,1:T(8,128)(2,1)}, bf16[128,64,128]{2,0,1:T(8,128)(2,1)S(1)}, u32[]{:S(2)}) copy-start(bf16[128,64,128]{2,0,1:T(8,128)(2,1)S(1)} %all-to-all-done.2) | copy-start | bytes 6291460
  104.0 61.0 %all-to-all-start = ((bf16[128,64,128]{2,0,1:T(8,128)(2,1)}), bf16[128,64,128]{2,0,1:T(8,128)(2,1)}, u32[]{:S(2)}, u32[]{:S(2)}) async-start(bf16[128,64,128]{2,0,1:T(8,128)(2,1)} %bitcast.2), calls=%async_computation | async-start | bytes 4194304 | tf_op jit(solution)/shard_map/all_to_all | solution.py:95
  111.8 49.6 %all-gather.3.cloned.1.call-start = ((), (), s32[]{:S(2)}) async-start(), calls=%async_computation.4 | async-start | bytes 2621440 | tf_op jit(solution)/shard_map/all_gather | solution.py:69
  112.6 183.4 %all-gather.5.cloned.1.call-start = ((), (), s32[]{:S(2)}) async-start(), calls=%async_computation.5 | async-start | bytes 2621440 | tf_op jit(solution)/shard_map/all_gather | solution.py:70
  170.4 6.1 %copy-start = (f32[1024,2048]{1,0:T(8,128)S(1)}, f32[1024,2048]{1,0:T(8,128)}, u32[]{:S(2)}) copy-start(f32[1024,2048]{1,0:T(8,128)} %get-tuple-element.156) | copy-start | bytes 25165828 | tf_op jit(solution)/shard_map/while
  184.8 5.9 %copy-start = (f32[1024,2048]{1,0:T(8,128)S(1)}, f32[1024,2048]{1,0:T(8,128)}, u32[]{:S(2)}) copy-start(f32[1024,2048]{1,0:T(8,128)} %get-tuple-element.156) | copy-start | bytes 25165828 | tf_op jit(solution)/shard_map/while
  199.0 5.8 %copy-start = (f32[1024,2048]{1,0:T(8,128)S(1)}, f32[1024,2048]{1,0:T(8,128)}, u32[]{:S(2)}) copy-start(f32[1024,2048]{1,0:T(8,128)} %get-tuple-element.156) | copy-start | bytes 25165828 | tf_op jit(solution)/shard_map/while
  213.0 5.8 %copy-start = (f32[1024,2048]{1,0:T(8,128)S(1)}, f32[1024,2048]{1,0:T(8,128)}, u32[]{:S(2)}) copy-start(f32[1024,2048]{1,0:T(8,128)} %get-tuple-element.156) | copy-start | bytes 25165828 | tf_op jit(solution)/shard_map/while
  227.1 5.8 %copy-start = (f32[1024,2048]{1,0:T(8,128)S(1)}, f32[1024,2048]{1,0:T(8,128)}, u32[]{:S(2)}) copy-start(f32[1024,2048]{1,0:T(8,128)} %get-tuple-element.156) | copy-start | bytes 25165828 | tf_op jit(solution)/shard_map/while
  241.1 5.8 %copy-start = (f32[1024,2048]{1,0:T(8,128)S(1)}, f32[1024,2048]{1,0:T(8,128)}, u32[]{:S(2)}) copy-start(f32[1024,2048]{1,0:T(8,128)} %get-tuple-element.156) | copy-start | bytes 25165828 | tf_op jit(solution)/shard_map/while
  255.2 5.8 %copy-start = (f32[1024,2048]{1,0:T(8,128)S(1)}, f32[1024,2048]{1,0:T(8,128)}, u32[]{:S(2)}) copy-start(f32[1024,2048]{1,0:T(8,128)} %get-tuple-element.156) | copy-start | bytes 25165828 | tf_op jit(solution)/shard_map/while
  269.2 5.8 %copy-start = (f32[1024,2048]{1,0:T(8,128)S(1)}, f32[1024,2048]{1,0:T(8,128)}, u32[]{:S(2)}) copy-start(f32[1024,2048]{1,0:T(8,128)} %get-tuple-element.156) | copy-start | bytes 25165828 | tf_op jit(solution)/shard_map/while
  279.3 28.3 %all-to-all-start.3 = ((bf16[64,32,128]{2,1,0:T(8,128)(2,1)}), bf16[64,32,128]{2,1,0:T(8,128)(2,1)S(1)}, u32[]{:S(2)}, u32[]{:S(2)}) async-start(bf16[64,32,128]{2,1,0:T(8,128)(2,1)} %bitcast.18), calls=%async_computation.3 | async-start | bytes 1048576 | tf_op jit(solution)/shard_map/all_to_all | solution.py:115
  298.2 9.6 %copy-start.4 = (bf16[1,128,2048]{2,1,0:T(8,128)(2,1)S(1)}, bf16[1,128,2048]{2,1,0:T(8,128)(2,1)}, u32[]{:S(2)}) copy-start(bf16[1,128,2048]{2,1,0:T(8,128)(2,1)} %param.8) | copy-start | bytes 1572868
Sparse Core Ops, SparseCore 0:
  114.5 46.9 all-gather.2
  163.2 31.6 all-gather.4
where the time goes:
time: 322 us; the launch traced here: 321 us
  waiting for transfers between devices  120 us (37%)
  matrix products  78.2 us (24%)
  starting transfers between devices  41.6 us (13%)
  other arithmetic  41.2 us (13%)
  local copies, waits for them, and re-layouts  26 us (8%)
  between operations  13.6 us (4%)
    all_to_all x1, waiting for transfers between devices, local(): lax.all_to_all(spread_items(value_local), 'seq', split_axis=1, concat_axi...  49.4 us
    all_gather x1, waiting for transfers between devices, local(): lax.all_gather(keys, 'view', axis=0, tiled=True)  46 us
    dot_general x8, matrix products, visit_block(): jnp.einsum('qgd,kgd->gqk', query_all, key_block, preferred_element_type=j...  43.4 us
    reduce_sum x8, other arithmetic, visit_block(): new_total = row_total * shrink + jnp.sum(expanded, axis=-1)  39.6 us
    dot_general x8, matrix products, visit_block(): jnp.einsum('gqk,kgd->qgd', expanded.astype(jnp.bfloat16), value_block, pr...  22.4 us
    all_to_all x1, waiting for transfers between devices, local(): lax.all_to_all(shaped.transpose(1, 2, 0, 3).reshape(query_rows, seq_count...  15.8 us
    all_to_all x1, starting transfers between devices, local(): lax.all_to_all(shaped.transpose(1, 2, 0, 3).reshape(query_rows, seq_count...  15.1 us
    all_to_all x1, starting transfers between devices, local(): lax.all_to_all(outgoing, 'seq', split_axis=0, concat_axis=0, tiled=True)  11.1 us
  transfers between devices with their start and end apart: 6, of which 4 were waited for; matrix products, arithmetic and copies ran while one was open for 39% of the time, Pallas kernels for 0%

commit v1 on v0

v1 whole, which is shorter than its diff:
```python
import functools
import math

import jax
import jax.numpy as jnp
import numpy as np
from jax import lax
from jax.experimental import pallas as pl
from jax.experimental.pallas import tpu as pltpu
from jax.sharding import Mesh, PartitionSpec as P

HEADS = 16
HD = 128
BF = jnp.bfloat16
F32 = jnp.float32
SCALE = HD**-0.5
LOG2E = math.log2(math.e)
NT = (((1,), (1,)), ((), ()))
VMEM_CAP = 56 * 2**20


def params(**kw):
    return pltpu.CompilerParams(vmem_limit_bytes=VMEM_CAP, **kw)


def pack_kernel(q_ref, k_ref, v_ref, o_ref):
    copies, heads, _, rows, _ = o_ref.shape
    for j, ref in enumerate((q_ref, k_ref, v_ref)):
        for h in range(heads):
            for r in range(copies):
                o_ref[r, h, j] = ref[r * rows : (r + 1) * rows, h * HD : (h + 1) * HD]


def pack(q, k, v, copies):
    tok, width = q.shape
    rows = tok // copies
    hb = 4
    spec = pl.BlockSpec((tok, hb * HD), lambda i: (0, i))
    return pl.pallas_call(
        pack_kernel,
        grid=(HEADS // hb,),
        in_specs=[spec] * 3,
        out_specs=pl.BlockSpec((copies, hb, 3, rows, HD), lambda i: (0, i, 0, 0, 0)),
        out_shape=jax.ShapeDtypeStruct((copies, HEADS, 3, rows, HD), BF),
        compiler_params=params(),
        name="pack",
    )(q, k, v)


def attend_kernel(*refs, first, last, groups, kb, skip_axis):
    refs = list(refs)
    q_ref = refs.pop(0)
    k_refs = [refs.pop(0) for _ in range(groups)]
    if not first:
        m_in, acc_in = refs.pop(0), refs.pop(0)
    if last:
        (o_ref,) = refs[:1]
        refs = refs[1:]
    else:
        m_out, acc_out = refs[:2]
        refs = refs[2:]
    k_all, v_all = refs
    qs = q_ref.shape[0] * q_ref.shape[2]
    total = k_all.shape[0]

    @pl.when(pl.program_id(0) == 0)
    def _():
        at = 0
        for ref in k_refs:
            n = ref.shape[0] * ref.shape[2]
            k_all[at : at + n, :] = ref[:, 0].reshape(n, HD)
            v_all[at : at + n, :HD] = ref[:, 1].reshape(n, HD)
            at += n
        v_all[:, HD:] = jnp.ones((total, HD), BF)

    q = q_ref[:, 0].reshape(qs, HD)
    c = SCALE * LOG2E
    if first:
        m = jnp.full((qs, 1), -jnp.inf, F32)
        acc = jnp.zeros((qs, 2 * HD), F32)
    else:
        m = m_in[:, :1]
        acc = acc_in[...]
    for i in range(total // kb):
        s = lax.dot_general(q, k_all[i * kb : (i + 1) * kb, :], NT, preferred_element_type=F32)
        new = jnp.maximum(m, jnp.max(s, axis=1, keepdims=True) * c)
        p = jnp.exp2(s * c - new).astype(BF)
        add = jnp.dot(p, v_all[i * kb : (i + 1) * kb, :], preferred_element_type=F32)
        if first and i == 0:
            acc = add
        else:
            acc = acc * jnp.exp2(m - new) + add
        m = new
    if last:
        out = acc[:, :HD] / acc[:, HD:]
        o_ref[...] = out.astype(BF).reshape(o_ref.shape)
    else:
        m_out[...] = jnp.broadcast_to(m, m_out.shape)
        acc_out[...] = acc


def attend(got, kv_list, state, last, qsrc=16, kb=1024):
    src, _, rows, _ = got.shape
    qb = qsrc * rows
    nq = src * rows
    total = sum(a.shape[0] * a.shape[2] for a in kv_list)
    in_specs = [pl.BlockSpec((qsrc, 1, rows, HD), lambda i: (i, 0, 0, 0))]
    args = [got]
    for a in kv_list:
        in_specs.append(pl.BlockSpec(a.shape, lambda i: (0, 0, 0, 0)))
        args.append(a)
    m_spec = pl.BlockSpec((qb, HD), lambda i: (i, 0))
    acc_spec = pl.BlockSpec((qb, 2 * HD), lambda i: (i, 0))
    if state is not None:
        in_specs += [m_spec, acc_spec]
        args += list(state)
    if last:
        out_shape = jax.ShapeDtypeStruct((src, rows, HD), BF)
        out_specs = pl.BlockSpec((qsrc, rows, HD), lambda i: (i, 0, 0))
    else:
        out_shape = (
            jax.ShapeDtypeStruct((nq, HD), F32),
            jax.ShapeDtypeStruct((nq, 2 * HD), F32),
        )
        out_specs = (m_spec, acc_spec)
    return pl.pallas_call(
        functools.partial(
            attend_kernel,
            first=state is None,
            last=last,
            groups=len(kv_list),
            kb=kb,
            skip_axis=None,
        ),
        grid=(src // qsrc,),
        in_specs=in_specs,
        out_specs=out_specs,
        out_shape=out_shape,
        scratch_shapes=[pltpu.VMEM((total, HD), BF), pltpu.VMEM((total, 2 * HD), BF)],
        compiler_params=params(),
        cost_estimate=pl.CostEstimate(
            flops=8 * nq * total * HD,
            bytes_accessed=4 * nq * HD + 4 * total * HD,
            transcendentals=nq * total,
        ),
        name="attend",
    )(*args)


def cross_kernel(q_ref, k_ref, v_ref, o_ref):
    views = k_ref.shape[0]
    heads = q_ref.shape[1] // HD
    for h in range(heads):
        cols = slice(h * HD, (h + 1) * HD)
        q = q_ref[:, cols].astype(F32)
        s = [
            jnp.sum(q * k_ref[b, :, cols].astype(F32), axis=1, keepdims=True) * SCALE
            for b in range(views)
        ]
        peak = functools.reduce(jnp.maximum, s)
        e = [jnp.exp(x - peak) for x in s]
        inv = 1.0 / functools.reduce(jnp.add, e)
        out = None
        for b in range(views):
            w = (e[b] * inv).astype(BF).astype(F32)
            t = w * v_ref[b, :, cols].astype(F32)
            out = t if out is None else out + t
        o_ref[:, cols] = out


def cross(q, k, v):
    tok, width = q.shape
    views = k.shape[0]
    hb = 4
    kv_spec = pl.BlockSpec((views, tok, hb * HD), lambda i: (0, 0, i))
    return pl.pallas_call(
        cross_kernel,
        grid=(width // (hb * HD),),
        in_specs=[pl.BlockSpec((tok, hb * HD), lambda i: (0, i)), kv_spec, kv_spec],
        out_specs=pl.BlockSpec((tok, hb * HD), lambda i: (0, i)),
        out_shape=jax.ShapeDtypeStruct((tok, width), F32),
        compiler_params=params(),
        cost_estimate=pl.CostEstimate(
            flops=16 * tok * width, bytes_accessed=(4 * views + 6) * tok * width, transcendentals=0
        ),
        name="cross",
    )(q, k, v)


def project_kernel(s_ref, c_ref, w_ref, h_ref, g_ref, o_ref, att):
    copies, heads, rows, _ = s_ref.shape

    @pl.when(pl.program_id(0) == 0)
    def _():
        for r in range(copies):
            for h in range(heads):
                at = (slice(r * rows, (r + 1) * rows), slice(h * HD, (h + 1) * HD))
                att[at] = (s_ref[r, h].astype(F32) + c_ref[at]).astype(BF)

    y = jnp.dot(att[...], w_ref[...], preferred_element_type=F32)
    o_ref[...] = (h_ref[...].astype(F32) + g_ref[...].astype(F32) * y).astype(BF)


def project(self_heads, cross_out, w, hidden, gate):
    copies, heads, rows, _ = self_heads.shape
    tok, width = cross_out.shape
    nb = 512
    return pl.pallas_call(
        project_kernel,
        grid=(width // nb,),
        in_specs=[
            pl.BlockSpec(self_heads.shape, lambda i: (0, 0, 0, 0)),
            pl.BlockSpec((tok, width), lambda i: (0, 0)),
            pl.BlockSpec((width, nb), lambda i: (0, i)),
            pl.BlockSpec((tok, nb), lambda i: (0, i)),
            pl.BlockSpec((1, nb), lambda i: (0, i)),
        ],
        out_specs=pl.BlockSpec((tok, nb), lambda i: (0, i)),
        out_shape=jax.ShapeDtypeStruct((tok, width), BF),
        scratch_shapes=[pltpu.VMEM((tok, width), BF)],
        compiler_params=params(),
        name="project",
    )(self_heads, cross_out, w, hidden, gate)


def local(hidden_in, queries, keys, values, out_weight, gate):
    hidden, q, k, v = hidden_in[0], queries[0], keys[0], values[0]
    tok, width = q.shape
    copies = lax.axis_size("y")
    seq = ("y", "z", "xh")
    view = ("xl", "c")
    rows = tok // copies
    n = copies * HEADS

    packed = pack(q, k, v, copies).reshape(n, 3 * rows, HD)
    got = lax.all_to_all(packed, seq, split_axis=0, concat_axis=0, tiled=True)
    got = got.reshape(n, 3, rows, HD)
    k_views = lax.all_gather(k, view, axis=0)
    v_views = lax.all_gather(v, view, axis=0)

    kv = got[:, 1:]
    kv_all = lax.all_gather(kv, "y", axis=0, tiled=True)
    state = None
    o = attend(got, [kv_all], state, True)
    cross_out = cross(q, k_views, v_views)
    back = lax.all_to_all(o, seq, split_axis=0, concat_axis=0, tiled=True)
    out = project(back.reshape(copies, HEADS, rows, HD), cross_out, out_weight, hidden, gate)
    return out[None]


def solution(mesh):
    devices = np.asarray(mesh.devices)
    fine = Mesh(devices.reshape(2, 2, 4, 8, 2), ("xl", "c", "y", "z", "xh"))
    spec = P(("xl", "c"), ("y", "z", "xh"), None)
    return jax.shard_map(
        local,
        mesh=fine,
        in_specs=(spec, spec, spec, spec, P(), P(("xl", "c"), None)),
        out_specs=spec,
        check_vma=False,
    )
```

time: 322 us -> 202 us (0.63)
  matrix products: 78.2 us -> 0 us
  blocking collectives: 0 us -> 55 us
  other arithmetic: 41.2 us -> 0 us
  waiting for transfers between devices: 120 us -> 79 us
  Pallas kernels: 0 us -> 40.8 us
  starting transfers between devices: 41.6 us -> 11.7 us
  local copies, waits for them, and re-layouts: 26 us -> 2.16 us
    dot_general x19 -> x0, matrix products: 78.2 us -> none  [the longest x8 43.4 us: visit_block(): jnp.einsum('qgd,kgd->gqk', query_all, key_block, preferred_element_type=j...]
    all_to_all x4 -> x1, waiting for transfers between devices: 72.2 us -> 0.01 us  [local(): back = lax.all_to_all(o, seq, split_axis=0, concat_axis=0, tiled=True)]
    all_to_all x0 -> x1, blocking collectives: none -> 55 us  [local(): got = lax.all_to_all(packed, seq, split_axis=0, concat_axis=0, tiled=True)]
    pallas_call x0 -> x4, Pallas kernels: none -> 40.8 us  [the longest x1 25.5 us: attend(): pl.pallas_call(functools.partial(attend_kernel, first=state is None, last...]
    reduce_sum x9 -> x0, other arithmetic: 39.6 us -> none  [the longest x8 39.6 us: visit_block(): new_total = row_total * shrink + jnp.sum(expanded, axis=-1)]
    all_gather x2 -> x3, waiting for transfers between devices: 46.1 us -> 77.6 us  [the longest x1 45.9 us: local(): kv_all = lax.all_gather(kv, 'y', axis=0, tiled=True)]
    all_to_all x4 -> x1, starting transfers between devices: 41.6 us -> 11.7 us  [local(): back = lax.all_to_all(o, seq, split_axis=0, concat_axis=0, tiled=True)]
    unnamed x15 -> x4, local copies, waits for them, and re-layouts: 8.14 us -> 0.82 us
  transfers between devices with their start and end apart: 6 -> 4, of which waited for: 4 -> 2; matrix products, arithmetic and copies ran while one was open for 39% -> 0% of each run, Pallas kernels for 0% -> 15%
where the time goes in v1:
time: 202 us
  waiting for transfers between devices  79 us (39%)
  blocking collectives  55 us (27%)
  Pallas kernels  40.8 us (20%)
  between operations  13.1 us (6%)
  starting transfers between devices  11.7 us (6%)
  local copies, waits for them, and re-layouts  2.16 us (1%)
    all_to_all x1, blocking collectives, local(): got = lax.all_to_all(packed, seq, split_axis=0, concat_axis=0, tiled=True)  55 us
    all_gather x1, waiting for transfers between devices, local(): kv_all = lax.all_gather(kv, 'y', axis=0, tiled=True)  45.9 us
    all_gather x1, waiting for transfers between devices, local(): v_views = lax.all_gather(v, view, axis=0)  31.7 us
    pallas_call x1, Pallas kernels, attend(): pl.pallas_call(functools.partial(attend_kernel, first=state is None, last...  25.5 us
    all_to_all x1, starting transfers between devices, local(): back = lax.all_to_all(o, seq, split_axis=0, concat_axis=0, tiled=True)  11.7 us
    pallas_call x1, Pallas kernels, project(): pl.pallas_call(project_kernel, grid=(width // nb,), in_specs=[pl.BlockSpe...  6.38 us
    pallas_call x1, Pallas kernels, cross(): pl.pallas_call(cross_kernel, grid=(width // (hb * HD),), in_specs=[pl.Blo...  5.15 us
  transfers between devices with their start and end apart: 4, of which 2 were waited for; matrix products, arithmetic and copies ran while one was open for 0% of the time, Pallas kernels for 15%

profile of v1, /device:TPU:1, one launch (start us, length us, event | category | flops | bytes accessed | tf_op | source)
XLA Modules:
  0.0 201.9 jit_solution(9468559388938250404)
XLA Ops:
  6.5 0.0 all-gather.4.cloned.1.call-start
  6.5 3.8 %pack.1 = bf16[4,16,3,32,128]{4,3,2,1,0:T(8,128)(2,1)} custom-call(bf16[128,2048]{1,0:T(8,128)(2,1)} %bitcast.14, bf16[128,2048]{1,0:T(8,128)(2,1)} %bitcast.12, bf16[128,2048]{1,0:T(8,128)(2,1)} %bitcast.13), custom_call_target="tpu_custom_call" | custom-call | tf_op jit(solution)/shard_map/pack/pallas_call | solution.py:39
  10.3 55.0 %all_to_all.10 = bf16[64,96,128]{2,1,0:T(8,128)(2,1)S(1)} all-to-all(bf16[64,96,128]{2,1,0:T(8,128)(2,1)} %bitcast.8), channel_id=1, replica_groups=mesh['xl'=2,'c'=2,'y'=4,'z'=8,'xh'=2] {'y','z','xh'}, dimensions={0} | all-to-all | bytes 3145728 | tf_op jit(solution)/shard_map/all_to_all | solution.py:236
  65.3 0.0 copy-start
  65.3 1.3 slice.4
  66.7 0.0 all-gather.4.cloned.1.call-update
  66.7 0.0 all-gather.6.cloned.1.call-start
  66.8 0.7 all-gather.6.cloned.1.call-update
  67.5 0.0 all-gather.8.cloned.1.call-start
  67.5 0.7 all-gather.8.cloned.1.call-update
  68.2 0.0 copy-done
  68.2 45.9 %all-gather.4.cloned.1.call-done.refs_1_ = bf16[256,2,32,128]{3,2,1,0:T(8,128)(2,1)} async-done(((bf16[64,2,32,128]{3,2,1,0:T(8,128)(2,1)}), bf16[256,2,32,128]{3,2,1,0:T(8,128)(2,1)}) %all-gather.4.cloned.1.call-update) | async-done | bytes 4194320 | tf_op jit(solution)/shard_map/all_gather | solution.py:242
  114.1 25.5 %attend.1 = bf16[64,32,128]{2,1,0:T(8,128)(2,1)} custom-call(bf16[64,3,32,128]{3,2,1,0:T(8,128)(2,1)} %bitcast.10, bf16[256,2,32,128]{3,2,1,0:T(8,128)(2,1)} %all-gather.4.cloned.1.call-done.refs_1_), custom_call_target="tpu_custom_call" | custom-call | flops 17179869184 | bytes 5242880 | tf_op jit(solution)/shard_map/attend/pallas_call | solution.py:126
  139.6 11.7 %all-to-all-start.1 = ((bf16[64,32,128]{2,1,0:T(8,128)(2,1)}), bf16[64,32,128]{2,1,0:T(8,128)(2,1)S(1)}, u32[]{:S(2)}, u32[]{:S(2)}) async-start(bf16[64,32,128]{2,1,0:T(8,128)(2,1)} %attend.1), calls=%async_computation.1 | async-start | bytes 1048576 | tf_op jit(solution)/shard_map/all_to_all | solution.py:246
  151.3 0.0 all-gather.6.cloned.1.call-done.k_ref
  151.3 31.7 %all-gather.8.cloned.1.call-done.v_ref = bf16[4,128,2048]{2,1,0:T(8,128)(2,1)} async-done(((bf16[1,128,2048]{2,1,0:T(8,128)(2,1)}), bf16[4,128,2048]{2,1,0:T(8,128)(2,1)}) %all-gather.8.cloned.1.call-update) | async-done | bytes 2097168 | tf_op jit(solution)/shard_map/all_gather | solution.py:239
  183.0 5.1 %cross.1.c_ref = f32[128,2048]{1,0:T(8,128)} custom-call(bf16[128,2048]{1,0:T(8,128)(2,1)} %bitcast.15, bf16[4,128,2048]{2,1,0:T(8,128)(2,1)} %all-gather.6.cloned.1.call-done.k_ref, bf16[4,128,2048]{2,1,0:T(8,128)(2,1)} %all-gather.8.cloned.1.call-done.v_ref), custom_call_target="tpu_custom_call" | custom-call | flops 4194304 | bytes 5767168 | tf_op jit(solution)/shard_map/cross/pallas_call | solution.py:176
  188.2 0.0 all-to-all-done.1
  188.2 0.0 copy-start.1
  188.2 0.8 copy-done.1
  189.0 6.4 %project.1 = bf16[128,2048]{1,0:T(8,128)(2,1)} custom-call(bf16[4,16,32,128]{3,2,1,0:T(8,128)(2,1)} %bitcast.11, f32[128,2048]{1,0:T(8,128)} %cross.1.c_ref, bf16[2048,2048]{1,0:T(8,128)(2,1)} %w_ref.1, bf16[128,2048]{1,0:T(8,128)(2,1)} %bitcast.16, bf16[1,2048]{1,0:T(2,128)(2,1)} %g_ref.1), custom_call_target="tpu_custom_call" | custom-call | tf_op jit(solution)/shard_map/project/pallas_call | solution.py:208
Async XLA Ops:
  6.5 107.6 %all-gather.4.cloned.1.call-start = ((), (), s32[]{:S(2)}) async-start(), calls=%async_computation.2 | async-start | bytes 5242880 | tf_op jit(solution)/shard_map/all_gather | solution.py:242
  65.3 2.9 %copy-start = (bf16[64,96,128]{2,1,0:T(8,128)(2,1)}, bf16[64,96,128]{2,1,0:T(8,128)(2,1)S(1)}, u32[]{:S(2)}) copy-start(bf16[64,96,128]{2,1,0:T(8,128)(2,1)S(1)} %all_to_all.10) | copy-start | bytes 4718596
  66.7 84.6 %all-gather.6.cloned.1.call-start = ((), (), s32[]{:S(2)}) async-start(), calls=%async_computation.3 | async-start | bytes 2621440 | tf_op jit(solution)/shard_map/all_gather | solution.py:238
  67.5 115.6 %all-gather.8.cloned.1.call-start = ((), (), s32[]{:S(2)}) async-start(), calls=%async_computation.4 | async-start | bytes 2621440 | tf_op jit(solution)/shard_map/all_gather | solution.py:239
  139.6 48.5 %all-to-all-start.1 = ((bf16[64,32,128]{2,1,0:T(8,128)(2,1)}), bf16[64,32,128]{2,1,0:T(8,128)(2,1)S(1)}, u32[]{:S(2)}, u32[]{:S(2)}) async-start(bf16[64,32,128]{2,1,0:T(8,128)(2,1)} %attend.1), calls=%async_computation.1 | async-start | bytes 1048576 | tf_op jit(solution)/shard_map/all_to_all | solution.py:246
  188.2 0.8 copy-start.1
Sparse Core Ops, SparseCore 0:
  66.8 47.2 all-gather.3
  115.9 32.4 all-gather.5
  150.2 32.8 all-gather.7

commit v2 on v1

--- a/solution.py
+++ b/solution.py
@@ -16,7 +16,7 @@
 SCALE = HD**-0.5
 LOG2E = math.log2(math.e)
 NT = (((1,), (1,)), ((), ()))
-VMEM_CAP = 56 * 2**20
+VMEM_CAP = 30 * 2**20
 
 
 def params(**kw):
@@ -47,7 +47,7 @@
     )(q, k, v)
 
 
-def attend_kernel(*refs, first, last, groups, kb, skip_axis):
+def attend_kernel(*refs, first, last, groups, kb):
     refs = list(refs)
     q_ref = refs.pop(0)
     k_refs = [refs.pop(0) for _ in range(groups)]
@@ -130,7 +130,6 @@
             last=last,
             groups=len(kv_list),
             kb=kb,
-            skip_axis=None,
         ),
         grid=(src // qsrc,),
         in_specs=in_specs,
@@ -147,70 +146,67 @@
     )(*args)
 
 
-def cross_kernel(q_ref, k_ref, v_ref, o_ref):
-    views = k_ref.shape[0]
-    heads = q_ref.shape[1] // HD
-    for h in range(heads):
-        cols = slice(h * HD, (h + 1) * HD)
-        q = q_ref[:, cols].astype(F32)
-        s = [
-            jnp.sum(q * k_ref[b, :, cols].astype(F32), axis=1, keepdims=True) * SCALE
-            for b in range(views)
-        ]
-        peak = functools.reduce(jnp.maximum, s)
-        e = [jnp.exp(x - peak) for x in s]
-        inv = 1.0 / functools.reduce(jnp.add, e)
-        out = None
-        for b in range(views):
-            w = (e[b] * inv).astype(BF).astype(F32)
-            t = w * v_ref[b, :, cols].astype(F32)
-            out = t if out is None else out + t
-        o_ref[:, cols] = out
-
-
-def cross(q, k, v):
-    tok, width = q.shape
-    views = k.shape[0]
+def cross_kernel(a_ref, b_ref, o_ref):
+    views, parts, heads = a_ref.shape[:3]
+    for r in range(parts):
+        for h in range(heads):
+            ks = [a_ref[b, r, h, 1].astype(F32) for b in range(views)]
+            ks += [b_ref[b, r, h, 0].astype(F32) for b in range(views)]
+            vs = [a_ref[b, r, h, 2].astype(F32) for b in range(views)]
+            vs += [b_ref[b, r, h, 1].astype(F32) for b in range(views)]
+            for a in range(views):
+                q = a_ref[a, r, h, 0].astype(F32)
+                s = [jnp.sum(q * k, axis=1, keepdims=True) * SCALE for k in ks]
+                peak = functools.reduce(jnp.maximum, s)
+                e = [jnp.exp(x - peak) for x in s]
+                inv = 1.0 / functools.reduce(jnp.add, e)
+                terms = [(x * inv).astype(BF).astype(F32) * v for x, v in zip(e, vs)]
+                o_ref[a, r, h] = functools.reduce(jnp.add, terms)
+
+
+def cross(mine, other):
+    views, parts, heads, _, rows, _ = mine.shape
     hb = 4
-    kv_spec = pl.BlockSpec((views, tok, hb * HD), lambda i: (0, 0, i))
+    size = views * parts * heads * rows * HD
     return pl.pallas_call(
         cross_kernel,
-        grid=(width // (hb * HD),),
-        in_specs=[pl.BlockSpec((tok, hb * HD), lambda i: (0, i)), kv_spec, kv_spec],
-        out_specs=pl.BlockSpec((tok, hb * HD), lambda i: (0, i)),
-        out_shape=jax.ShapeDtypeStruct((tok, width), F32),
+        grid=(heads // hb,),
+        in_specs=[
+            pl.BlockSpec((views, parts, hb, 3, rows, HD), lambda i: (0, 0, i, 0, 0, 0)),
+            pl.BlockSpec((views, parts, hb, 2, rows, HD), lambda i: (0, 0, i, 0, 0, 0)),
+        ],
+        out_specs=pl.BlockSpec((views, parts, hb, rows, HD), lambda i: (0, 0, i, 0, 0)),
+        out_shape=jax.ShapeDtypeStruct((views, parts, heads, rows, HD), F32),
         compiler_params=params(),
         cost_estimate=pl.CostEstimate(
-            flops=16 * tok * width, bytes_accessed=(4 * views + 6) * tok * width, transcendentals=0
+            flops=16 * size, bytes_accessed=14 * size, transcendentals=0
         ),
         name="cross",
-    )(q, k, v)
-
-
-def project_kernel(s_ref, c_ref, w_ref, h_ref, g_ref, o_ref, att):
-    copies, heads, rows, _ = s_ref.shape
+    )(mine, other)
+
+
+def project_kernel(a_ref, w_ref, h_ref, g_ref, o_ref, att):
+    copies, heads, rows, _ = a_ref.shape
 
     @pl.when(pl.program_id(0) == 0)
     def _():
         for r in range(copies):
             for h in range(heads):
-                at = (slice(r * rows, (r + 1) * rows), slice(h * HD, (h + 1) * HD))
-                att[at] = (s_ref[r, h].astype(F32) + c_ref[at]).astype(BF)
+                att[r * rows : (r + 1) * rows, h * HD : (h + 1) * HD] = a_ref[r, h]
 
     y = jnp.dot(att[...], w_ref[...], preferred_element_type=F32)
     o_ref[...] = (h_ref[...].astype(F32) + g_ref[...].astype(F32) * y).astype(BF)
 
 
-def project(self_heads, cross_out, w, hidden, gate):
-    copies, heads, rows, _ = self_heads.shape
-    tok, width = cross_out.shape
+def project(attended, w, hidden, gate):
+    copies, heads, rows, _ = attended.shape
+    tok, width = hidden.shape
     nb = 512
     return pl.pallas_call(
         project_kernel,
         grid=(width // nb,),
         in_specs=[
-            pl.BlockSpec(self_heads.shape, lambda i: (0, 0, 0, 0)),
-            pl.BlockSpec((tok, width), lambda i: (0, 0)),
+            pl.BlockSpec(attended.shape, lambda i: (0, 0, 0, 0)),
             pl.BlockSpec((width, nb), lambda i: (0, i)),
             pl.BlockSpec((tok, nb), lambda i: (0, i)),
             pl.BlockSpec((1, nb), lambda i: (0, i)),
@@ -220,42 +216,59 @@
         scratch_shapes=[pltpu.VMEM((tok, width), BF)],
         compiler_params=params(),
         name="project",
-    )(self_heads, cross_out, w, hidden, gate)
+    )(attended, w, hidden, gate)
+
+
+SWAP = [(0, 1), (1, 0)]
+CHUNKS = 4
+
+
+def swap(chunks, axis):
+    return [lax.ppermute(x, axis, SWAP) for x in chunks]
 
 
 def local(hidden_in, queries, keys, values, out_weight, gate):
     hidden, q, k, v = hidden_in[0], queries[0], keys[0], values[0]
-    tok, width = q.shape
-    copies = lax.axis_size("y")
-    seq = ("y", "z", "xh")
-    view = ("xl", "c")
-    rows = tok // copies
-    n = copies * HEADS
-
-    packed = pack(q, k, v, copies).reshape(n, 3 * rows, HD)
-    got = lax.all_to_all(packed, seq, split_axis=0, concat_axis=0, tiled=True)
+    tok, _ = q.shape
+    seq = ("yv", "yr", "z", "xh")
+    rows = tok // 4
+    n = 4 * HEADS
+
+    packed = pack(q, k, v, 4)
+    mine = lax.all_to_all(packed, "c", split_axis=0, concat_axis=0, tiled=True)
+    mine = mine.reshape(2, 2, HEADS, 3, rows, HD)
+    got = lax.all_to_all(mine.reshape(n, 3 * rows, HD), seq, split_axis=0, concat_axis=0, tiled=True)
     got = got.reshape(n, 3, rows, HD)
-    k_views = lax.all_gather(k, view, axis=0)
-    v_views = lax.all_gather(v, view, axis=0)
-
-    kv = got[:, 1:]
-    kv_all = lax.all_gather(kv, "y", axis=0, tiled=True)
-    state = None
-    o = attend(got, [kv_all], state, True)
-    cross_out = cross(q, k_views, v_views)
+
+    step = n // CHUNKS
+    own = [got[i * step : (i + 1) * step, 1:] for i in range(CHUNKS)]
+    mate = swap([got[: n // 2, 1:], got[n // 2 :, 1:]], "yr")
+    other = lax.ppermute(mine[:, :, :, 1:], "xl", SWAP)
+    own_pair = swap(own, "c")
+    state = attend(got, own + own_pair, None, False)
+    mate, other, state = lax.optimization_barrier((mate, other, state))
+    cross_out = cross(mine, other)
+    mate_pair = swap([x[i * step : (i + 1) * step] for x in mate for i in range(2)], "c")
+    cross_out, state = lax.optimization_barrier((cross_out, state))
+    o = attend(got, mate + mate_pair, state, True)
+
     back = lax.all_to_all(o, seq, split_axis=0, concat_axis=0, tiled=True)
-    out = project(back.reshape(copies, HEADS, rows, HD), cross_out, out_weight, hidden, gate)
-    return out[None]
+    attended = (back.reshape(cross_out.shape).astype(F32) + cross_out).astype(BF)
+    attended = lax.all_to_all(
+        attended.reshape(4, HEADS, rows, HD), "c", split_axis=0, concat_axis=0, tiled=True
+    )
+    return project(attended, out_weight, hidden, gate)[None]
 
 
 def solution(mesh):
     devices = np.asarray(mesh.devices)
-    fine = Mesh(devices.reshape(2, 2, 4, 8, 2), ("xl", "c", "y", "z", "xh"))
-    spec = P(("xl", "c"), ("y", "z", "xh"), None)
+    fine = Mesh(devices.reshape(2, 2, 2, 2, 8, 2), ("xl", "c", "yv", "yr", "z", "xh"))
+    view, seq = ("xl", "c"), ("yv", "yr", "z", "xh")
+    spec = P(view, seq, None)
     return jax.shard_map(
         local,
         mesh=fine,
-        in_specs=(spec, spec, spec, spec, P(), P(("xl", "c"), None)),
+        in_specs=(spec, spec, spec, spec, P(), P(view, None)),
         out_specs=spec,
         check_vma=False,
     )

time: 202 us -> 148 us (0.73)
  waiting for transfers between devices: 79 us -> 47.7 us
  blocking collectives: 55 us -> 38.1 us
  between operations: 13.1 us -> 0.15 us
  starting transfers between devices: 11.7 us -> 20 us
  Pallas kernels: 40.8 us -> 35.5 us
  local copies, waits for them, and re-layouts: 2.16 us -> 5.8 us
    all_gather x3 -> x0, waiting for transfers between devices: 77.6 us -> none  [the longest x1 45.9 us: local(): kv_all = lax.all_gather(kv, 'y', axis=0, tiled=True)]
    all_to_all x1, waiting for transfers between devices: 0.01 us -> 37.4 us  [local(): lax.all_to_all(mine.reshape(n, 3 * rows, HD), seq, split_axis=0, concat_a...]
    all_to_all x1 -> x3, blocking collectives: 55 us -> 38.1 us  [the longest x1 23 us: local(): back = lax.all_to_all(o, seq, split_axis=0, concat_axis=0, tiled=True)]
    ppermute x0 -> x11, waiting for transfers between devices: none -> 10.4 us  [the longest x10 10.4 us: swap(): return [lax.ppermute(x, axis, SWAP) for x in chunks]]
    ppermute x0 -> x11, starting transfers between devices: none -> 7.46 us  [the longest x10 7.15 us: swap(): return [lax.ppermute(x, axis, SWAP) for x in chunks]]
    pallas_call x1, Pallas kernels: 3.76 us -> 0.58 us  [pack(): pl.pallas_call(pack_kernel, grid=(HEADS // hb,), in_specs=[spec] * 3, out...]
    pallas_call x1, Pallas kernels: 6.38 us -> 3.33 us  [project(): pl.pallas_call(project_kernel, grid=(width // nb,), in_specs=[pl.BlockSpe...]
    pallas_call x1 -> x2, Pallas kernels: 25.5 us -> 28 us  [attend(): pl.pallas_call(functools.partial(attend_kernel, first=state is None, last...]
  transfers between devices with their start and end apart: 4 -> 12, of which waited for: 2 -> 3; matrix products, arithmetic and copies ran while one was open for 0% -> 2% of each run, Pallas kernels for 15% -> 11%
where the time goes in v2:
time: 148 us; the launch traced here: 147 us
  waiting for transfers between devices  47.7 us (32%)
  blocking collectives  38.1 us (26%)
  Pallas kernels  35.5 us (24%)
  starting transfers between devices  20 us (14%)
  local copies, waits for them, and re-layouts  5.8 us (4%)
    all_to_all x1, waiting for transfers between devices, local(): lax.all_to_all(mine.reshape(n, 3 * rows, HD), seq, split_axis=0, concat_a...  37.4 us
    pallas_call x2, Pallas kernels, attend(): pl.pallas_call(functools.partial(attend_kernel, first=state is None, last...  28 us
    all_to_all x1, blocking collectives, local(): back = lax.all_to_all(o, seq, split_axis=0, concat_axis=0, tiled=True)  23 us
    all_to_all x1, starting transfers between devices, local(): lax.all_to_all(mine.reshape(n, 3 * rows, HD), seq, split_axis=0, concat_a...  12.5 us
    ppermute x10, waiting for transfers between devices, swap(): return [lax.ppermute(x, axis, SWAP) for x in chunks]  10.4 us
    all_to_all x1, blocking collectives, local(): mine = lax.all_to_all(packed, 'c', split_axis=0, concat_axis=0, tiled=True)  8.71 us
    ppermute x10, starting transfers between devices, swap(): return [lax.ppermute(x, axis, SWAP) for x in chunks]  7.15 us
    all_to_all x1, blocking collectives, local(): lax.all_to_all(attended.reshape(4, HEADS, rows, HD), 'c', split_axis=0, c...  6.42 us
  transfers between devices with their start and end apart: 12, of which 3 were waited for; matrix products, arithmetic and copies ran while one was open for 2% of the time, Pallas kernels for 11%

profile of v2, /device:TPU:1, one launch (start us, length us, event | category | flops | bytes accessed | tf_op | source)
XLA Modules:
  0.0 147.5 jit_solution(4308524799114253802)
XLA Ops:
  0.0 0.0 copy-start.1
  0.0 1.0 copy-done.1
  1.0 0.0 copy-start.2
  1.0 1.0 copy-done.2
  2.1 0.0 copy-start.3
  2.1 1.0 copy-done.3
  3.1 0.6 pack.1
  3.7 8.7 %all_to_all.20 = bf16[4,16,3,32,128]{4,3,2,1,0:T(8,128)(2,1)} all-to-all(bf16[4,16,3,32,128]{4,3,2,1,0:T(8,128)(2,1)S(1)} %pack.1), channel_id=1, replica_groups=mesh['xl'=2,'c'=2,'yv'=2,'yr'=2,'z'=8,'xh'=2] {'c'}, dimensions={0} | all-to-all | bytes 3145728 | tf_op jit(solution)/shard_map/all_to_all | solution.py:238
  12.4 12.5 %all-to-all-start.1 = ((bf16[64,96,128]{2,1,0:T(8,128)(2,1)}), bf16[64,96,128]{2,1,0:T(8,128)(2,1)S(1)}, u32[]{:S(2)}, u32[]{:S(2)}) async-start(bf16[64,96,128]{2,1,0:T(8,128)(2,1)} %bitcast.3), calls=%async_computation.1 | async-start | bytes 3145728 | tf_op jit(solution)/shard_map/all_to_all | solution.py:240
  25.0 2.3 %slice.46 = bf16[2,2,16,2,32,128]{5,4,3,2,1,0:T(8,128)(2,1)} slice(bf16[2,2,16,3,32,128]{5,4,3,2,1,0:T(8,128)(2,1)} %bitcast.5.a_ref), slice={[0:2], [0:2], [0:16], [1:3], [0:32], [0:128]} | slice | bytes 2097152 | tf_op jit(solution)/shard_map/slice | solution.py:246
  27.3 0.3 collective-permute-start.2
  27.6 37.4 %all-to-all-done.1 = bf16[64,96,128]{2,1,0:T(8,128)(2,1)S(1)} async-done(((bf16[64,96,128]{2,1,0:T(8,128)(2,1)}), bf16[64,96,128]{2,1,0:T(8,128)(2,1)S(1)}, u32[]{:S(2)}, u32[]{:S(2)}) %all-to-all-start.1) | async-done | bytes 1572896 | tf_op jit(solution)/shard_map/all_to_all | solution.py:240
  65.0 0.1 fusion.1
  65.1 2.9 %collective-permute-start.6 = (bf16[16,2,32,128]{3,2,1,0:T(8,128)(2,1)S(1)}, bf16[16,2,32,128]{3,2,1,0:T(8,128)(2,1)S(1)}, u32[]{:S(2)}, u32[]{:S(2)}) collective-permute-start(bf16[16,2,32,128]{3,2,1,0:T(8,128)(2,1)S(1)} %get-tuple-element.25.refs_4_), channel_id=1, source_target_pairs={{0,64},{64,0},{1,65},{65,1},{2,66},{66,2},{3,67},{67,3},{4,68},{68... | collective-permute-start | bytes 786440 | tf_op jit(solution)/shard_map/ppermute | solution.py:227
  68.0 0.1 collective-permute-start.5
  68.1 0.4 collective-permute-start.4
  68.5 0.1 collective-permute-start.3
  68.6 0.1 fusion.2
  68.8 0.4 collective-permute-done.6.refs_8_
  69.2 0.4 collective-permute-start.1
  69.6 0.0 collective-permute-done.5.refs_7_
  69.6 1.1 collective-permute-start
  70.7 0.0 collective-permute-done.4.refs_6_
  70.7 0.0 collective-permute-done.3.refs_5_
  70.7 12.9 %attend.2 = (f32[2048,128]{1,0:T(8,128)S(1)}, f32[2048,256]{1,0:T(8,128)S(1)}) custom-call(bf16[64,3,32,128]{3,2,1,0:T(8,128)(2,1)S(1)} %bitcast.13, bf16[16,2,32,128]{3,2,1,0:T(8,128)(2,1)S(1)} %get-tuple-element.28.refs_1_, bf16[16,2,32,128]{3,2,1,0:T(8,128)(2,1)S(1)} %get-tuple-element.27.refs_2_, bf16[16,2,32,128]{3,2,1,0:T(8,128)(2,1)S(1)} %get-tuple-element.26.refs_3_, ...), custom_call_target="tpu_custom_call" | custom-call | flops 8589934592 | bytes 3145728 | tf_op jit(solution)/shard_map/attend/pallas_call | solution.py:126
  83.6 0.0 collective-permute-done.2.b_ref
  83.6 0.0 collective-permute-done.1.refs_2_
  83.6 10.0 %collective-permute-done.refs_1_ = bf16[32,2,32,128]{3,2,1,0:T(8,128)(2,1)S(1)} collective-permute-done((bf16[32,2,32,128]{3,2,1,0:T(8,128)(2,1)S(1)}, bf16[32,2,32,128]{3,2,1,0:T(8,128)(2,1)S(1)}, u32[]{:S(2)}, u32[]{:S(2)}) %collective-permute-start) | collective-permute-done | bytes 524320 | tf_op jit(solution)/shard_map/ppermute | solution.py:227
  93.6 1.3 collective-permute-start.8
  94.9 0.1 collective-permute-start.7
  95.0 0.5 collective-permute-start.10
  95.5 0.3 collective-permute-start.9
  95.8 0.0 slice-start
  95.8 3.5 %cross.1 = f32[2,2,16,32,128]{4,3,2,1,0:T(8,128)S(1)} custom-call(bf16[2,2,16,3,32,128]{5,4,3,2,1,0:T(8,128)(2,1)} %bitcast.5.a_ref, bf16[2,2,16,2,32,128]{5,4,3,2,1,0:T(8,128)(2,1)S(1)} %collective-permute-done.2.b_ref), custom_call_target="tpu_custom_call" | custom-call | flops 4194304 | bytes 3670016 | tf_op jit(solution)/shard_map/cross/pallas_call | solution.py:171
  99.4 0.0 slice-start.1
  99.4 0.0 collective-permute-done.8.refs_4_
  99.4 0.0 collective-permute-done.7.refs_3_
  99.4 0.0 collective-permute-done.10.refs_6_
  99.4 0.0 collective-permute-done.9.refs_5_
  99.4 15.1 %attend.3 = bf16[64,32,128]{2,1,0:T(8,128)(2,1)S(1)} custom-call(bf16[64,3,32,128]{3,2,1,0:T(8,128)(2,1)S(1)} %bitcast.14, bf16[32,2,32,128]{3,2,1,0:T(8,128)(2,1)S(1)} %collective-permute-done.refs_1_, bf16[32,2,32,128]{3,2,1,0:T(8,128)(2,1)S(1)} %collective-permute-done.1.refs_2_, bf16[16,2,32,128]{3,2,1,0:T(8,128)(2,1)S(1)} %collective-permute-done.7.refs_3_, ...), custom_call_target="tpu_custom_call" | custom-call | flops 8589934592 | bytes 3145728 | tf_op jit(solution)/shard_map/attend/pallas_call | solution.py:126
  114.5 23.0 %all_to_all.21 = bf16[64,32,128]{2,1,0:T(8,128)(2,1)S(1)} all-to-all(bf16[64,32,128]{2,1,0:T(8,128)(2,1)S(1)} %attend.3), channel_id=1, replica_groups=mesh['xl'=2,'c'=2,'yv'=2,'yr'=2,'z'=8,'xh'=2] {'yv','yr','z','xh'}, dimensions={0} | all-to-all | bytes 1048576 | tf_op jit(solution)/shard_map/all_to_all | solution.py:255
  137.6 0.2 fusion
  137.7 6.4 %all_to_all.22.a_ref = bf16[4,16,32,128]{3,2,1,0:T(8,128)(2,1)S(1)} all-to-all(bf16[4,16,32,128]{3,2,1,0:T(8,128)(2,1)S(1)} %bitcast.22), channel_id=1, replica_groups=mesh['xl'=2,'c'=2,'yv'=2,'yr'=2,'z'=8,'xh'=2] {'c'}, dimensions={0} | all-to-all | bytes 1048576 | tf_op jit(solution)/shard_map/all_to_all | solution.py:257
  144.1 0.0 slice-done
  144.1 0.0 slice-done.1
  144.1 0.0 copy-done
  144.1 0.0 copy-done.4
  144.2 3.3 %project.1 = bf16[128,2048]{1,0:T(8,128)(2,1)} custom-call(bf16[4,16,32,128]{3,2,1,0:T(8,128)(2,1)S(1)} %all_to_all.22.a_ref, bf16[2048,2048]{1,0:T(8,128)(2,1)S(1)} %bitcast.16, bf16[128,2048]{1,0:T(8,128)(2,1)S(1)} %bitcast.17, bf16[1,2048]{1,0:T(2,128)(2,1)S(1)} %copy-done.4), custom_call_target="tpu_custom_call" | custom-call | tf_op jit(solution)/shard_map/project/pallas_call | solution.py:205
  (5 shorter events, 0.1 us)
Async XLA Ops:
  0.0 1.0 copy-start.1
  1.0 1.0 copy-start.2
  2.1 1.0 copy-start.3
  12.4 52.6 %all-to-all-start.1 = ((bf16[64,96,128]{2,1,0:T(8,128)(2,1)}), bf16[64,96,128]{2,1,0:T(8,128)(2,1)S(1)}, u32[]{:S(2)}, u32[]{:S(2)}) async-start(bf16[64,96,128]{2,1,0:T(8,128)(2,1)} %bitcast.3), calls=%async_computation.1 | async-start | bytes 3145728 | tf_op jit(solution)/shard_map/all_to_all | solution.py:240
  27.3 56.3 %collective-permute-start.2 = (bf16[2,2,16,2,32,128]{5,4,3,2,1,0:T(8,128)(2,1)}, bf16[2,2,16,2,32,128]{5,4,3,2,1,0:T(8,128)(2,1)S(1)}, u32[]{:S(2)}, u32[]{:S(2)}) collective-permute-start(bf16[2,2,16,2,32,128]{5,4,3,2,1,0:T(8,128)(2,1)} %slice.46), channel_id=1, source_target_pairs={{0,128},{128,0},{1,129},{129,1},{2,130},{130,2},{3,131},{131,3},{4... | collective-permute-start | bytes 3145736 | tf_op jit(solution)/shard_map/ppermute | solution.py:246
  65.1 4.1 %collective-permute-start.6 = (bf16[16,2,32,128]{3,2,1,0:T(8,128)(2,1)S(1)}, bf16[16,2,32,128]{3,2,1,0:T(8,128)(2,1)S(1)}, u32[]{:S(2)}, u32[]{:S(2)}) collective-permute-start(bf16[16,2,32,128]{3,2,1,0:T(8,128)(2,1)S(1)} %get-tuple-element.25.refs_4_), channel_id=1, source_target_pairs={{0,64},{64,0},{1,65},{65,1},{2,66},{66,2},{3,67},{67,3},{4,68},{68... | collective-permute-start | bytes 786440 | tf_op jit(solution)/shard_map/ppermute | solution.py:227
  68.0 1.6 %collective-permute-start.5 = (bf16[16,2,32,128]{3,2,1,0:T(8,128)(2,1)S(1)}, bf16[16,2,32,128]{3,2,1,0:T(8,128)(2,1)S(1)}, u32[]{:S(2)}, u32[]{:S(2)}) collective-permute-start(bf16[16,2,32,128]{3,2,1,0:T(8,128)(2,1)S(1)} %get-tuple-element.26.refs_3_), channel_id=1, source_target_pairs={{0,64},{64,0},{1,65},{65,1},{2,66},{66,2},{3,67},{67,3},{4,68},{68... | collective-permute-start | bytes 786440 | tf_op jit(solution)/shard_map/ppermute | solution.py:227
  68.1 2.5 %collective-permute-start.4 = (bf16[16,2,32,128]{3,2,1,0:T(8,128)(2,1)S(1)}, bf16[16,2,32,128]{3,2,1,0:T(8,128)(2,1)S(1)}, u32[]{:S(2)}, u32[]{:S(2)}) collective-permute-start(bf16[16,2,32,128]{3,2,1,0:T(8,128)(2,1)S(1)} %get-tuple-element.27.refs_2_), channel_id=1, source_target_pairs={{0,64},{64,0},{1,65},{65,1},{2,66},{66,2},{3,67},{67,3},{4,68},{68... | collective-permute-start | bytes 786440 | tf_op jit(solution)/shard_map/ppermute | solution.py:227
  68.5 2.1 %collective-permute-start.3 = (bf16[16,2,32,128]{3,2,1,0:T(8,128)(2,1)S(1)}, bf16[16,2,32,128]{3,2,1,0:T(8,128)(2,1)S(1)}, u32[]{:S(2)}, u32[]{:S(2)}) collective-permute-start(bf16[16,2,32,128]{3,2,1,0:T(8,128)(2,1)S(1)} %get-tuple-element.28.refs_1_), channel_id=1, source_target_pairs={{0,64},{64,0},{1,65},{65,1},{2,66},{66,2},{3,67},{67,3},{4,68},{68... | collective-permute-start | bytes 786440 | tf_op jit(solution)/shard_map/ppermute | solution.py:227
  69.2 14.4 %collective-permute-start.1 = (bf16[32,2,32,128]{3,2,1,0:T(8,128)(2,1)S(1)}, bf16[32,2,32,128]{3,2,1,0:T(8,128)(2,1)S(1)}, u32[]{:S(2)}, u32[]{:S(2)}) collective-permute-start(bf16[32,2,32,128]{3,2,1,0:T(8,128)(2,1)S(1)} %get-tuple-element.29), channel_id=1, source_target_pairs={{0,16},{16,0},{1,17},{17,1},{2,18},{18,2},{3,19},{19,3},{4,20},{20... | collective-permute-start | bytes 1572872 | tf_op jit(solution)/shard_map/ppermute | solution.py:227
  69.6 24.0 %collective-permute-start = (bf16[32,2,32,128]{3,2,1,0:T(8,128)(2,1)S(1)}, bf16[32,2,32,128]{3,2,1,0:T(8,128)(2,1)S(1)}, u32[]{:S(2)}, u32[]{:S(2)}) collective-permute-start(bf16[32,2,32,128]{3,2,1,0:T(8,128)(2,1)S(1)} %get-tuple-element.30), channel_id=1, source_target_pairs={{0,16},{16,0},{1,17},{17,1},{2,18},{18,2},{3,19},{19,3},{4,20},{20... | collective-permute-start | bytes 1572872 | tf_op jit(solution)/shard_map/ppermute | solution.py:227
  93.6 5.8 %collective-permute-start.8 = (bf16[16,2,32,128]{3,2,1,0:T(8,128)(2,1)S(1)}, bf16[16,2,32,128]{3,2,1,0:T(8,128)(2,1)S(1)}, u32[]{:S(2)}, u32[]{:S(2)}) collective-permute-start(bf16[16,2,32,128]{3,2,1,0:T(8,128)(2,1)S(1)} %get-tuple-element.33), channel_id=1, source_target_pairs={{0,64},{64,0},{1,65},{65,1},{2,66},{66,2},{3,67},{67,3},{4,68},{68... | collective-permute-start | bytes 786440 | tf_op jit(solution)/shard_map/ppermute | solution.py:227
  94.9 4.5 %collective-permute-start.7 = (bf16[16,2,32,128]{3,2,1,0:T(8,128)(2,1)S(1)}, bf16[16,2,32,128]{3,2,1,0:T(8,128)(2,1)S(1)}, u32[]{:S(2)}, u32[]{:S(2)}) collective-permute-start(bf16[16,2,32,128]{3,2,1,0:T(8,128)(2,1)S(1)} %get-tuple-element.34), channel_id=1, source_target_pairs={{0,64},{64,0},{1,65},{65,1},{2,66},{66,2},{3,67},{67,3},{4,68},{68... | collective-permute-start | bytes 786440 | tf_op jit(solution)/shard_map/ppermute | solution.py:227
  95.0 4.4 %collective-permute-start.10 = (bf16[16,2,32,128]{3,2,1,0:T(8,128)(2,1)S(1)}, bf16[16,2,32,128]{3,2,1,0:T(8,128)(2,1)S(1)}, u32[]{:S(2)}, u32[]{:S(2)}) collective-permute-start(bf16[16,2,32,128]{3,2,1,0:T(8,128)(2,1)S(1)} %get-tuple-element.31), channel_id=1, source_target_pairs={{0,64},{64,0},{1,65},{65,1},{2,66},{66,2},{3,67},{67,3},{4,68},{68... | collective-permute-start | bytes 786440 | tf_op jit(solution)/shard_map/ppermute | solution.py:227
  95.5 3.9 %collective-permute-start.9 = (bf16[16,2,32,128]{3,2,1,0:T(8,128)(2,1)S(1)}, bf16[16,2,32,128]{3,2,1,0:T(8,128)(2,1)S(1)}, u32[]{:S(2)}, u32[]{:S(2)}) collective-permute-start(bf16[16,2,32,128]{3,2,1,0:T(8,128)(2,1)S(1)} %get-tuple-element.32), channel_id=1, source_target_pairs={{0,64},{64,0},{1,65},{65,1},{2,66},{66,2},{3,67},{67,3},{4,68},{68... | collective-permute-start | bytes 786440 | tf_op jit(solution)/shard_map/ppermute | solution.py:227
  95.8 48.3 %slice-start = ((s8[8388608]{0:T(1024)(128)(4,1)}), s8[4194304]{0:T(1024)(128)(4,1)S(1)}, s32[]{:S(2)}) async-start(s8[8388608]{0:T(1024)(128)(4,1)} %bitcast.15), calls=%async_computation.4 | async-start | bytes 8388608
  99.4 44.8 %slice-start.1 = ((s8[8388608]{0:T(1024)(128)(4,1)}), s8[4194304]{0:T(1024)(128)(4,1)S(1)}, s32[]{:S(2)}) async-start(s8[8388608]{0:T(1024)(128)(4,1)} %bitcast.15), calls=%async_computation.5 | async-start | bytes 8388608
  137.6 6.6 %copy-start = (bf16[1,128,2048]{2,1,0:T(8,128)(2,1)S(1)}, bf16[1,128,2048]{2,1,0:T(8,128)(2,1)}, u32[]{:S(2)}) copy-start(bf16[1,128,2048]{2,1,0:T(8,128)(2,1)} %param.6) | copy-start | bytes 1572868
  137.6 6.6 %copy-start.4 = (bf16[1,2048]{1,0:T(2,128)(2,1)S(1)}, bf16[1,2048]{1,0:T(2,128)(2,1)}, u32[]{:S(2)}) copy-start(bf16[1,2048]{1,0:T(2,128)(2,1)} %g_ref.1) | copy-start | bytes 12292

commit v3 on v2

v3 whole, which is shorter than its diff:
```python
import functools
import math

import jax
import jax.numpy as jnp
import numpy as np
from jax import lax
from jax.experimental import pallas as pl
from jax.experimental.pallas import tpu as pltpu
from jax.sharding import Mesh, PartitionSpec as P

HEADS = 16
HD = 128
BF = jnp.bfloat16
F32 = jnp.float32
SCALE = HD**-0.5
LOG2E = math.log2(math.e)
NT = (((1,), (1,)), ((), ()))
VMEM_CAP = 30 * 2**20


def params(**kw):
    return pltpu.CompilerParams(vmem_limit_bytes=VMEM_CAP, **kw)


def whole(n):
    return [pl.BlockSpec(memory_space=pltpu.VMEM)] * n


def pack_kernel(q_ref, k_ref, v_ref, o_ref, sq_ref, sk_ref, sv_ref, held, sems):
    _, parts, heads, _, rows, _ = o_ref.shape
    half = parts * rows
    me = lax.axis_index("c")
    moves = []
    for to, core in ((0, 1 - me), (1, me)):
        for j, ref in enumerate((q_ref, k_ref, v_ref)):
            part = pl.ds(pl.multiple_of(core * half, half), half)
            moves.append(pltpu.make_async_copy(ref.at[part], held.at[to, j], sems.at[to, j]))
    for move in moves:
        move.start()
    for j, out in enumerate((sq_ref, sk_ref, sv_ref)):
        moves[j].wait()
        for r in range(parts):
            for h in range(heads):
                out[r, h] = held[0, j, r * rows : (r + 1) * rows, h * HD : (h + 1) * HD]
    for j in range(3):
        moves[3 + j].wait()
        for r in range(parts):
            for h in range(heads):
                o_ref[me, r, h, j] = held[1, j, r * rows : (r + 1) * rows, h * HD : (h + 1) * HD]


def pack(q, k, v):
    tok, width = q.shape
    rows = tok // 4
    away = jax.ShapeDtypeStruct((2, HEADS, rows, HD), BF)
    return pl.pallas_call(
        pack_kernel,
        in_specs=[pl.BlockSpec(memory_space=pltpu.HBM)] * 3,
        out_specs=whole(4),
        out_shape=[jax.ShapeDtypeStruct((2, 2, HEADS, 3, rows, HD), BF)] + [away] * 3,
        scratch_shapes=[
            pltpu.VMEM((2, 3, tok // 2, width), BF),
            pltpu.SemaphoreType.DMA((2, 3)),
        ],
        compiler_params=params(),
        name="pack",
    )(*(pltpu.with_memory_space_constraint(x, pltpu.HBM) for x in (q, k, v)))


def place_kernel(a_ref, q_ref, k_ref, v_ref, o_ref):
    _, parts, heads = a_ref.shape[:3]
    you = 1 - lax.axis_index("c")
    for j, ref in enumerate((q_ref, k_ref, v_ref)):
        for r in range(parts):
            for h in range(heads):
                o_ref[you, r, h, j] = ref[r, h]


def place(mine, got):
    return pl.pallas_call(
        place_kernel,
        in_specs=whole(4),
        out_specs=pl.BlockSpec(memory_space=pltpu.VMEM),
        out_shape=jax.ShapeDtypeStruct(mine.shape, BF),
        input_output_aliases={0: 0},
        compiler_params=params(),
        name="place",
    )(mine, *got)


def gather_kv(kv_refs, k_all, v_all):
    at = 0
    for ref in kv_refs:
        n = ref.shape[0] * ref.shape[2]
        k_all[at : at + n, :] = ref[:, 0].reshape(n, HD)
        v_all[at : at + n, :HD] = ref[:, 1].reshape(n, HD)
        at += n
    v_all[:, HD:] = jnp.ones((at, HD), BF)


def eye():
    shape = (HD, HD)
    return lax.broadcasted_iota(jnp.int32, shape, 0) == lax.broadcasted_iota(jnp.int32, shape, 1)


def attend_block(q, k_all, v_all, kb):
    c = SCALE * LOG2E
    total = k_all.shape[0]

    def score(i):
        return lax.dot_general(q, k_all[i * kb : (i + 1) * kb, :], NT, preferred_element_type=F32)

    m = acc = None
    s = score(0)
    for i in range(total // kb):
        following = score(i + 1) if (i + 1) * kb < total else None
        peak = jnp.max(s, axis=1, keepdims=True) * c
        new = peak if m is None else jnp.maximum(m, peak)
        p = jnp.exp2(s * c - new).astype(BF)
        add = jnp.dot(p, v_all[i * kb : (i + 1) * kb, :], preferred_element_type=F32)
        acc = add if acc is None else acc * jnp.exp2(m - new) + add
        m, s = new, following
    return acc[:, :HD] / acc[:, HD:], m + jnp.log2(acc[:, HD:])


def attend_kernel(*refs, first, travels, qb, kb):
    if first:
        q_ref, *kv_refs, o_ref, l_ref, k_all, v_all = refs
        gather_kv(kv_refs, k_all, v_all)
    else:
        q_ref, k_all, v_all, o_ref, l_ref = refs
    src, rows, _ = q_ref.shape
    qsrc = qb // rows
    diag = eye()
    for j in range(src // qsrc):
        q = q_ref[j * qsrc : (j + 1) * qsrc].reshape(qb, HD)
        o, lse = attend_block(q, k_all, v_all, kb)
        o_ref[j * qsrc : (j + 1) * qsrc] = o.reshape(qsrc, rows, HD).astype(o_ref.dtype)
        for g in range(qb // HD):
            line = jnp.where(diag, lse[g * HD : (g + 1) * HD], 0.0)
            l_ref[j * (qb // HD) + g, :] = jnp.sum(line, axis=0)
    if travels:
        lines = l_ref.shape[0]
        lse = l_ref[...]
        terms = []
        for _ in range(3):
            terms.append(lse.astype(BF))
            lse = lse - terms[-1].astype(F32)
        terms.append(jnp.zeros((rows - 3 * lines, HD), BF))
        o_ref[src] = jnp.concatenate(terms, axis=0)


def attend(q, kv, first, travels, qb=512, kb=2048):
    src, rows, _ = q.shape
    nq = src * rows
    total = sum(a.shape[0] * a.shape[2] for a in kv) if first else kv[0].shape[0]
    out_shape = [
        jax.ShapeDtypeStruct((src + travels, rows, HD), BF if travels else F32),
        jax.ShapeDtypeStruct((nq // HD, HD), F32),
    ]
    if first:
        out_shape += [
            jax.ShapeDtypeStruct((total, HD), BF),
            jax.ShapeDtypeStruct((total, 2 * HD), BF),
        ]
    return pl.pallas_call(
        functools.partial(attend_kernel, first=first, travels=travels, qb=qb, kb=min(kb, total)),
        in_specs=whole(1 + len(kv)),
        out_specs=whole(len(out_shape)),
        out_shape=out_shape,
        compiler_params=params(),
        cost_estimate=pl.CostEstimate(
            flops=0,
            bytes_accessed=0,
            transcendentals=0,
        ),
        name="attend",
    )(q, *kv)


def merge_kernel(*refs):
    *parts, out_ref = refs
    diag = eye()
    at = 0
    while parts:
        oa, la, ob = parts[:3]
        parts = parts[3:]
        src, rows, _ = oa.shape
        lines, per = la.shape[0], HD // rows
        terms = ob[src].astype(F32)
        lb = terms[:lines] + terms[lines : 2 * lines] + terms[2 * lines : 3 * lines]
        peak = jnp.maximum(la[...], lb)
        ea, eb = jnp.exp2(la[...] - peak), jnp.exp2(lb - peak)
        wa = ea / (ea + eb)
        for g in range(lines):
            w = jnp.sum(jnp.where(diag, wa[g : g + 1, :], 0.0), axis=1, keepdims=True)
            a = oa[g * per : (g + 1) * per].reshape(HD, HD)
            b = ob[g * per : (g + 1) * per].reshape(HD, HD).astype(F32)
            out = (b + w * (a - b)).astype(BF)
            out_ref[at + g * per : at + (g + 1) * per] = out.reshape(per, rows, HD)
        at += src


def merge(parts):
    src = sum(p[0].shape[0] for p in parts)
    flat = [x for p in parts for x in p]
    return pl.pallas_call(
        merge_kernel,
        in_specs=whole(len(flat)),
        out_specs=pl.BlockSpec(memory_space=pltpu.VMEM),
        out_shape=jax.ShapeDtypeStruct((src,) + parts[0][0].shape[1:], BF),
        compiler_params=params(),
        name="merge",
    )(*flat)


def cross_kernel(a_ref, b_ref, o_ref):
    views, parts, heads = a_ref.shape[:3]

    def one_head(h, carry):
        for r in range(parts):
            ks = [a_ref[b, r, h, 1].astype(F32) for b in range(views)]
            ks += [b_ref[b, r, h, 0].astype(F32) for b in range(views)]
            vs = [a_ref[b, r, h, 2].astype(F32) for b in range(views)]
            vs += [b_ref[b, r, h, 1].astype(F32) for b in range(views)]
            for a in range(views):
                q = a_ref[a, r, h, 0].astype(F32)
                s = [jnp.sum(q * k, axis=1, keepdims=True) * SCALE for k in ks]
                peak = functools.reduce(jnp.maximum, s)
                e = [jnp.exp(x - peak) for x in s]
                inv = 1.0 / functools.reduce(jnp.add, e)
                terms = [(x * inv).astype(BF).astype(F32) * v for x, v in zip(e, vs)]
                o_ref[a, r, h] = functools.reduce(jnp.add, terms)
        return carry

    lax.fori_loop(0, heads, one_head, 0)


def cross(mine, other):
    views, parts, heads, _, rows, _ = mine.shape
    return pl.pallas_call(
        cross_kernel,
        in_specs=whole(2),
        out_specs=pl.BlockSpec(memory_space=pltpu.VMEM),
        out_shape=jax.ShapeDtypeStruct((views, parts, heads, rows, HD), F32),
        compiler_params=params(),
        name="cross",
    )(mine, other)


def add_kernel(s_ref, c_ref, keep_ref, send_ref):
    me = lax.axis_index("c")
    for view, out in ((1 - me, send_ref), (me, keep_ref)):
        out[...] = (s_ref[view].astype(F32) + c_ref[view]).astype(BF)


def add_cross(self_out, cross_out):
    out = jax.ShapeDtypeStruct(self_out.shape[1:], BF)
    return pl.pallas_call(
        add_kernel,
        in_specs=whole(2),
        out_specs=whole(2),
        out_shape=[out, out],
        compiler_params=params(),
        name="add_cross",
    )(self_out, cross_out)


def project_kernel(keep_ref, came_ref, w_ref, h_ref, g_ref, o_ref, att):
    half = o_ref.shape[0] // 2
    me = lax.axis_index("c")
    for core, ref in ((me, keep_ref), (1 - me, came_ref)):
        parts, heads, rows, _ = ref.shape
        for r in range(parts):
            at = pl.ds(pl.multiple_of(core * half + r * rows, rows), rows)
            for h in range(heads):
                att[at, h * HD : (h + 1) * HD] = ref[r, h]
    nb = 512
    for i in range(o_ref.shape[1] // nb):
        cols = slice(i * nb, (i + 1) * nb)
        y = jnp.dot(att[...], w_ref[:, cols], preferred_element_type=F32)
        o_ref[:, cols] = (h_ref[:, cols].astype(F32) + g_ref[:, cols].astype(F32) * y).astype(BF)


def project(keep, came, w, hidden, gate):
    return pl.pallas_call(
        project_kernel,
        in_specs=whole(5),
        out_specs=pl.BlockSpec(memory_space=pltpu.VMEM),
        out_shape=jax.ShapeDtypeStruct(hidden.shape, BF),
        scratch_shapes=[pltpu.VMEM(hidden.shape, BF)],
        compiler_params=params(),
        name="project",
    )(keep, came, w, hidden, gate)


SWAP = [(0, 1), (1, 0)]
CHUNKS = 4


def swap(chunks, axis):
    return [lax.ppermute(x, axis, SWAP) for x in chunks]


def local(hidden_in, queries, keys, values, out_weight, gate):
    hidden, q, k, v = hidden_in[0], queries[0], keys[0], values[0]
    tok, _ = q.shape
    seq = ("yv", "yr", "z", "xh")
    rows = tok // 4
    n = 4 * HEADS

    mine, *away = pack(q, k, v)
    mine = place(mine, swap(away, "c"))
    got = lax.all_to_all(mine.reshape(n, 3 * rows, HD), seq, split_axis=0, concat_axis=0, tiled=True)
    got = got.reshape(n, 3, rows, HD)

    step, half = n // CHUNKS, n // 2
    own = [got[i * step : (i + 1) * step, 1:] for i in range(CHUNKS)]
    own_pair = swap(own, "c")
    qs = [got[:half, 0], got[half:, 0]]
    mate_q = swap(qs, "yr")

    o1, l1, keys_all, values_all = attend(qs[0], own + own_pair, True, False)
    kv = keys_all, values_all
    q_in, away, o1 = lax.optimization_barrier((mate_q[0], mine, o1))
    other = lax.ppermute(away[:, :, :, 1:], "xl", SWAP)
    mo1, _ = attend(q_in, kv, False, True)
    back1 = lax.ppermute(mo1, "yr", SWAP)
    q_in, mo1 = lax.optimization_barrier((mate_q[1], mo1))
    mo2, _ = attend(q_in, kv, False, True)
    back2 = lax.ppermute(mo2, "yr", SWAP)
    q_in, back1, mo2 = lax.optimization_barrier((qs[1], back1, mo2))
    o2, l2 = attend(q_in, kv, False, False)
    o = merge([(o1, l1, back1), (o2, l2, back2)])
    back = lax.all_to_all(o, seq, split_axis=0, concat_axis=0, tiled=True)
    here, back = lax.optimization_barrier((mine, back))
    cross_out = cross(here, other)
    keep, send = add_cross(back.reshape(cross_out.shape), cross_out)
    came = lax.ppermute(send, "c", SWAP)
    return project(keep, came, out_weight, hidden, gate)[None]


def solution(mesh):
    devices = np.asarray(mesh.devices)
    fine = Mesh(devices.reshape(2, 2, 2, 2, 8, 2), ("xl", "c", "yv", "yr", "z", "xh"))
    view, seq = ("xl", "c"), ("yv", "yr", "z", "xh")
    spec = P(view, seq, None)
    return jax.shard_map(
        local,
        mesh=fine,
        in_specs=(spec, spec, spec, spec, P(), P(view, None)),
        out_specs=spec,
        check_vma=False,
    )
```

time: 148 us -> 123 us (0.83)
  waiting for transfers between devices: 47.7 us -> 3.23 us
  blocking collectives: 38.1 us -> 75.2 us
  Pallas kernels: 35.5 us -> 28.7 us
  local copies, waits for them, and re-layouts: 5.8 us -> 0.29 us
  starting transfers between devices: 20 us -> 15.3 us
    all_to_all x1 -> x0, waiting for transfers between devices: 37.4 us -> none  [local(): lax.all_to_all(mine.reshape(n, 3 * rows, HD), seq, split_axis=0, concat_a...]
    all_to_all x2 -> x1, blocking collectives: 15.1 us -> 52.3 us  [local(): lax.all_to_all(mine.reshape(n, 3 * rows, HD), seq, split_axis=0, concat_a...]
    all_to_all x1 -> x0, starting transfers between devices: 12.5 us -> none  [local(): lax.all_to_all(mine.reshape(n, 3 * rows, HD), seq, split_axis=0, concat_a...]
    ppermute x10 -> x9, waiting for transfers between devices: 10.4 us -> 2.06 us  [swap(): return [lax.ppermute(x, axis, SWAP) for x in chunks]]
    pallas_call x5 -> x10, Pallas kernels: 35.5 us -> 28.7 us  [the longest x4 21.6 us: attend(): pl.pallas_call(functools.partial(attend_kernel, first=first, travels=trav...]
    ppermute x1 -> x4, starting transfers between devices: 0.31 us -> 6.46 us  [the longest x1 4.6 us: local(): came = lax.ppermute(send, 'c', SWAP)]
    unnamed x14 -> x8, local copies, waits for them, and re-layouts: 3.14 us -> 0.02 us
    slice x4 -> x1, local copies, waits for them, and re-layouts: 2.52 us -> 0.12 us  [local(): other = lax.ppermute(away[:, :, :, 1:], 'xl', SWAP)]
  transfers between devices with their start and end apart: 12 -> 13, of which waited for: 3 -> 6; matrix products, arithmetic and copies ran while one was open for 2% -> 0% of each run, Pallas kernels for 11% -> 18%
where the time goes in v3:
time: 123 us
  blocking collectives  75.2 us (61%)
  Pallas kernels  28.7 us (23%)
  starting transfers between devices  15.3 us (12%)
  waiting for transfers between devices  3.23 us (3%)
    all_to_all x1, blocking collectives, local(): lax.all_to_all(mine.reshape(n, 3 * rows, HD), seq, split_axis=0, concat_a...  52.3 us
    all_to_all x1, blocking collectives, local(): back = lax.all_to_all(o, seq, split_axis=0, concat_axis=0, tiled=True)  22.9 us
    pallas_call x4, Pallas kernels, attend(): pl.pallas_call(functools.partial(attend_kernel, first=first, travels=trav...  21.6 us
    ppermute x9, starting transfers between devices, swap(): return [lax.ppermute(x, axis, SWAP) for x in chunks]  8.88 us
    ppermute x1, starting transfers between devices, local(): came = lax.ppermute(send, 'c', SWAP)  4.6 us
    pallas_call x1, Pallas kernels, cross(): pl.pallas_call(cross_kernel, in_specs=whole(2), out_specs=pl.BlockSpec(me...  2.95 us
  transfers between devices with their start and end apart: 13, of which 6 were waited for; matrix products, arithmetic and copies ran while one was open for 0% of the time, Pallas kernels for 18%

profile of v3, /device:TPU:1, one launch (start us, length us, event | category | flops | bytes accessed | tf_op | source)
XLA Modules:
  0.0 122.9 jit_solution(4251435390801564301)
XLA Ops:
  0.0 1.4 %pack.1 = (bf16[2,2,16,3,32,128]{5,4,3,2,1,0:T(8,128)(2,1)S(1)}, bf16[2,16,32,128]{3,2,1,0:T(8,128)(2,1)S(1)}, bf16[2,16,32,128]{3,2,1,0:T(8,128)(2,1)S(1)}, bf16[2,16,32,128]{3,2,1,0:T(8,128)(2,1)S(1)}) custom-call(bf16[128,2048]{1,0:T(8,128)(2,1)} %bitcast.23, bf16[128,2048]{1,0:T(8,128)(2,1)} %bitcast.24, bf16[128,2048]{1,0:T(8,128)(2,1)} %bitcast.25), custom_call_target="tpu_custom_call" | custom-call | tf_op jit(solution)/shard_map/pack/pallas_call | solution.py:57
  1.4 3.3 %collective-permute-start = (bf16[2,16,32,128]{3,2,1,0:T(8,128)(2,1)S(1)}, bf16[2,16,32,128]{3,2,1,0:T(8,128)(2,1)S(1)}, u32[]{:S(2)}, u32[]{:S(2)}) collective-permute-start(bf16[2,16,32,128]{3,2,1,0:T(8,128)(2,1)S(1)} %get-tuple-element.28), channel_id=1, source_target_pairs={{0,64},{64,0},{1,65},{65,1},{2,66},{66,2},{3,67},{67,3},{4,68},{68... | collective-permute-start | bytes 786440 | tf_op jit(solution)/shard_map/ppermute | solution.py:303
  4.8 0.1 collective-permute-start.1
  4.9 0.4 collective-permute-start.2
  5.3 0.7 collective-permute-done.q_ref
  5.9 0.4 collective-permute-done.1.k_ref
  6.3 0.4 collective-permute-done.2.v_ref
  6.7 0.1 place.1.a_ref
  6.8 52.3 %all_to_all.10 = bf16[64,96,128]{2,1,0:T(8,128)(2,1)S(1)} all-to-all(bf16[64,96,128]{2,1,0:T(8,128)(2,1)S(1)} %bitcast.16), channel_id=1, replica_groups=mesh['xl'=2,'c'=2,'yv'=2,'yr'=2,'z'=8,'xh'=2] {'yv','yr','z','xh'}, dimensions={0} | all-to-all | bytes 3145728 | tf_op jit(solution)/shard_map/all_to_all | solution.py:315
  59.1 0.1 fusion
  59.2 2.9 %collective-permute-start.4 = (bf16[16,2,32,128]{3,2,1,0:T(8,128)(2,1)S(1)}, bf16[16,2,32,128]{3,2,1,0:T(8,128)(2,1)S(1)}, u32[]{:S(2)}, u32[]{:S(2)}) collective-permute-start(bf16[16,2,32,128]{3,2,1,0:T(8,128)(2,1)S(1)} %get-tuple-element.54.refs_1_), channel_id=1, source_target_pairs={{0,64},{64,0},{1,65},{65,1},{2,66},{66,2},{3,67},{67,3},{4,68},{68... | collective-permute-start | bytes 786440 | tf_op jit(solution)/shard_map/ppermute | solution.py:303
  62.1 0.1 collective-permute-start.5
  62.2 0.5 collective-permute-start.6
  62.7 0.1 collective-permute-start.7
  62.8 0.4 collective-permute-start.3
  63.2 0.0 collective-permute-done.4.refs_5_
  63.3 1.0 collective-permute-start.9
  64.3 0.0 collective-permute-done.5.refs_6_
  64.3 0.0 collective-permute-done.6.refs_7_
  64.3 0.1 collective-permute-done.7.refs_8_
  64.4 5.4 %attend.4 = (f32[32,32,128]{2,1,0:T(8,128)S(1)}, f32[8,128]{1,0:T(8,128)S(1)}, bf16[4096,128]{1,0:T(8,128)(2,1)S(1)}, bf16[4096,256]{1,0:T(8,128)(2,1)S(1)}) custom-call(bf16[32,32,128]{2,1,0:T(8,128)(2,1)S(1)} %get-tuple-element.50.refs_0_, bf16[16,2,32,128]{3,2,1,0:T(8,128)(2,1)S(1)} %get-tuple-element.54.refs_1_, ...), custom_call_target="tpu_custom_call" | custom-call | tf_op jit(solution)/shard_map/attend/pallas_call | solution.py:167
  69.8 0.5 collective-permute-done.3.refs_0_
  70.3 5.6 %attend.5 = (bf16[33,32,128]{2,1,0:T(8,128)(2,1)S(1)}, f32[8,128]{1,0:T(8,128)}) custom-call(bf16[32,32,128]{2,1,0:T(8,128)(2,1)S(1)} %collective-permute-done.3.refs_0_, bf16[4096,128]{1,0:T(8,128)(2,1)S(1)} %get-tuple-element.35.refs_1_, bf16[4096,256]{1,0:T(8,128)(2,1)S(1)} %get-tuple-element.36.refs_2_), custom_call_target="tpu_custom_call" | custom-call | tf_op jit(solution)/shard_map/attend/pallas_call | solution.py:167
  75.9 0.4 collective-permute-start.8
  76.3 0.0 collective-permute-done.9.refs_0_
  76.3 0.0 slice-start
  76.3 5.6 %attend.6 = (bf16[33,32,128]{2,1,0:T(8,128)(2,1)S(1)}, f32[8,128]{1,0:T(8,128)}) custom-call(bf16[32,32,128]{2,1,0:T(8,128)(2,1)S(1)} %collective-permute-done.9.refs_0_, bf16[4096,128]{1,0:T(8,128)(2,1)S(1)} %get-tuple-element.35.refs_1_, bf16[4096,256]{1,0:T(8,128)(2,1)S(1)} %get-tuple-element.36.refs_2_), custom_call_target="tpu_custom_call" | custom-call | tf_op jit(solution)/shard_map/attend/pallas_call | solution.py:167
  81.9 1.1 collective-permute-start.10
  83.0 0.1 slice.27
  83.1 0.0 slice-start.1
  83.1 0.4 collective-permute-start.11
  83.5 0.0 collective-permute-done.8.refs_2_
  83.5 5.0 %attend.7 = (f32[32,32,128]{2,1,0:T(8,128)S(1)}, f32[8,128]{1,0:T(8,128)S(1)}) custom-call(bf16[32,32,128]{2,1,0:T(8,128)(2,1)S(1)} %get-tuple-element.41.refs_0_, bf16[4096,128]{1,0:T(8,128)(2,1)S(1)} %get-tuple-element.35.refs_1_, bf16[4096,256]{1,0:T(8,128)(2,1)S(1)} %get-tuple-element.36.refs_2_), custom_call_target="tpu_custom_call" | custom-call | tf_op jit(solution)/shard_map/attend/pallas_call | solution.py:167
  88.5 0.0 collective-permute-done.10.refs_5_
  88.5 0.4 merge.1
  88.9 22.9 %all_to_all.11 = bf16[64,32,128]{2,1,0:T(8,128)(2,1)S(1)} all-to-all(bf16[64,32,128]{2,1,0:T(8,128)(2,1)S(1)} %merge.1), channel_id=1, replica_groups=mesh['xl'=2,'c'=2,'yv'=2,'yr'=2,'z'=8,'xh'=2] {'yv','yr','z','xh'}, dimensions={0} | all-to-all | bytes 1048576 | tf_op jit(solution)/shard_map/all_to_all | solution.py:336
  111.8 0.0 collective-permute-done.11.b_ref
  111.8 2.9 %cross.1.c_ref = f32[2,2,16,32,128]{4,3,2,1,0:T(8,128)S(1)} custom-call(bf16[2,2,16,3,32,128]{5,4,3,2,1,0:T(8,128)(2,1)S(1)} %place.1.a_ref, bf16[2,2,16,2,32,128]{5,4,3,2,1,0:T(8,128)(2,1)S(1)} %collective-permute-done.11.b_ref), custom_call_target="tpu_custom_call" | custom-call | tf_op jit(solution)/shard_map/cross/pallas_call | solution.py:242
  114.8 0.0 copy-start
  114.8 0.0 copy-start.1
  114.8 0.1 add_cross.1
  114.9 4.6 %collective-permute-start.12 = (bf16[2,16,32,128]{3,2,1,0:T(8,128)(2,1)S(1)}, bf16[2,16,32,128]{3,2,1,0:T(8,128)(2,1)S(1)}, u32[]{:S(2)}, u32[]{:S(2)}) collective-permute-start(bf16[2,16,32,128]{3,2,1,0:T(8,128)(2,1)S(1)} %get-tuple-element.48), channel_id=1, source_target_pairs={{0,64},{64,0},{1,65},{65,1},{2,66},{66,2},{3,67},{67,3},{4,68},{68... | collective-permute-start | bytes 786440 | tf_op jit(solution)/shard_map/ppermute | solution.py:340
  119.5 1.2 collective-permute-done.12.came_ref
  120.7 0.0 slice-done
  120.7 0.0 slice-done.1
  120.7 0.0 copy-done
  120.7 0.0 copy-done.1
  120.7 2.2 %project.1 = bf16[128,2048]{1,0:T(8,128)(2,1)} custom-call(bf16[2,16,32,128]{3,2,1,0:T(8,128)(2,1)S(1)} %get-tuple-element.47.keep_ref, bf16[2,16,32,128]{3,2,1,0:T(8,128)(2,1)S(1)} %collective-permute-done.12.came_ref, bf16[2048,2048]{1,0:T(8,128)(2,1)S(1)} %bitcast.18, bf16[128,2048]{1,0:T(8,128)(2,1)S(1)} %bitcast.20, bf16[1,2048]{1,0:T(2,128)(2,1)S(1)} %copy-done.1), custom_call_target="tpu_custom_call" | custom-call | tf_op jit(solution)/shard_map/project/pallas_call | solution.py:287
  (2 shorter events, 0.0 us)
Async XLA Ops:
  1.4 4.5 %collective-permute-start = (bf16[2,16,32,128]{3,2,1,0:T(8,128)(2,1)S(1)}, bf16[2,16,32,128]{3,2,1,0:T(8,128)(2,1)S(1)}, u32[]{:S(2)}, u32[]{:S(2)}) collective-permute-start(bf16[2,16,32,128]{3,2,1,0:T(8,128)(2,1)S(1)} %get-tuple-element.28), channel_id=1, source_target_pairs={{0,64},{64,0},{1,65},{65,1},{2,66},{66,2},{3,67},{67,3},{4,68},{68... | collective-permute-start | bytes 786440 | tf_op jit(solution)/shard_map/ppermute | solution.py:303
  4.8 1.5 %collective-permute-start.1 = (bf16[2,16,32,128]{3,2,1,0:T(8,128)(2,1)S(1)}, bf16[2,16,32,128]{3,2,1,0:T(8,128)(2,1)S(1)}, u32[]{:S(2)}, u32[]{:S(2)}) collective-permute-start(bf16[2,16,32,128]{3,2,1,0:T(8,128)(2,1)S(1)} %get-tuple-element.29), channel_id=1, source_target_pairs={{0,64},{64,0},{1,65},{65,1},{2,66},{66,2},{3,67},{67,3},{4,68},{68... | collective-permute-start | bytes 786440 | tf_op jit(solution)/shard_map/ppermute | solution.py:303
  4.9 1.8 %collective-permute-start.2 = (bf16[2,16,32,128]{3,2,1,0:T(8,128)(2,1)S(1)}, bf16[2,16,32,128]{3,2,1,0:T(8,128)(2,1)S(1)}, u32[]{:S(2)}, u32[]{:S(2)}) collective-permute-start(bf16[2,16,32,128]{3,2,1,0:T(8,128)(2,1)S(1)} %get-tuple-element.30), channel_id=1, source_target_pairs={{0,64},{64,0},{1,65},{65,1},{2,66},{66,2},{3,67},{67,3},{4,68},{68... | collective-permute-start | bytes 786440 | tf_op jit(solution)/shard_map/ppermute | solution.py:303
  59.2 4.1 %collective-permute-start.4 = (bf16[16,2,32,128]{3,2,1,0:T(8,128)(2,1)S(1)}, bf16[16,2,32,128]{3,2,1,0:T(8,128)(2,1)S(1)}, u32[]{:S(2)}, u32[]{:S(2)}) collective-permute-start(bf16[16,2,32,128]{3,2,1,0:T(8,128)(2,1)S(1)} %get-tuple-element.54.refs_1_), channel_id=1, source_target_pairs={{0,64},{64,0},{1,65},{65,1},{2,66},{66,2},{3,67},{67,3},{4,68},{68... | collective-permute-start | bytes 786440 | tf_op jit(solution)/shard_map/ppermute | solution.py:303
  62.1 2.2 %collective-permute-start.5 = (bf16[16,2,32,128]{3,2,1,0:T(8,128)(2,1)S(1)}, bf16[16,2,32,128]{3,2,1,0:T(8,128)(2,1)S(1)}, u32[]{:S(2)}, u32[]{:S(2)}) collective-permute-start(bf16[16,2,32,128]{3,2,1,0:T(8,128)(2,1)S(1)} %get-tuple-element.53.refs_2_), channel_id=1, source_target_pairs={{0,64},{64,0},{1,65},{65,1},{2,66},{66,2},{3,67},{67,3},{4,68},{68... | collective-permute-start | bytes 786440 | tf_op jit(solution)/shard_map/ppermute | solution.py:303
  62.2 2.1 %collective-permute-start.6 = (bf16[16,2,32,128]{3,2,1,0:T(8,128)(2,1)S(1)}, bf16[16,2,32,128]{3,2,1,0:T(8,128)(2,1)S(1)}, u32[]{:S(2)}, u32[]{:S(2)}) collective-permute-start(bf16[16,2,32,128]{3,2,1,0:T(8,128)(2,1)S(1)} %get-tuple-element.52.refs_3_), channel_id=1, source_target_pairs={{0,64},{64,0},{1,65},{65,1},{2,66},{66,2},{3,67},{67,3},{4,68},{68... | collective-permute-start | bytes 786440 | tf_op jit(solution)/shard_map/ppermute | solution.py:303
  62.7 1.7 %collective-permute-start.7 = (bf16[16,2,32,128]{3,2,1,0:T(8,128)(2,1)S(1)}, bf16[16,2,32,128]{3,2,1,0:T(8,128)(2,1)S(1)}, u32[]{:S(2)}, u32[]{:S(2)}) collective-permute-start(bf16[16,2,32,128]{3,2,1,0:T(8,128)(2,1)S(1)} %get-tuple-element.51.refs_4_), channel_id=1, source_target_pairs={{0,64},{64,0},{1,65},{65,1},{2,66},{66,2},{3,67},{67,3},{4,68},{68... | collective-permute-start | bytes 786440 | tf_op jit(solution)/shard_map/ppermute | solution.py:303
  62.8 7.5 %collective-permute-start.3 = (bf16[32,32,128]{2,1,0:T(8,128)(2,1)S(1)}, bf16[32,32,128]{2,1,0:T(8,128)(2,1)S(1)}, u32[]{:S(2)}, u32[]{:S(2)}) collective-permute-start(bf16[32,32,128]{2,1,0:T(8,128)(2,1)S(1)} %get-tuple-element.50.refs_0_), channel_id=1, source_target_pairs={{0,16},{16,0},{1,17},{17,1},{2,18},{18,2},{3,19},{19,3},{4,20},{20... | collective-permute-start | bytes 786440 | tf_op jit(solution)/shard_map/ppermute | solution.py:303
  63.3 13.1 %collective-permute-start.9 = (bf16[32,32,128]{2,1,0:T(8,128)(2,1)S(1)}, bf16[32,32,128]{2,1,0:T(8,128)(2,1)S(1)}, u32[]{:S(2)}, u32[]{:S(2)}) collective-permute-start(bf16[32,32,128]{2,1,0:T(8,128)(2,1)S(1)} %get-tuple-element.41.refs_0_), channel_id=1, source_target_pairs={{0,16},{16,0},{1,17},{17,1},{2,18},{18,2},{3,19},{19,3},{4,20},{20... | collective-permute-start | bytes 786440 | tf_op jit(solution)/shard_map/ppermute | solution.py:303
  75.9 7.6 %collective-permute-start.8 = (bf16[33,32,128]{2,1,0:T(8,128)(2,1)S(1)}, bf16[33,32,128]{2,1,0:T(8,128)(2,1)S(1)}, u32[]{:S(2)}, u32[]{:S(2)}) collective-permute-start(bf16[33,32,128]{2,1,0:T(8,128)(2,1)S(1)} %get-tuple-element.37), channel_id=1, source_target_pairs={{0,16},{16,0},{1,17},{17,1},{2,18},{18,2},{3,19},{19,3},{4,20},{20... | collective-permute-start | bytes 811016 | tf_op jit(solution)/shard_map/ppermute | solution.py:329
  76.3 44.4 %slice-start = ((s8[8388608]{0:T(1024)(128)(4,1)}), s8[4194304]{0:T(1024)(128)(4,1)S(1)}, s32[]{:S(2)}) async-start(s8[8388608]{0:T(1024)(128)(4,1)} %bitcast.17), calls=%async_computation.2 | async-start | bytes 8388608
  81.9 6.6 %collective-permute-start.10 = (bf16[33,32,128]{2,1,0:T(8,128)(2,1)S(1)}, bf16[33,32,128]{2,1,0:T(8,128)(2,1)S(1)}, u32[]{:S(2)}, u32[]{:S(2)}) collective-permute-start(bf16[33,32,128]{2,1,0:T(8,128)(2,1)S(1)} %get-tuple-element.39), channel_id=1, source_target_pairs={{0,16},{16,0},{1,17},{17,1},{2,18},{18,2},{3,19},{19,3},{4,20},{20... | collective-permute-start | bytes 811016 | tf_op jit(solution)/shard_map/ppermute | solution.py:332
  83.1 37.6 %slice-start.1 = ((s8[8388608]{0:T(1024)(128)(4,1)}), s8[4194304]{0:T(1024)(128)(4,1)S(1)}, s32[]{:S(2)}) async-start(s8[8388608]{0:T(1024)(128)(4,1)} %bitcast.17), calls=%async_computation.3 | async-start | bytes 8388608
  83.1 28.7 %collective-permute-start.11 = (bf16[2,2,16,2,32,128]{5,4,3,2,1,0:T(8,128)(2,1)S(1)}, bf16[2,2,16,2,32,128]{5,4,3,2,1,0:T(8,128)(2,1)S(1)}, u32[]{:S(2)}, u32[]{:S(2)}) collective-permute-start(bf16[2,2,16,2,32,128]{5,4,3,2,1,0:T(8,128)(2,1)S(1)} %slice.27), channel_id=1, source_target_pairs={{0,128},{128,0},{1,129},{129,1},{2,130},{130,2},{3,131},{131,3},{4... | collective-permute-start | bytes 3145736 | tf_op jit(solution)/shard_map/ppermute | solution.py:327
  114.8 5.9 %copy-start = (bf16[1,128,2048]{2,1,0:T(8,128)(2,1)S(1)}, bf16[1,128,2048]{2,1,0:T(8,128)(2,1)}, u32[]{:S(2)}) copy-start(bf16[1,128,2048]{2,1,0:T(8,128)(2,1)} %param.6) | copy-start | bytes 1572868
  114.8 5.9 %copy-start.1 = (bf16[1,2048]{1,0:T(2,128)(2,1)S(1)}, bf16[1,2048]{1,0:T(2,128)(2,1)}, u32[]{:S(2)}) copy-start(bf16[1,2048]{1,0:T(2,128)(2,1)} %g_ref.1) | copy-start | bytes 12292
  114.9 5.8 %collective-permute-start.12 = (bf16[2,16,32,128]{3,2,1,0:T(8,128)(2,1)S(1)}, bf16[2,16,32,128]{3,2,1,0:T(8,128)(2,1)S(1)}, u32[]{:S(2)}, u32[]{:S(2)}) collective-permute-start(bf16[2,16,32,128]{3,2,1,0:T(8,128)(2,1)S(1)} %get-tuple-element.48), channel_id=1, source_target_pairs={{0,64},{64,0},{1,65},{65,1},{2,66},{66,2},{3,67},{67,3},{4,68},{68... | collective-permute-start | bytes 786440 | tf_op jit(solution)/shard_map/ppermute | solution.py:340

commit v4 on v3

--- a/solution.py
+++ b/solution.py
@@ -27,42 +27,42 @@
     return [pl.BlockSpec(memory_space=pltpu.VMEM)] * n
 
 
-def pack_kernel(q_ref, k_ref, v_ref, o_ref, sq_ref, sk_ref, sv_ref, held, sems):
-    _, parts, heads, _, rows, _ = o_ref.shape
-    half = parts * rows
-    me = lax.axis_index("c")
-    moves = []
-    for to, core in ((0, 1 - me), (1, me)):
-        for j, ref in enumerate((q_ref, k_ref, v_ref)):
-            part = pl.ds(pl.multiple_of(core * half, half), half)
-            moves.append(pltpu.make_async_copy(ref.at[part], held.at[to, j], sems.at[to, j]))
+def fetch_half(core, refs, held, sems):
+    half = held.shape[1]
+    part = pl.ds(pl.multiple_of(core * half, half), half)
+    moves = [
+        pltpu.make_async_copy(ref.at[part], held.at[j], sems.at[j]) for j, ref in enumerate(refs)
+    ]
     for move in moves:
         move.start()
+    return moves
+
+
+def pack_send_kernel(q_ref, k_ref, v_ref, sq_ref, sk_ref, sv_ref, held, sems):
+    moves = fetch_half(1 - lax.axis_index("c"), (q_ref, k_ref, v_ref), held, sems)
     for j, out in enumerate((sq_ref, sk_ref, sv_ref)):
         moves[j].wait()
-        for r in range(parts):
-            for h in range(heads):
-                out[r, h] = held[0, j, r * rows : (r + 1) * rows, h * HD : (h + 1) * HD]
+        for h in range(out.shape[1]):
+            out[0, h] = held[j, :, h * HD : (h + 1) * HD]
+
+
+def pack_keep_kernel(q_ref, k_ref, v_ref, o_ref, held, sems):
+    me = lax.axis_index("c")
+    moves = fetch_half(me, (q_ref, k_ref, v_ref), held, sems)
     for j in range(3):
-        moves[3 + j].wait()
-        for r in range(parts):
-            for h in range(heads):
-                o_ref[me, r, h, j] = held[1, j, r * rows : (r + 1) * rows, h * HD : (h + 1) * HD]
-
-
-def pack(q, k, v):
+        moves[j].wait()
+        for h in range(o_ref.shape[2]):
+            o_ref[me, 0, h, j] = held[j, :, h * HD : (h + 1) * HD]
+
+
+def pack(kernel, out_shape, q, k, v):
     tok, width = q.shape
-    rows = tok // 4
-    away = jax.ShapeDtypeStruct((2, HEADS, rows, HD), BF)
-    return pl.pallas_call(
-        pack_kernel,
+    return pl.pallas_call(
+        kernel,
         in_specs=[pl.BlockSpec(memory_space=pltpu.HBM)] * 3,
-        out_specs=whole(4),
-        out_shape=[jax.ShapeDtypeStruct((2, 2, HEADS, 3, rows, HD), BF)] + [away] * 3,
-        scratch_shapes=[
-            pltpu.VMEM((2, 3, tok // 2, width), BF),
-            pltpu.SemaphoreType.DMA((2, 3)),
-        ],
+        out_specs=whole(len(out_shape)),
+        out_shape=[jax.ShapeDtypeStruct(x, BF) for x in out_shape],
+        scratch_shapes=[pltpu.VMEM((3, tok // 2, width), BF), pltpu.SemaphoreType.DMA((3,))],
         compiler_params=params(),
         name="pack",
     )(*(pltpu.with_memory_space_constraint(x, pltpu.HBM) for x in (q, k, v)))
@@ -215,8 +215,11 @@
     )(*flat)
 
 
-def cross_kernel(a_ref, b_ref, o_ref):
+def cross_kernel(a_ref, b_ref, s_ref, o_ref, *, flip):
     views, parts, heads = a_ref.shape[:3]
+    view = lax.axis_index("c")
+    if flip:
+        view = 1 - view
 
     def one_head(h, carry):
         for r in range(parts):
@@ -224,47 +227,28 @@
             ks += [b_ref[b, r, h, 0].astype(F32) for b in range(views)]
             vs = [a_ref[b, r, h, 2].astype(F32) for b in range(views)]
             vs += [b_ref[b, r, h, 1].astype(F32) for b in range(views)]
-            for a in range(views):
-                q = a_ref[a, r, h, 0].astype(F32)
-                s = [jnp.sum(q * k, axis=1, keepdims=True) * SCALE for k in ks]
-                peak = functools.reduce(jnp.maximum, s)
-                e = [jnp.exp(x - peak) for x in s]
-                inv = 1.0 / functools.reduce(jnp.add, e)
-                terms = [(x * inv).astype(BF).astype(F32) * v for x, v in zip(e, vs)]
-                o_ref[a, r, h] = functools.reduce(jnp.add, terms)
+            q = a_ref[view, r, h, 0].astype(F32)
+            s = [jnp.sum(q * k, axis=1, keepdims=True) * SCALE for k in ks]
+            peak = functools.reduce(jnp.maximum, s)
+            e = [jnp.exp(x - peak) for x in s]
+            inv = 1.0 / functools.reduce(jnp.add, e)
+            terms = [(x * inv).astype(BF).astype(F32) * v for x, v in zip(e, vs)]
+            cross_out = functools.reduce(jnp.add, terms)
+            o_ref[r, h] = (s_ref[view, r, h].astype(F32) + cross_out).astype(BF)
         return carry
 
-    lax.fori_loop(0, heads, one_head, 0)
-
-
-def cross(mine, other):
-    views, parts, heads, _, rows, _ = mine.shape
-    return pl.pallas_call(
-        cross_kernel,
-        in_specs=whole(2),
+    lax.fori_loop(0, heads, one_head, 0, unroll=2)
+
+
+def attended(mine, other, back, flip):
+    return pl.pallas_call(
+        functools.partial(cross_kernel, flip=flip),
+        in_specs=whole(3),
         out_specs=pl.BlockSpec(memory_space=pltpu.VMEM),
-        out_shape=jax.ShapeDtypeStruct((views, parts, heads, rows, HD), F32),
+        out_shape=jax.ShapeDtypeStruct(back.shape[1:], BF),
         compiler_params=params(),
         name="cross",
-    )(mine, other)
-
-
-def add_kernel(s_ref, c_ref, keep_ref, send_ref):
-    me = lax.axis_index("c")
-    for view, out in ((1 - me, send_ref), (me, keep_ref)):
-        out[...] = (s_ref[view].astype(F32) + c_ref[view]).astype(BF)
-
-
-def add_cross(self_out, cross_out):
-    out = jax.ShapeDtypeStruct(self_out.shape[1:], BF)
-    return pl.pallas_call(
-        add_kernel,
-        in_specs=whole(2),
-        out_specs=whole(2),
-        out_shape=[out, out],
-        compiler_params=params(),
-        name="add_cross",
-    )(self_out, cross_out)
+    )(mine, other, back)
 
 
 def project_kernel(keep_ref, came_ref, w_ref, h_ref, g_ref, o_ref, att):
@@ -306,12 +290,14 @@
 def local(hidden_in, queries, keys, values, out_weight, gate):
     hidden, q, k, v = hidden_in[0], queries[0], keys[0], values[0]
     tok, _ = q.shape
-    seq = ("yv", "yr", "z", "xh")
-    rows = tok // 4
-    n = 4 * HEADS
-
-    mine, *away = pack(q, k, v)
-    mine = place(mine, swap(away, "c"))
+    seq = ("yv", "z", "xh")
+    rows = tok // 2
+    n = 2 * HEADS
+
+    away = pack(pack_send_kernel, [(1, HEADS, rows, HD)] * 3, q, k, v)
+    came = swap(away, "c")
+    (mine,) = pack(pack_keep_kernel, [(2, 1, HEADS, 3, rows, HD)], q, k, v)
+    mine = place(mine, came)
     got = lax.all_to_all(mine.reshape(n, 3 * rows, HD), seq, split_axis=0, concat_axis=0, tiled=True)
     got = got.reshape(n, 3, rows, HD)
 
@@ -335,9 +321,10 @@
     o = merge([(o1, l1, back1), (o2, l2, back2)])
     back = lax.all_to_all(o, seq, split_axis=0, concat_axis=0, tiled=True)
     here, back = lax.optimization_barrier((mine, back))
-    cross_out = cross(here, other)
-    keep, send = add_cross(back.reshape(cross_out.shape), cross_out)
+    back = back.reshape(mine.shape[:3] + (rows, HD))
+    send = attended(here, other, back, True)
     came = lax.ppermute(send, "c", SWAP)
+    keep = attended(here, other, back, False)
     return project(keep, came, out_weight, hidden, gate)[None]
 
 

time: 123 us -> 121 us (0.984)
  waiting for transfers between devices: 3.23 us -> 0.87 us
    pallas_call x3 -> x4, Pallas kernels: 4.49 us -> 5.42 us  [the longest x2 3.07 us: attended(): pl.pallas_call(functools.partial(cross_kernel, flip=flip), in_specs=whole...]
  transfers between devices with their start and end apart: 13 -> 13, of which waited for: 6 -> 3; matrix products, arithmetic and copies ran while one was open for 0% -> 0% of each run, Pallas kernels for 18% -> 20%
where the time goes in v4:
time: 121 us; the launch traced here: 120 us
  blocking collectives  74.9 us (62%)
  Pallas kernels  29.7 us (25%)
  starting transfers between devices  14.6 us (12%)
    all_to_all x1, blocking collectives, local(): lax.all_to_all(mine.reshape(n, 3 * rows, HD), seq, split_axis=0, concat_a...  52 us
    all_to_all x1, blocking collectives, local(): back = lax.all_to_all(o, seq, split_axis=0, concat_axis=0, tiled=True)  22.8 us
    pallas_call x4, Pallas kernels, attend(): pl.pallas_call(functools.partial(attend_kernel, first=first, travels=trav...  21.6 us
    ppermute x9, starting transfers between devices, swap(): return [lax.ppermute(x, axis, SWAP) for x in chunks]  9.11 us
    ppermute x1, starting transfers between devices, local(): came = lax.ppermute(send, 'c', SWAP)  3.66 us
    pallas_call x2, Pallas kernels, attended(): pl.pallas_call(functools.partial(cross_kernel, flip=flip), in_specs=whole...  3.07 us
  transfers between devices with their start and end apart: 13, of which 3 were waited for; matrix products, arithmetic and copies ran while one was open for 0% of the time, Pallas kernels for 20%

profile of v4, /device:TPU:1, one launch (start us, length us, event | category | flops | bytes accessed | tf_op | source)
XLA Modules:
  0.0 120.4 jit_solution(8570281033944379429)
XLA Ops:
  0.0 1.2 pack.3
  1.2 3.3 %collective-permute-start = (bf16[1,16,64,128]{3,2,1,0:T(8,128)(2,1)S(1)}, bf16[1,16,64,128]{3,2,1,0:T(8,128)(2,1)S(1)}, u32[]{:S(2)}, u32[]{:S(2)}) collective-permute-start(bf16[1,16,64,128]{3,2,1,0:T(8,128)(2,1)S(1)} %get-tuple-element.24), channel_id=1, source_target_pairs={{0,64},{64,0},{1,65},{65,1},{2,66},{66,2},{3,67},{67,3},{4,68},{68... | collective-permute-start | bytes 786440 | tf_op jit(solution)/shard_map/ppermute | solution.py:287
  4.5 0.1 collective-permute-start.1
  4.6 0.4 collective-permute-start.2
  5.0 1.2 pack.2.a_ref
  6.2 0.0 collective-permute-done.q_ref
  6.2 0.0 collective-permute-done.1.k_ref
  6.2 0.2 collective-permute-done.2.v_ref
  6.4 0.1 place.1.a_ref
  6.5 52.0 %all_to_all.10 = bf16[32,192,128]{2,1,0:T(8,128)(2,1)S(1)} all-to-all(bf16[32,192,128]{2,1,0:T(8,128)(2,1)S(1)} %bitcast.16), channel_id=1, replica_groups=mesh['xl'=2,'c'=2,'yv'=2,'yr'=2,'z'=8,'xh'=2] {'yv','z','xh'}, dimensions={0} | all-to-all | bytes 3145728 | tf_op jit(solution)/shard_map/all_to_all | solution.py:301
  58.5 0.1 fusion
  58.6 3.1 %collective-permute-start.4 = (bf16[8,2,64,128]{3,2,1,0:T(8,128)(2,1)S(1)}, bf16[8,2,64,128]{3,2,1,0:T(8,128)(2,1)S(1)}, u32[]{:S(2)}, u32[]{:S(2)}) collective-permute-start(bf16[8,2,64,128]{3,2,1,0:T(8,128)(2,1)S(1)} %get-tuple-element.48.refs_1_), channel_id=1, source_target_pairs={{0,64},{64,0},{1,65},{65,1},{2,66},{66,2},{3,67},{67,3},{4,68},{68... | collective-permute-start | bytes 786440 | tf_op jit(solution)/shard_map/ppermute | solution.py:287
  61.7 0.1 collective-permute-start.5
  61.9 0.5 collective-permute-start.6
  62.4 0.1 collective-permute-start.7
  62.5 0.4 collective-permute-start.3
  62.9 0.0 collective-permute-done.4.refs_5_
  62.9 1.0 collective-permute-start.9
  64.0 0.0 collective-permute-done.5.refs_6_
  64.0 0.0 collective-permute-done.6.refs_7_
  64.0 0.1 collective-permute-done.7.refs_8_
  64.0 5.4 %attend.4 = (f32[16,64,128]{2,1,0:T(8,128)S(1)}, f32[8,128]{1,0:T(8,128)S(1)}, bf16[4096,128]{1,0:T(8,128)(2,1)S(1)}, bf16[4096,256]{1,0:T(8,128)(2,1)S(1)}) custom-call(bf16[16,64,128]{2,1,0:T(8,128)(2,1)S(1)} %get-tuple-element.44.refs_0_, bf16[8,2,64,128]{3,2,1,0:T(8,128)(2,1)S(1)} %get-tuple-element.48.refs_1_, ...), custom_call_target="tpu_custom_call" | custom-call | tf_op jit(solution)/shard_map/attend/pallas_call | solution.py:167
  69.4 0.5 collective-permute-done.3.refs_0_
  70.0 5.6 %attend.5 = (bf16[17,64,128]{2,1,0:T(8,128)(2,1)S(1)}, f32[8,128]{1,0:T(8,128)}) custom-call(bf16[16,64,128]{2,1,0:T(8,128)(2,1)S(1)} %collective-permute-done.3.refs_0_, bf16[4096,128]{1,0:T(8,128)(2,1)S(1)} %get-tuple-element.31.refs_1_, bf16[4096,256]{1,0:T(8,128)(2,1)S(1)} %get-tuple-element.32.refs_2_), custom_call_target="tpu_custom_call" | custom-call | tf_op jit(solution)/shard_map/attend/pallas_call | solution.py:167
  75.6 0.4 collective-permute-start.8
  76.0 0.0 collective-permute-done.9.refs_0_
  76.0 5.6 %attend.6 = (bf16[17,64,128]{2,1,0:T(8,128)(2,1)S(1)}, f32[8,128]{1,0:T(8,128)}) custom-call(bf16[16,64,128]{2,1,0:T(8,128)(2,1)S(1)} %collective-permute-done.9.refs_0_, bf16[4096,128]{1,0:T(8,128)(2,1)S(1)} %get-tuple-element.31.refs_1_, bf16[4096,256]{1,0:T(8,128)(2,1)S(1)} %get-tuple-element.32.refs_2_), custom_call_target="tpu_custom_call" | custom-call | tf_op jit(solution)/shard_map/attend/pallas_call | solution.py:167
  81.6 1.1 collective-permute-start.10
  82.6 0.1 slice.27
  82.7 0.4 collective-permute-start.11
  83.1 0.0 collective-permute-done.8.refs_2_
  83.1 5.0 %attend.7 = (f32[16,64,128]{2,1,0:T(8,128)S(1)}, f32[8,128]{1,0:T(8,128)S(1)}) custom-call(bf16[16,64,128]{2,1,0:T(8,128)(2,1)S(1)} %get-tuple-element.37.refs_0_, bf16[4096,128]{1,0:T(8,128)(2,1)S(1)} %get-tuple-element.31.refs_1_, bf16[4096,256]{1,0:T(8,128)(2,1)S(1)} %get-tuple-element.32.refs_2_), custom_call_target="tpu_custom_call" | custom-call | tf_op jit(solution)/shard_map/attend/pallas_call | solution.py:167
  88.1 0.0 collective-permute-done.10.refs_5_
  88.2 0.4 merge.1
  88.5 0.0 slice-start.1
  88.6 22.8 %all_to_all.11 = bf16[32,64,128]{2,1,0:T(8,128)(2,1)S(1)} all-to-all(bf16[32,64,128]{2,1,0:T(8,128)(2,1)S(1)} %merge.1), channel_id=1, replica_groups=mesh['xl'=2,'c'=2,'yv'=2,'yr'=2,'z'=8,'xh'=2] {'yv','z','xh'}, dimensions={0} | all-to-all | bytes 1048576 | tf_op jit(solution)/shard_map/all_to_all | solution.py:322
  111.4 0.0 collective-permute-done.11.b_ref
  111.4 1.5 %cross.3 = bf16[1,16,64,128]{3,2,1,0:T(8,128)(2,1)S(1)} custom-call(bf16[2,1,16,3,64,128]{5,4,3,2,1,0:T(8,128)(2,1)S(1)} %place.1.a_ref, bf16[2,1,16,2,64,128]{5,4,3,2,1,0:T(8,128)(2,1)S(1)} %collective-permute-done.11.b_ref, bf16[2,1,16,64,128]{4,3,2,1,0:T(8,128)(2,1)S(1)} %bitcast.19), custom_call_target="tpu_custom_call" | custom-call | tf_op jit(solution)/shard_map/cross/pallas_call | solution.py:244
  112.9 0.0 copy-start
  112.9 0.0 copy-start.1
  113.0 3.7 %collective-permute-start.12 = (bf16[1,16,64,128]{3,2,1,0:T(8,128)(2,1)S(1)}, bf16[1,16,64,128]{3,2,1,0:T(8,128)(2,1)S(1)}, u32[]{:S(2)}, u32[]{:S(2)}) collective-permute-start(bf16[1,16,64,128]{3,2,1,0:T(8,128)(2,1)S(1)} %cross.3), channel_id=1, source_target_pairs={{0,64},{64,0},{1,65},{65,1},{2,66},{66,2},{3,67},{67,3},{4,68},{68... | collective-permute-start | bytes 786440 | tf_op jit(solution)/shard_map/ppermute | solution.py:326
  116.6 1.5 %cross.2.keep_ref = bf16[1,16,64,128]{3,2,1,0:T(8,128)(2,1)S(1)} custom-call(bf16[2,1,16,3,64,128]{5,4,3,2,1,0:T(8,128)(2,1)S(1)} %place.1.a_ref, bf16[2,1,16,2,64,128]{5,4,3,2,1,0:T(8,128)(2,1)S(1)} %collective-permute-done.11.b_ref, bf16[2,1,16,64,128]{4,3,2,1,0:T(8,128)(2,1)S(1)} %bitcast.20), custom_call_target="tpu_custom_call" | custom-call | tf_op jit(solution)/shard_map/cross/pallas_call | solution.py:244
  118.2 0.0 collective-permute-done.12.came_ref
  118.2 0.0 slice-done
  118.2 0.0 slice-done.1
  118.2 0.0 copy-done
  118.2 0.0 copy-done.1
  118.2 2.2 %project.1 = bf16[128,2048]{1,0:T(8,128)(2,1)} custom-call(bf16[1,16,64,128]{3,2,1,0:T(8,128)(2,1)S(1)} %cross.2.keep_ref, bf16[1,16,64,128]{3,2,1,0:T(8,128)(2,1)S(1)} %collective-permute-done.12.came_ref, bf16[2048,2048]{1,0:T(8,128)(2,1)S(1)} %bitcast.18, bf16[128,2048]{1,0:T(8,128)(2,1)S(1)} %bitcast.21, bf16[1,2048]{1,0:T(2,128)(2,1)S(1)} %copy-done.1), custom_call_target="tpu_custom_call" | custom-call | tf_op jit(solution)/shard_map/project/pallas_call | solution.py:271
  (3 shorter events, 0.0 us)
Async XLA Ops:
  1.2 5.0 %collective-permute-start = (bf16[1,16,64,128]{3,2,1,0:T(8,128)(2,1)S(1)}, bf16[1,16,64,128]{3,2,1,0:T(8,128)(2,1)S(1)}, u32[]{:S(2)}, u32[]{:S(2)}) collective-permute-start(bf16[1,16,64,128]{3,2,1,0:T(8,128)(2,1)S(1)} %get-tuple-element.24), channel_id=1, source_target_pairs={{0,64},{64,0},{1,65},{65,1},{2,66},{66,2},{3,67},{67,3},{4,68},{68... | collective-permute-start | bytes 786440 | tf_op jit(solution)/shard_map/ppermute | solution.py:287
  4.5 1.7 %collective-permute-start.1 = (bf16[1,16,64,128]{3,2,1,0:T(8,128)(2,1)S(1)}, bf16[1,16,64,128]{3,2,1,0:T(8,128)(2,1)S(1)}, u32[]{:S(2)}, u32[]{:S(2)}) collective-permute-start(bf16[1,16,64,128]{3,2,1,0:T(8,128)(2,1)S(1)} %get-tuple-element.25), channel_id=1, source_target_pairs={{0,64},{64,0},{1,65},{65,1},{2,66},{66,2},{3,67},{67,3},{4,68},{68... | collective-permute-start | bytes 786440 | tf_op jit(solution)/shard_map/ppermute | solution.py:287
  4.6 1.8 %collective-permute-start.2 = (bf16[1,16,64,128]{3,2,1,0:T(8,128)(2,1)S(1)}, bf16[1,16,64,128]{3,2,1,0:T(8,128)(2,1)S(1)}, u32[]{:S(2)}, u32[]{:S(2)}) collective-permute-start(bf16[1,16,64,128]{3,2,1,0:T(8,128)(2,1)S(1)} %get-tuple-element.26), channel_id=1, source_target_pairs={{0,64},{64,0},{1,65},{65,1},{2,66},{66,2},{3,67},{67,3},{4,68},{68... | collective-permute-start | bytes 786440 | tf_op jit(solution)/shard_map/ppermute | solution.py:287
  58.6 4.3 %collective-permute-start.4 = (bf16[8,2,64,128]{3,2,1,0:T(8,128)(2,1)S(1)}, bf16[8,2,64,128]{3,2,1,0:T(8,128)(2,1)S(1)}, u32[]{:S(2)}, u32[]{:S(2)}) collective-permute-start(bf16[8,2,64,128]{3,2,1,0:T(8,128)(2,1)S(1)} %get-tuple-element.48.refs_1_), channel_id=1, source_target_pairs={{0,64},{64,0},{1,65},{65,1},{2,66},{66,2},{3,67},{67,3},{4,68},{68... | collective-permute-start | bytes 786440 | tf_op jit(solution)/shard_map/ppermute | solution.py:287
  61.7 2.2 %collective-permute-start.5 = (bf16[8,2,64,128]{3,2,1,0:T(8,128)(2,1)S(1)}, bf16[8,2,64,128]{3,2,1,0:T(8,128)(2,1)S(1)}, u32[]{:S(2)}, u32[]{:S(2)}) collective-permute-start(bf16[8,2,64,128]{3,2,1,0:T(8,128)(2,1)S(1)} %get-tuple-element.47.refs_2_), channel_id=1, source_target_pairs={{0,64},{64,0},{1,65},{65,1},{2,66},{66,2},{3,67},{67,3},{4,68},{68... | collective-permute-start | bytes 786440 | tf_op jit(solution)/shard_map/ppermute | solution.py:287
  61.9 2.1 %collective-permute-start.6 = (bf16[8,2,64,128]{3,2,1,0:T(8,128)(2,1)S(1)}, bf16[8,2,64,128]{3,2,1,0:T(8,128)(2,1)S(1)}, u32[]{:S(2)}, u32[]{:S(2)}) collective-permute-start(bf16[8,2,64,128]{3,2,1,0:T(8,128)(2,1)S(1)} %get-tuple-element.46.refs_3_), channel_id=1, source_target_pairs={{0,64},{64,0},{1,65},{65,1},{2,66},{66,2},{3,67},{67,3},{4,68},{68... | collective-permute-start | bytes 786440 | tf_op jit(solution)/shard_map/ppermute | solution.py:287
  62.4 1.7 %collective-permute-start.7 = (bf16[8,2,64,128]{3,2,1,0:T(8,128)(2,1)S(1)}, bf16[8,2,64,128]{3,2,1,0:T(8,128)(2,1)S(1)}, u32[]{:S(2)}, u32[]{:S(2)}) collective-permute-start(bf16[8,2,64,128]{3,2,1,0:T(8,128)(2,1)S(1)} %get-tuple-element.45.refs_4_), channel_id=1, source_target_pairs={{0,64},{64,0},{1,65},{65,1},{2,66},{66,2},{3,67},{67,3},{4,68},{68... | collective-permute-start | bytes 786440 | tf_op jit(solution)/shard_map/ppermute | solution.py:287
  62.5 7.5 %collective-permute-start.3 = (bf16[16,64,128]{2,1,0:T(8,128)(2,1)S(1)}, bf16[16,64,128]{2,1,0:T(8,128)(2,1)S(1)}, u32[]{:S(2)}, u32[]{:S(2)}) collective-permute-start(bf16[16,64,128]{2,1,0:T(8,128)(2,1)S(1)} %get-tuple-element.44.refs_0_), channel_id=1, source_target_pairs={{0,16},{16,0},{1,17},{17,1},{2,18},{18,2},{3,19},{19,3},{4,20},{20... | collective-permute-start | bytes 786440 | tf_op jit(solution)/shard_map/ppermute | solution.py:287
  62.9 13.1 %collective-permute-start.9 = (bf16[16,64,128]{2,1,0:T(8,128)(2,1)S(1)}, bf16[16,64,128]{2,1,0:T(8,128)(2,1)S(1)}, u32[]{:S(2)}, u32[]{:S(2)}) collective-permute-start(bf16[16,64,128]{2,1,0:T(8,128)(2,1)S(1)} %get-tuple-element.37.refs_0_), channel_id=1, source_target_pairs={{0,16},{16,0},{1,17},{17,1},{2,18},{18,2},{3,19},{19,3},{4,20},{20... | collective-permute-start | bytes 786440 | tf_op jit(solution)/shard_map/ppermute | solution.py:287
  75.6 7.6 %collective-permute-start.8 = (bf16[17,64,128]{2,1,0:T(8,128)(2,1)S(1)}, bf16[17,64,128]{2,1,0:T(8,128)(2,1)S(1)}, u32[]{:S(2)}, u32[]{:S(2)}) collective-permute-start(bf16[17,64,128]{2,1,0:T(8,128)(2,1)S(1)} %get-tuple-element.33), channel_id=1, source_target_pairs={{0,16},{16,0},{1,17},{17,1},{2,18},{18,2},{3,19},{19,3},{4,20},{20... | collective-permute-start | bytes 835592 | tf_op jit(solution)/shard_map/ppermute | solution.py:315
  81.6 6.6 %collective-permute-start.10 = (bf16[17,64,128]{2,1,0:T(8,128)(2,1)S(1)}, bf16[17,64,128]{2,1,0:T(8,128)(2,1)S(1)}, u32[]{:S(2)}, u32[]{:S(2)}) collective-permute-start(bf16[17,64,128]{2,1,0:T(8,128)(2,1)S(1)} %get-tuple-element.35), channel_id=1, source_target_pairs={{0,16},{16,0},{1,17},{17,1},{2,18},{18,2},{3,19},{19,3},{4,20},{20... | collective-permute-start | bytes 835592 | tf_op jit(solution)/shard_map/ppermute | solution.py:318
  82.6 35.5 %slice-start = ((s8[8388608]{0:T(1024)(128)(4,1)}), s8[4194304]{0:T(1024)(128)(4,1)S(1)}, s32[]{:S(2)}) async-start(s8[8388608]{0:T(1024)(128)(4,1)} %bitcast.17), calls=%async_computation.2 | async-start | bytes 8388608
  82.7 28.7 %collective-permute-start.11 = (bf16[2,1,16,2,64,128]{5,4,3,2,1,0:T(8,128)(2,1)S(1)}, bf16[2,1,16,2,64,128]{5,4,3,2,1,0:T(8,128)(2,1)S(1)}, u32[]{:S(2)}, u32[]{:S(2)}) collective-permute-start(bf16[2,1,16,2,64,128]{5,4,3,2,1,0:T(8,128)(2,1)S(1)} %slice.27), channel_id=1, source_target_pairs={{0,128},{128,0},{1,129},{129,1},{2,130},{130,2},{3,131},{131,3},{4... | collective-permute-start | bytes 3145736 | tf_op jit(solution)/shard_map/ppermute | solution.py:313
  88.5 29.6 %slice-start.1 = ((s8[8388608]{0:T(1024)(128)(4,1)}), s8[4194304]{0:T(1024)(128)(4,1)S(1)}, s32[]{:S(2)}) async-start(s8[8388608]{0:T(1024)(128)(4,1)} %bitcast.17), calls=%async_computation.3 | async-start | bytes 8388608
  112.9 5.3 %copy-start = (bf16[1,128,2048]{2,1,0:T(8,128)(2,1)S(1)}, bf16[1,128,2048]{2,1,0:T(8,128)(2,1)}, u32[]{:S(2)}) copy-start(bf16[1,128,2048]{2,1,0:T(8,128)(2,1)} %param.6) | copy-start | bytes 1572868
  112.9 5.3 %copy-start.1 = (bf16[1,2048]{1,0:T(2,128)(2,1)S(1)}, bf16[1,2048]{1,0:T(2,128)(2,1)}, u32[]{:S(2)}) copy-start(bf16[1,2048]{1,0:T(2,128)(2,1)} %g_ref.1) | copy-start | bytes 12292
  113.0 5.2 %collective-permute-start.12 = (bf16[1,16,64,128]{3,2,1,0:T(8,128)(2,1)S(1)}, bf16[1,16,64,128]{3,2,1,0:T(8,128)(2,1)S(1)}, u32[]{:S(2)}, u32[]{:S(2)}) collective-permute-start(bf16[1,16,64,128]{3,2,1,0:T(8,128)(2,1)S(1)} %cross.3), channel_id=1, source_target_pairs={{0,64},{64,0},{1,65},{65,1},{2,66},{66,2},{3,67},{67,3},{4,68},{68... | collective-permute-start | bytes 786440 | tf_op jit(solution)/shard_map/ppermute | solution.py:326

commit v5 on v4

--- a/solution.py
+++ b/solution.py
@@ -151,14 +151,14 @@
         o_ref[src] = jnp.concatenate(terms, axis=0)
 
 
-def attend(q, kv, first, travels, qb=512, kb=2048):
+def attend(q, kv, first, travels, kb=2048):
     src, rows, _ = q.shape
     nq = src * rows
+    qb = nq // 2
     total = sum(a.shape[0] * a.shape[2] for a in kv) if first else kv[0].shape[0]
-    out_shape = [
-        jax.ShapeDtypeStruct((src + travels, rows, HD), BF if travels else F32),
-        jax.ShapeDtypeStruct((nq // HD, HD), F32),
-    ]
+    out_shape = [jax.ShapeDtypeStruct((src + travels, rows, HD), BF if travels else F32)]
+    if not travels:
+        out_shape.append(jax.ShapeDtypeStruct((nq // HD, HD), F32))
     if first:
         out_shape += [
             jax.ShapeDtypeStruct((total, HD), BF),
@@ -169,6 +169,7 @@
         in_specs=whole(1 + len(kv)),
         out_specs=whole(len(out_shape)),
         out_shape=out_shape,
+        scratch_shapes=[pltpu.VMEM((nq // HD, HD), F32)] if travels else [],
         compiler_params=params(),
         cost_estimate=pl.CostEstimate(
             flops=0,
@@ -179,43 +180,46 @@
     )(q, *kv)
 
 
-def merge_kernel(*refs):
-    *parts, out_ref = refs
+def merge_kernel(*refs, own_parts):
+    *refs, out_ref = refs
     diag = eye()
-    at = 0
-    while parts:
-        oa, la, ob = parts[:3]
-        parts = parts[3:]
-        src, rows, _ = oa.shape
-        lines, per = la.shape[0], HD // rows
-        terms = ob[src].astype(F32)
-        lb = terms[:lines] + terms[lines : 2 * lines] + terms[2 * lines : 3 * lines]
-        peak = jnp.maximum(la[...], lb)
-        ea, eb = jnp.exp2(la[...] - peak), jnp.exp2(lb - peak)
-        wa = ea / (ea + eb)
+    rows = out_ref.shape[1]
+    per = HD // rows
+    here, there = [], []
+    for o_ref, l_ref in zip(refs[: 2 * own_parts : 2], refs[1 : 2 * own_parts : 2]):
+        for g in range(l_ref.shape[0]):
+            here.append((o_ref, g, l_ref[g : g + 1, :]))
+    for o_ref in refs[2 * own_parts :]:
+        src = o_ref.shape[0] - 1
+        lines = src // per
+        terms = o_ref[src].astype(F32)
+        lse = terms[:lines] + terms[lines : 2 * lines] + terms[2 * lines : 3 * lines]
         for g in range(lines):
-            w = jnp.sum(jnp.where(diag, wa[g : g + 1, :], 0.0), axis=1, keepdims=True)
-            a = oa[g * per : (g + 1) * per].reshape(HD, HD)
-            b = ob[g * per : (g + 1) * per].reshape(HD, HD).astype(F32)
-            out = (b + w * (a - b)).astype(BF)
-            out_ref[at + g * per : at + (g + 1) * per] = out.reshape(per, rows, HD)
-        at += src
-
-
-def merge(parts):
-    src = sum(p[0].shape[0] for p in parts)
-    flat = [x for p in parts for x in p]
-    return pl.pallas_call(
-        merge_kernel,
+            there.append((o_ref, g, lse[g : g + 1, :]))
+    for i, ((oa, ga, la), (ob, gb, lb)) in enumerate(zip(here, there)):
+        peak = jnp.maximum(la, lb)
+        ea, eb = jnp.exp2(la - peak), jnp.exp2(lb - peak)
+        w = jnp.sum(jnp.where(diag, ea / (ea + eb), 0.0), axis=1, keepdims=True)
+        a = oa[ga * per : (ga + 1) * per].reshape(HD, HD)
+        b = ob[gb * per : (gb + 1) * per].reshape(HD, HD).astype(F32)
+        out_ref[i * per : (i + 1) * per] = (b + w * (a - b)).astype(BF).reshape(per, rows, HD)
+
+
+def merge(own, travelled):
+    src = sum(o.shape[0] for o, _ in own)
+    flat = [x for p in own for x in p] + travelled
+    return pl.pallas_call(
+        functools.partial(merge_kernel, own_parts=len(own)),
         in_specs=whole(len(flat)),
         out_specs=pl.BlockSpec(memory_space=pltpu.VMEM),
-        out_shape=jax.ShapeDtypeStruct((src,) + parts[0][0].shape[1:], BF),
+        out_shape=jax.ShapeDtypeStruct((src,) + own[0][0].shape[1:], BF),
         compiler_params=params(),
         name="merge",
     )(*flat)
 
 
-def cross_kernel(a_ref, b_ref, s_ref, o_ref, *, flip):
+def cross_kernel(a_ref, b_ref, *refs, flip):
+    *s_ref, o_ref = refs
     views, parts, heads = a_ref.shape[:3]
     view = lax.axis_index("c")
     if flip:
@@ -233,22 +237,41 @@
             e = [jnp.exp(x - peak) for x in s]
             inv = 1.0 / functools.reduce(jnp.add, e)
             terms = [(x * inv).astype(BF).astype(F32) * v for x, v in zip(e, vs)]
-            cross_out = functools.reduce(jnp.add, terms)
-            o_ref[r, h] = (s_ref[view, r, h].astype(F32) + cross_out).astype(BF)
+            out = functools.reduce(jnp.add, terms)
+            if s_ref:
+                out = s_ref[0][view, r, h].astype(F32) + out
+            o_ref[r, h] = out.astype(o_ref.dtype)
         return carry
 
-    lax.fori_loop(0, heads, one_head, 0, unroll=2)
-
-
-def attended(mine, other, back, flip):
+    lax.fori_loop(0, heads, one_head, 0, unroll=8)
+
+
+def cross(mine, other, back, flip):
+    args = (mine, other) if back is None else (mine, other, back)
+    out = jax.ShapeDtypeStruct(mine.shape[1:3] + mine.shape[4:], F32 if back is None else BF)
     return pl.pallas_call(
         functools.partial(cross_kernel, flip=flip),
-        in_specs=whole(3),
-        out_specs=pl.BlockSpec(memory_space=pltpu.VMEM),
-        out_shape=jax.ShapeDtypeStruct(back.shape[1:], BF),
+        in_specs=whole(len(args)),
+        out_specs=pl.BlockSpec(memory_space=pltpu.VMEM),
+        out_shape=out,
         compiler_params=params(),
         name="cross",
-    )(mine, other, back)
+    )(*args)
+
+
+def add_kernel(s_ref, c_ref, o_ref):
+    o_ref[...] = (s_ref[1 - lax.axis_index("c")].astype(F32) + c_ref[...]).astype(BF)
+
+
+def add_send(back, cross_out):
+    return pl.pallas_call(
+        add_kernel,
+        in_specs=whole(2),
+        out_specs=pl.BlockSpec(memory_space=pltpu.VMEM),
+        out_shape=jax.ShapeDtypeStruct(cross_out.shape, BF),
+        compiler_params=params(),
+        name="add_send",
+    )(back, cross_out)
 
 
 def project_kernel(keep_ref, came_ref, w_ref, h_ref, g_ref, o_ref, att):
@@ -280,7 +303,7 @@
 
 
 SWAP = [(0, 1), (1, 0)]
-CHUNKS = 4
+CHUNKS = 2
 
 
 def swap(chunks, axis):
@@ -301,30 +324,34 @@
     got = lax.all_to_all(mine.reshape(n, 3 * rows, HD), seq, split_axis=0, concat_axis=0, tiled=True)
     got = got.reshape(n, 3, rows, HD)
 
-    step, half = n // CHUNKS, n // 2
+    step, half, lead = n // CHUNKS, n // 2, n * 5 // 8
     own = [got[i * step : (i + 1) * step, 1:] for i in range(CHUNKS)]
     own_pair = swap(own, "c")
-    qs = [got[:half, 0], got[half:, 0]]
-    mate_q = swap(qs, "yr")
-
-    o1, l1, keys_all, values_all = attend(qs[0], own + own_pair, True, False)
+    q_first, q_last = got[:lead, 0], got[lead:, 0]
+    here, got = lax.optimization_barrier((mine, got))
+    other = lax.ppermute(here[:, :, :, 1:], "xl", SWAP)
+    mate_q = swap([got[:half, 0], got[half:, 0]], "yr")
+
+    o1, l1, keys_all, values_all = attend(q_first, own + own_pair, True, False)
     kv = keys_all, values_all
-    q_in, away, o1 = lax.optimization_barrier((mate_q[0], mine, o1))
-    other = lax.ppermute(away[:, :, :, 1:], "xl", SWAP)
-    mo1, _ = attend(q_in, kv, False, True)
+    q_in, o1 = lax.optimization_barrier((mate_q[0], o1))
+    (mo1,) = attend(q_in, kv, False, True)
     back1 = lax.ppermute(mo1, "yr", SWAP)
     q_in, mo1 = lax.optimization_barrier((mate_q[1], mo1))
-    mo2, _ = attend(q_in, kv, False, True)
+    (mo2,) = attend(q_in, kv, False, True)
     back2 = lax.ppermute(mo2, "yr", SWAP)
-    q_in, back1, mo2 = lax.optimization_barrier((qs[1], back1, mo2))
+    q_in, back1, mo2 = lax.optimization_barrier((q_last, back1, mo2))
     o2, l2 = attend(q_in, kv, False, False)
-    o = merge([(o1, l1, back1), (o2, l2, back2)])
+    other, o2 = lax.optimization_barrier((other, o2))
+    cross_send = cross(mine, other, None, True)
+    back2, cross_send = lax.optimization_barrier((back2, cross_send))
+    o = merge([(o1, l1), (o2, l2)], [back1, back2])
     back = lax.all_to_all(o, seq, split_axis=0, concat_axis=0, tiled=True)
     here, back = lax.optimization_barrier((mine, back))
     back = back.reshape(mine.shape[:3] + (rows, HD))
-    send = attended(here, other, back, True)
+    send = add_send(back, cross_send)
     came = lax.ppermute(send, "c", SWAP)
-    keep = attended(here, other, back, False)
+    keep = cross(here, other, back, False)
     return project(keep, came, out_weight, hidden, gate)[None]
 
 

time: 121 us -> 119 us (0.983)
  Pallas kernels: 29.7 us -> 27.7 us
  waiting for transfers between devices: 0.87 us -> 2.75 us
  blocking collectives: 74.9 us -> 73.3 us
    all_to_all x1, blocking collectives: 22.8 us -> 21.3 us  [local(): back = lax.all_to_all(o, seq, split_axis=0, concat_axis=0, tiled=True)]
    pallas_call x3 -> x4, Pallas kernels: 3.45 us -> 2.32 us  [the longest x2 1.88 us: cross(): pl.pallas_call(functools.partial(cross_kernel, flip=flip), in_specs=whole...]
    ppermute x9 -> x7, starting transfers between devices: 9.11 us -> 8.9 us  [swap(): return [lax.ppermute(x, axis, SWAP) for x in chunks]]
  transfers between devices with their start and end apart: 13 -> 11, of which waited for: 3 -> 5; matrix products, arithmetic and copies ran while one was open for 0% -> 0% of each run, Pallas kernels for 20% -> 20%
where the time goes in v5:
time: 119 us
  blocking collectives  73.3 us (62%)
  Pallas kernels  27.7 us (23%)
  starting transfers between devices  14.7 us (12%)
  waiting for transfers between devices  2.75 us (2%)
    all_to_all x1, blocking collectives, local(): lax.all_to_all(mine.reshape(n, 3 * rows, HD), seq, split_axis=0, concat_a...  52 us
    all_to_all x1, blocking collectives, local(): back = lax.all_to_all(o, seq, split_axis=0, concat_axis=0, tiled=True)  21.3 us
    pallas_call x4, Pallas kernels, attend(): pl.pallas_call(functools.partial(attend_kernel, first=first, travels=trav...  20.8 us
    ppermute x7, starting transfers between devices, swap(): return [lax.ppermute(x, axis, SWAP) for x in chunks]  8.9 us
    ppermute x1, starting transfers between devices, local(): came = lax.ppermute(send, 'c', SWAP)  3.58 us
  transfers between devices with their start and end apart: 11, of which 5 were waited for; matrix products, arithmetic and copies ran while one was open for 0% of the time, Pallas kernels for 20%

profile of v5, /device:TPU:1, one launch (start us, length us, event | category | flops | bytes accessed | tf_op | source)
XLA Modules:
  0.0 118.9 jit_solution(9819244246105947689)
XLA Ops:
  0.0 1.2 pack.3
  1.2 3.3 %collective-permute-start = (bf16[1,16,64,128]{3,2,1,0:T(8,128)(2,1)S(1)}, bf16[1,16,64,128]{3,2,1,0:T(8,128)(2,1)S(1)}, u32[]{:S(2)}, u32[]{:S(2)}) collective-permute-start(bf16[1,16,64,128]{3,2,1,0:T(8,128)(2,1)S(1)} %get-tuple-element.27), channel_id=1, source_target_pairs={{0,64},{64,0},{1,65},{65,1},{2,66},{66,2},{3,67},{67,3},{4,68},{68... | collective-permute-start | bytes 786440 | tf_op jit(solution)/shard_map/ppermute | solution.py:310
  4.5 0.1 collective-permute-start.1
  4.6 0.4 collective-permute-start.2
  5.0 1.2 pack.2.a_ref
  6.2 0.0 collective-permute-done.q_ref
  6.2 0.0 collective-permute-done.1.k_ref
  6.2 0.2 collective-permute-done.2.v_ref
  6.4 0.1 place.1.a_ref
  6.5 52.0 %all_to_all.10 = bf16[32,192,128]{2,1,0:T(8,128)(2,1)S(1)} all-to-all(bf16[32,192,128]{2,1,0:T(8,128)(2,1)S(1)} %bitcast.20), channel_id=1, replica_groups=mesh['xl'=2,'c'=2,'yv'=2,'yr'=2,'z'=8,'xh'=2] {'yv','z','xh'}, dimensions={0} | all-to-all | bytes 3145728 | tf_op jit(solution)/shard_map/all_to_all | solution.py:324
  58.5 0.1 slice.25
  58.6 0.4 collective-permute-start.6
  59.0 0.1 fusion
  59.1 3.4 %collective-permute-start.4 = (bf16[16,2,64,128]{3,2,1,0:T(8,128)(2,1)S(1)}, bf16[16,2,64,128]{3,2,1,0:T(8,128)(2,1)S(1)}, u32[]{:S(2)}, u32[]{:S(2)}) collective-permute-start(bf16[16,2,64,128]{3,2,1,0:T(8,128)(2,1)S(1)} %get-tuple-element.52.refs_1_), channel_id=1, source_target_pairs={{0,64},{64,0},{1,65},{65,1},{2,66},{66,2},{3,67},{67,3},{4,68},{68... | collective-permute-start | bytes 1572872 | tf_op jit(solution)/shard_map/ppermute | solution.py:310
  62.5 0.1 collective-permute-start.5
  62.6 0.5 collective-permute-start.3
  63.1 1.1 collective-permute-start.8
  64.2 0.0 collective-permute-done.4.refs_3_
  64.2 0.6 collective-permute-done.5.refs_4_
  64.8 6.6 %attend.4 = (f32[20,64,128]{2,1,0:T(8,128)S(1)}, f32[10,128]{1,0:T(8,128)S(1)}, bf16[4096,128]{1,0:T(8,128)(2,1)S(1)}, bf16[4096,256]{1,0:T(8,128)(2,1)S(1)}) custom-call(bf16[20,64,128]{2,1,0:T(8,128)(2,1)S(1)} %slice_bitcast_fusion.refs_0_, bf16[16,2,64,128]{3,2,1,0:T(8,128)(2,1)S(1)} %get-tuple-element.52.refs_1_, ...), custom_call_target="tpu_custom_call" | custom-call | tf_op jit(solution)/shard_map/attend/pallas_call | solution.py:167
  71.4 0.0 collective-permute-done.3.refs_0_
  71.4 5.1 %attend.5 = bf16[17,64,128]{2,1,0:T(8,128)(2,1)S(1)} custom-call(bf16[16,64,128]{2,1,0:T(8,128)(2,1)S(1)} %collective-permute-done.3.refs_0_, bf16[4096,128]{1,0:T(8,128)(2,1)S(1)} %get-tuple-element.36.refs_1_, bf16[4096,256]{1,0:T(8,128)(2,1)S(1)} %get-tuple-element.37.refs_2_), custom_call_target="tpu_custom_call" | custom-call | tf_op jit(solution)/shard_map/attend/pallas_call | solution.py:167
  76.5 0.7 collective-permute-start.7
  77.2 0.0 collective-permute-done.8.refs_0_
  77.2 0.0 slice-start
  77.2 5.1 %attend.6 = bf16[17,64,128]{2,1,0:T(8,128)(2,1)S(1)} custom-call(bf16[16,64,128]{2,1,0:T(8,128)(2,1)S(1)} %collective-permute-done.8.refs_0_, bf16[4096,128]{1,0:T(8,128)(2,1)S(1)} %get-tuple-element.36.refs_1_, bf16[4096,256]{1,0:T(8,128)(2,1)S(1)} %get-tuple-element.37.refs_2_), custom_call_target="tpu_custom_call" | custom-call | tf_op jit(solution)/shard_map/attend/pallas_call | solution.py:167
  82.3 1.2 collective-permute-start.9
  83.5 0.7 collective-permute-done.7.refs_4_
  84.1 4.0 %attend.7 = (f32[12,64,128]{2,1,0:T(8,128)S(1)}, f32[6,128]{1,0:T(8,128)S(1)}) custom-call(bf16[12,64,128]{2,1,0:T(8,128)(2,1)S(1)} %slice_bitcast_fusion.3.refs_0_, bf16[4096,128]{1,0:T(8,128)(2,1)S(1)} %get-tuple-element.36.refs_1_, bf16[4096,256]{1,0:T(8,128)(2,1)S(1)} %get-tuple-element.37.refs_2_), custom_call_target="tpu_custom_call" | custom-call | tf_op jit(solution)/shard_map/attend/pallas_call | solution.py:167
  88.1 0.0 collective-permute-done.6.b_ref
  88.1 0.0 slice-start.1
  88.1 0.9 cross.2.c_ref
  89.1 1.1 collective-permute-done.9.refs_5_
  90.2 0.4 merge.1
  90.6 21.3 %all_to_all.11 = bf16[32,64,128]{2,1,0:T(8,128)(2,1)S(1)} all-to-all(bf16[32,64,128]{2,1,0:T(8,128)(2,1)S(1)} %merge.1), channel_id=1, replica_groups=mesh['xl'=2,'c'=2,'yv'=2,'yr'=2,'z'=8,'xh'=2] {'yv','z','xh'}, dimensions={0} | all-to-all | bytes 1048576 | tf_op jit(solution)/shard_map/all_to_all | solution.py:349
  111.8 0.1 add_send.1
  111.9 0.0 copy-start
  111.9 0.0 copy-start.1
  111.9 3.6 %collective-permute-start.10 = (bf16[1,16,64,128]{3,2,1,0:T(8,128)(2,1)S(1)}, bf16[1,16,64,128]{3,2,1,0:T(8,128)(2,1)S(1)}, u32[]{:S(2)}, u32[]{:S(2)}) collective-permute-start(bf16[1,16,64,128]{3,2,1,0:T(8,128)(2,1)S(1)} %add_send.1), channel_id=1, source_target_pairs={{0,64},{64,0},{1,65},{65,1},{2,66},{66,2},{3,67},{67,3},{4,68},{68... | collective-permute-start | bytes 786440 | tf_op jit(solution)/shard_map/ppermute | solution.py:353
  115.5 1.0 cross.3.keep_ref
  116.5 0.2 collective-permute-done.10.came_ref
  116.7 0.0 slice-done
  116.7 0.0 slice-done.1
  116.7 0.0 copy-done
  116.7 0.0 copy-done.1
  116.7 2.2 %project.1 = bf16[128,2048]{1,0:T(8,128)(2,1)} custom-call(bf16[1,16,64,128]{3,2,1,0:T(8,128)(2,1)S(1)} %cross.3.keep_ref, bf16[1,16,64,128]{3,2,1,0:T(8,128)(2,1)S(1)} %collective-permute-done.10.came_ref, bf16[2048,2048]{1,0:T(8,128)(2,1)S(1)} %bitcast.22, bf16[128,2048]{1,0:T(8,128)(2,1)S(1)} %bitcast.25, bf16[1,2048]{1,0:T(2,128)(2,1)S(1)} %copy-done.1), custom_call_target="tpu_custom_call" | custom-call | tf_op jit(solution)/shard_map/project/pallas_call | solution.py:294
  (4 shorter events, 0.1 us)
Async XLA Ops:
  1.2 5.0 %collective-permute-start = (bf16[1,16,64,128]{3,2,1,0:T(8,128)(2,1)S(1)}, bf16[1,16,64,128]{3,2,1,0:T(8,128)(2,1)S(1)}, u32[]{:S(2)}, u32[]{:S(2)}) collective-permute-start(bf16[1,16,64,128]{3,2,1,0:T(8,128)(2,1)S(1)} %get-tuple-element.27), channel_id=1, source_target_pairs={{0,64},{64,0},{1,65},{65,1},{2,66},{66,2},{3,67},{67,3},{4,68},{68... | collective-permute-start | bytes 786440 | tf_op jit(solution)/shard_map/ppermute | solution.py:310
  4.5 1.7 %collective-permute-start.1 = (bf16[1,16,64,128]{3,2,1,0:T(8,128)(2,1)S(1)}, bf16[1,16,64,128]{3,2,1,0:T(8,128)(2,1)S(1)}, u32[]{:S(2)}, u32[]{:S(2)}) collective-permute-start(bf16[1,16,64,128]{3,2,1,0:T(8,128)(2,1)S(1)} %get-tuple-element.28), channel_id=1, source_target_pairs={{0,64},{64,0},{1,65},{65,1},{2,66},{66,2},{3,67},{67,3},{4,68},{68... | collective-permute-start | bytes 786440 | tf_op jit(solution)/shard_map/ppermute | solution.py:310
  4.6 1.8 %collective-permute-start.2 = (bf16[1,16,64,128]{3,2,1,0:T(8,128)(2,1)S(1)}, bf16[1,16,64,128]{3,2,1,0:T(8,128)(2,1)S(1)}, u32[]{:S(2)}, u32[]{:S(2)}) collective-permute-start(bf16[1,16,64,128]{3,2,1,0:T(8,128)(2,1)S(1)} %get-tuple-element.29), channel_id=1, source_target_pairs={{0,64},{64,0},{1,65},{65,1},{2,66},{66,2},{3,67},{67,3},{4,68},{68... | collective-permute-start | bytes 786440 | tf_op jit(solution)/shard_map/ppermute | solution.py:310
  58.6 29.5 %collective-permute-start.6 = (bf16[2,1,16,2,64,128]{5,4,3,2,1,0:T(8,128)(2,1)S(1)}, bf16[2,1,16,2,64,128]{5,4,3,2,1,0:T(8,128)(2,1)S(1)}, u32[]{:S(2)}, u32[]{:S(2)}) collective-permute-start(bf16[2,1,16,2,64,128]{5,4,3,2,1,0:T(8,128)(2,1)S(1)} %slice.25), channel_id=1, source_target_pairs={{0,128},{128,0},{1,129},{129,1},{2,130},{130,2},{3,131},{131,3},{4... | collective-permute-start | bytes 3145736 | tf_op jit(solution)/shard_map/ppermute | solution.py:332
  59.1 5.1 %collective-permute-start.4 = (bf16[16,2,64,128]{3,2,1,0:T(8,128)(2,1)S(1)}, bf16[16,2,64,128]{3,2,1,0:T(8,128)(2,1)S(1)}, u32[]{:S(2)}, u32[]{:S(2)}) collective-permute-start(bf16[16,2,64,128]{3,2,1,0:T(8,128)(2,1)S(1)} %get-tuple-element.52.refs_1_), channel_id=1, source_target_pairs={{0,64},{64,0},{1,65},{65,1},{2,66},{66,2},{3,67},{67,3},{4,68},{68... | collective-permute-start | bytes 1572872 | tf_op jit(solution)/shard_map/ppermute | solution.py:310
  62.5 2.3 %collective-permute-start.5 = (bf16[16,2,64,128]{3,2,1,0:T(8,128)(2,1)S(1)}, bf16[16,2,64,128]{3,2,1,0:T(8,128)(2,1)S(1)}, u32[]{:S(2)}, u32[]{:S(2)}) collective-permute-start(bf16[16,2,64,128]{3,2,1,0:T(8,128)(2,1)S(1)} %get-tuple-element.51.refs_2_), channel_id=1, source_target_pairs={{0,64},{64,0},{1,65},{65,1},{2,66},{66,2},{3,67},{67,3},{4,68},{68... | collective-permute-start | bytes 1572872 | tf_op jit(solution)/shard_map/ppermute | solution.py:310
  62.6 8.8 %collective-permute-start.3 = (bf16[16,64,128]{2,1,0:T(8,128)(2,1)S(1)}, bf16[16,64,128]{2,1,0:T(8,128)(2,1)S(1)}, u32[]{:S(2)}, u32[]{:S(2)}) collective-permute-start(bf16[16,64,128]{2,1,0:T(8,128)(2,1)S(1)} %get-tuple-element.50), channel_id=1, source_target_pairs={{0,16},{16,0},{1,17},{17,1},{2,18},{18,2},{3,19},{19,3},{4,20},{20... | collective-permute-start | bytes 786440 | tf_op jit(solution)/shard_map/ppermute | solution.py:310
  63.1 14.1 %collective-permute-start.8 = (bf16[16,64,128]{2,1,0:T(8,128)(2,1)S(1)}, bf16[16,64,128]{2,1,0:T(8,128)(2,1)S(1)}, u32[]{:S(2)}, u32[]{:S(2)}) collective-permute-start(bf16[16,64,128]{2,1,0:T(8,128)(2,1)S(1)} %get-tuple-element.49), channel_id=1, source_target_pairs={{0,16},{16,0},{1,17},{17,1},{2,18},{18,2},{3,19},{19,3},{4,20},{20... | collective-permute-start | bytes 786440 | tf_op jit(solution)/shard_map/ppermute | solution.py:310
  76.5 7.6 %collective-permute-start.7 = (bf16[17,64,128]{2,1,0:T(8,128)(2,1)S(1)}, bf16[17,64,128]{2,1,0:T(8,128)(2,1)S(1)}, u32[]{:S(2)}, u32[]{:S(2)}) collective-permute-start(bf16[17,64,128]{2,1,0:T(8,128)(2,1)S(1)} %attend.5), channel_id=1, source_target_pairs={{0,16},{16,0},{1,17},{17,1},{2,18},{18,2},{3,19},{19,3},{4,20},{20... | collective-permute-start | bytes 835592 | tf_op jit(solution)/shard_map/ppermute | solution.py:339
  77.2 39.5 %slice-start = ((s8[8388608]{0:T(1024)(128)(4,1)}), s8[4194304]{0:T(1024)(128)(4,1)S(1)}, s32[]{:S(2)}) async-start(s8[8388608]{0:T(1024)(128)(4,1)} %bitcast.21), calls=%async_computation.2 | async-start | bytes 8388608
  82.3 7.9 %collective-permute-start.9 = (bf16[17,64,128]{2,1,0:T(8,128)(2,1)S(1)}, bf16[17,64,128]{2,1,0:T(8,128)(2,1)S(1)}, u32[]{:S(2)}, u32[]{:S(2)}) collective-permute-start(bf16[17,64,128]{2,1,0:T(8,128)(2,1)S(1)} %attend.6), channel_id=1, source_target_pairs={{0,16},{16,0},{1,17},{17,1},{2,18},{18,2},{3,19},{19,3},{4,20},{20... | collective-permute-start | bytes 835592 | tf_op jit(solution)/shard_map/ppermute | solution.py:342
  88.1 28.6 %slice-start.1 = ((s8[8388608]{0:T(1024)(128)(4,1)}), s8[4194304]{0:T(1024)(128)(4,1)S(1)}, s32[]{:S(2)}) async-start(s8[8388608]{0:T(1024)(128)(4,1)} %bitcast.21), calls=%async_computation.3 | async-start | bytes 8388608
  111.9 4.8 %copy-start = (bf16[1,128,2048]{2,1,0:T(8,128)(2,1)S(1)}, bf16[1,128,2048]{2,1,0:T(8,128)(2,1)}, u32[]{:S(2)}) copy-start(bf16[1,128,2048]{2,1,0:T(8,128)(2,1)} %param.6) | copy-start | bytes 1572868
  111.9 4.8 %copy-start.1 = (bf16[1,2048]{1,0:T(2,128)(2,1)S(1)}, bf16[1,2048]{1,0:T(2,128)(2,1)}, u32[]{:S(2)}) copy-start(bf16[1,2048]{1,0:T(2,128)(2,1)} %g_ref.1) | copy-start | bytes 12292
  111.9 4.7 %collective-permute-start.10 = (bf16[1,16,64,128]{3,2,1,0:T(8,128)(2,1)S(1)}, bf16[1,16,64,128]{3,2,1,0:T(8,128)(2,1)S(1)}, u32[]{:S(2)}, u32[]{:S(2)}) collective-permute-start(bf16[1,16,64,128]{3,2,1,0:T(8,128)(2,1)S(1)} %add_send.1), channel_id=1, source_target_pairs={{0,64},{64,0},{1,65},{65,1},{2,66},{66,2},{3,67},{67,3},{4,68},{68... | collective-permute-start | bytes 786440 | tf_op jit(solution)/shard_map/ppermute | solution.py:353

commit v6 on v5

--- a/solution.py
+++ b/solution.py
@@ -324,28 +324,31 @@
     got = lax.all_to_all(mine.reshape(n, 3 * rows, HD), seq, split_axis=0, concat_axis=0, tiled=True)
     got = got.reshape(n, 3, rows, HD)
 
-    step, half, lead = n // CHUNKS, n // 2, n * 5 // 8
+    step, half = n // CHUNKS, n // 2
     own = [got[i * step : (i + 1) * step, 1:] for i in range(CHUNKS)]
     own_pair = swap(own, "c")
-    q_first, q_last = got[:lead, 0], got[lead:, 0]
+    qs = [got[a * n // 4 : b * n // 4, 0] for a, b in ((0, 1), (1, 2), (2, 4))]
     here, got = lax.optimization_barrier((mine, got))
     other = lax.ppermute(here[:, :, :, 1:], "xl", SWAP)
-    mate_q = swap([got[:half, 0], got[half:, 0]], "yr")
-
-    o1, l1, keys_all, values_all = attend(q_first, own + own_pair, True, False)
+    mate_q1 = lax.ppermute(got[:half, 0], "yr", SWAP)
+
+    o1, l1, keys_all, values_all = attend(qs[0], own + own_pair, True, False)
     kv = keys_all, values_all
-    q_in, o1 = lax.optimization_barrier((mate_q[0], o1))
+    q_in, q2, o1 = lax.optimization_barrier((qs[1], got[half:, 0], o1))
+    mate_q2 = lax.ppermute(q2, "yr", SWAP)
+    o2, l2 = attend(q_in, kv, False, False)
+    q_in, o2 = lax.optimization_barrier((mate_q1, o2))
     (mo1,) = attend(q_in, kv, False, True)
     back1 = lax.ppermute(mo1, "yr", SWAP)
-    q_in, mo1 = lax.optimization_barrier((mate_q[1], mo1))
+    q_in, mo1 = lax.optimization_barrier((mate_q2, mo1))
     (mo2,) = attend(q_in, kv, False, True)
     back2 = lax.ppermute(mo2, "yr", SWAP)
-    q_in, back1, mo2 = lax.optimization_barrier((q_last, back1, mo2))
-    o2, l2 = attend(q_in, kv, False, False)
-    other, o2 = lax.optimization_barrier((other, o2))
+    q_in, back1, mo2 = lax.optimization_barrier((qs[2], back1, mo2))
+    o3, l3 = attend(q_in, kv, False, False)
+    other, o3 = lax.optimization_barrier((other, o3))
     cross_send = cross(mine, other, None, True)
     back2, cross_send = lax.optimization_barrier((back2, cross_send))
-    o = merge([(o1, l1), (o2, l2)], [back1, back2])
+    o = merge([(o1, l1), (o2, l2), (o3, l3)], [back1, back2])
     back = lax.all_to_all(o, seq, split_axis=0, concat_axis=0, tiled=True)
     here, back = lax.optimization_barrier((mine, back))
     back = back.reshape(mine.shape[:3] + (rows, HD))

time: 119 us -> 119 us (level)
    ppermute x7 -> x5, starting transfers between devices: 8.9 us -> 7.07 us  [swap(): return [lax.ppermute(x, axis, SWAP) for x in chunks]]
    pallas_call x4 -> x5, Pallas kernels: 20.8 us -> 21.1 us  [attend(): pl.pallas_call(functools.partial(attend_kernel, first=first, travels=trav...]
  transfers between devices with their start and end apart: 11 -> 11, of which waited for: 5 -> 6; matrix products, arithmetic and copies ran while one was open for 0% -> 0% of each run, Pallas kernels for 20% -> 20%
where the time goes in v6:
time: 119 us; the launch traced here: 118 us
  blocking collectives  73.4 us (62%)
  Pallas kernels  28 us (24%)
  starting transfers between devices  14.1 us (12%)
  waiting for transfers between devices  2.4 us (2%)
    all_to_all x1, blocking collectives, local(): lax.all_to_all(mine.reshape(n, 3 * rows, HD), seq, split_axis=0, concat_a...  52 us
    all_to_all x1, blocking collectives, local(): back = lax.all_to_all(o, seq, split_axis=0, concat_axis=0, tiled=True)  21.4 us
    pallas_call x5, Pallas kernels, attend(): pl.pallas_call(functools.partial(attend_kernel, first=first, travels=trav...  21.1 us
    ppermute x5, starting transfers between devices, swap(): return [lax.ppermute(x, axis, SWAP) for x in chunks]  7.07 us
    ppermute x1, starting transfers between devices, local(): came = lax.ppermute(send, 'c', SWAP)  3.59 us
  transfers between devices with their start and end apart: 11, of which 6 were waited for; matrix products, arithmetic and copies ran while one was open for 0% of the time, Pallas kernels for 20%

profile of v6, /device:TPU:1, one launch (start us, length us, event | category | flops | bytes accessed | tf_op | source)
XLA Modules:
  0.0 118.3 jit_solution(8359110087080518259)
XLA Ops:
  0.0 1.2 pack.3
  1.2 3.3 %collective-permute-start = (bf16[1,16,64,128]{3,2,1,0:T(8,128)(2,1)S(1)}, bf16[1,16,64,128]{3,2,1,0:T(8,128)(2,1)S(1)}, u32[]{:S(2)}, u32[]{:S(2)}) collective-permute-start(bf16[1,16,64,128]{3,2,1,0:T(8,128)(2,1)S(1)} %get-tuple-element.32), channel_id=1, source_target_pairs={{0,64},{64,0},{1,65},{65,1},{2,66},{66,2},{3,67},{67,3},{4,68},{68... | collective-permute-start | bytes 786440 | tf_op jit(solution)/shard_map/ppermute | solution.py:310
  4.5 0.1 collective-permute-start.1
  4.6 0.4 collective-permute-start.2
  5.0 1.2 pack.2.a_ref
  6.2 0.0 collective-permute-done.q_ref
  6.2 0.0 collective-permute-done.1.k_ref
  6.2 0.2 collective-permute-done.2.v_ref
  6.4 0.1 place.1.a_ref
  6.5 52.0 %all_to_all.10 = bf16[32,192,128]{2,1,0:T(8,128)(2,1)S(1)} all-to-all(bf16[32,192,128]{2,1,0:T(8,128)(2,1)S(1)} %bitcast.24), channel_id=1, replica_groups=mesh['xl'=2,'c'=2,'yv'=2,'yr'=2,'z'=8,'xh'=2] {'yv','z','xh'}, dimensions={0} | all-to-all | bytes 3145728 | tf_op jit(solution)/shard_map/all_to_all | solution.py:324
  58.5 0.1 fusion
  58.6 3.1 %collective-permute-start.3 = (bf16[16,2,64,128]{3,2,1,0:T(8,128)(2,1)S(1)}, bf16[16,2,64,128]{3,2,1,0:T(8,128)(2,1)S(1)}, u32[]{:S(2)}, u32[]{:S(2)}) collective-permute-start(bf16[16,2,64,128]{3,2,1,0:T(8,128)(2,1)S(1)} %get-tuple-element.62.refs_1_), channel_id=1, source_target_pairs={{0,64},{64,0},{1,65},{65,1},{2,66},{66,2},{3,67},{67,3},{4,68},{68... | collective-permute-start | bytes 1572872 | tf_op jit(solution)/shard_map/ppermute | solution.py:310
  61.7 0.1 collective-permute-start.4
  61.8 0.1 slice.30
  61.9 0.4 collective-permute-start.6
  62.4 0.5 collective-permute-start.5
  62.9 0.4 collective-permute-done.3.refs_3_
  63.3 0.7 collective-permute-done.4.refs_4_
  64.0 3.2 %attend.5 = (f32[8,64,128]{2,1,0:T(8,128)S(1)}, f32[4,128]{1,0:T(4,128)S(1)}, bf16[4096,128]{1,0:T(8,128)(2,1)S(1)}, bf16[4096,256]{1,0:T(8,128)(2,1)S(1)}) custom-call(bf16[8,64,128]{2,1,0:T(8,128)(2,1)S(1)} %get-tuple-element.63.refs_0_, bf16[16,2,64,128]{3,2,1,0:T(8,128)(2,1)S(1)} %get-tuple-element.62.refs_1_, ...), custom_call_target="tpu_custom_call" | custom-call | tf_op jit(solution)/shard_map/attend/pallas_call | solution.py:167
  67.2 0.7 collective-permute-start.8
  67.8 2.9 %attend.6 = (f32[8,64,128]{2,1,0:T(8,128)S(1)}, f32[4,128]{1,0:T(4,128)S(1)}) custom-call(bf16[8,64,128]{2,1,0:T(8,128)(2,1)S(1)} %get-tuple-element.39.refs_0_, bf16[4096,128]{1,0:T(8,128)(2,1)S(1)} %get-tuple-element.40.refs_1_, bf16[4096,256]{1,0:T(8,128)(2,1)S(1)} %get-tuple-element.41.refs_2_), custom_call_target="tpu_custom_call" | custom-call | tf_op jit(solution)/shard_map/attend/pallas_call | solution.py:167
  70.7 0.0 collective-permute-done.5.refs_0_
  70.7 5.0 %attend.7 = bf16[17,64,128]{2,1,0:T(8,128)(2,1)S(1)} custom-call(bf16[16,64,128]{2,1,0:T(8,128)(2,1)S(1)} %collective-permute-done.5.refs_0_, bf16[4096,128]{1,0:T(8,128)(2,1)S(1)} %get-tuple-element.40.refs_1_, bf16[4096,256]{1,0:T(8,128)(2,1)S(1)} %get-tuple-element.41.refs_2_), custom_call_target="tpu_custom_call" | custom-call | tf_op jit(solution)/shard_map/attend/pallas_call | solution.py:167
  75.7 1.4 %collective-permute-start.7 = (bf16[17,64,128]{2,1,0:T(8,128)(2,1)S(1)}, bf16[17,64,128]{2,1,0:T(8,128)(2,1)S(1)}, u32[]{:S(2)}, u32[]{:S(2)}) collective-permute-start(bf16[17,64,128]{2,1,0:T(8,128)(2,1)S(1)} %attend.7), channel_id=1, source_target_pairs={{0,16},{16,0},{1,17},{17,1},{2,18},{18,2},{3,19},{19,3},{4,20},{20... | collective-permute-start | bytes 835592 | tf_op jit(solution)/shard_map/ppermute | solution.py:342
  77.1 0.0 collective-permute-done.8.refs_0_
  77.1 0.0 slice-start
  77.1 5.0 %attend.8 = bf16[17,64,128]{2,1,0:T(8,128)(2,1)S(1)} custom-call(bf16[16,64,128]{2,1,0:T(8,128)(2,1)S(1)} %collective-permute-done.8.refs_0_, bf16[4096,128]{1,0:T(8,128)(2,1)S(1)} %get-tuple-element.40.refs_1_, bf16[4096,256]{1,0:T(8,128)(2,1)S(1)} %get-tuple-element.41.refs_2_), custom_call_target="tpu_custom_call" | custom-call | tf_op jit(solution)/shard_map/attend/pallas_call | solution.py:167
  82.1 0.5 collective-permute-start.9
  82.6 0.5 collective-permute-done.7.refs_6_
  83.2 5.0 %attend.9 = (f32[16,64,128]{2,1,0:T(8,128)S(1)}, f32[8,128]{1,0:T(8,128)S(1)}) custom-call(bf16[16,64,128]{2,1,0:T(8,128)(2,1)S(1)} %slice_bitcast_fusion.refs_0_, bf16[4096,128]{1,0:T(8,128)(2,1)S(1)} %get-tuple-element.40.refs_1_, bf16[4096,256]{1,0:T(8,128)(2,1)S(1)} %get-tuple-element.41.refs_2_), custom_call_target="tpu_custom_call" | custom-call | tf_op jit(solution)/shard_map/attend/pallas_call | solution.py:167
  88.2 0.0 collective-permute-done.6.b_ref
  88.2 0.0 slice-start.1
  88.2 0.9 cross.2.c_ref
  89.1 0.3 collective-permute-done.9.refs_7_
  89.5 0.4 merge.1
  89.8 21.4 %all_to_all.11 = bf16[32,64,128]{2,1,0:T(8,128)(2,1)S(1)} all-to-all(bf16[32,64,128]{2,1,0:T(8,128)(2,1)S(1)} %merge.1), channel_id=1, replica_groups=mesh['xl'=2,'c'=2,'yv'=2,'yr'=2,'z'=8,'xh'=2] {'yv','z','xh'}, dimensions={0} | all-to-all | bytes 1048576 | tf_op jit(solution)/shard_map/all_to_all | solution.py:352
  111.2 0.1 add_send.1
  111.3 0.0 copy-start
  111.3 0.0 copy-start.1
  111.3 3.6 %collective-permute-start.10 = (bf16[1,16,64,128]{3,2,1,0:T(8,128)(2,1)S(1)}, bf16[1,16,64,128]{3,2,1,0:T(8,128)(2,1)S(1)}, u32[]{:S(2)}, u32[]{:S(2)}) collective-permute-start(bf16[1,16,64,128]{3,2,1,0:T(8,128)(2,1)S(1)} %add_send.1), channel_id=1, source_target_pairs={{0,64},{64,0},{1,65},{65,1},{2,66},{66,2},{3,67},{67,3},{4,68},{68... | collective-permute-start | bytes 786440 | tf_op jit(solution)/shard_map/ppermute | solution.py:356
  114.9 1.0 cross.3.keep_ref
  115.9 0.2 collective-permute-done.10.came_ref
  116.1 0.0 slice-done
  116.1 0.0 slice-done.1
  116.1 0.0 copy-done
  116.1 0.0 copy-done.1
  116.1 2.2 %project.1 = bf16[128,2048]{1,0:T(8,128)(2,1)} custom-call(bf16[1,16,64,128]{3,2,1,0:T(8,128)(2,1)S(1)} %cross.3.keep_ref, bf16[1,16,64,128]{3,2,1,0:T(8,128)(2,1)S(1)} %collective-permute-done.10.came_ref, bf16[2048,2048]{1,0:T(8,128)(2,1)S(1)} %bitcast.26, bf16[128,2048]{1,0:T(8,128)(2,1)S(1)} %bitcast.29, bf16[1,2048]{1,0:T(2,128)(2,1)S(1)} %copy-done.1), custom_call_target="tpu_custom_call" | custom-call | tf_op jit(solution)/shard_map/project/pallas_call | solution.py:294
  (4 shorter events, 0.1 us)
Async XLA Ops:
  1.2 5.0 %collective-permute-start = (bf16[1,16,64,128]{3,2,1,0:T(8,128)(2,1)S(1)}, bf16[1,16,64,128]{3,2,1,0:T(8,128)(2,1)S(1)}, u32[]{:S(2)}, u32[]{:S(2)}) collective-permute-start(bf16[1,16,64,128]{3,2,1,0:T(8,128)(2,1)S(1)} %get-tuple-element.32), channel_id=1, source_target_pairs={{0,64},{64,0},{1,65},{65,1},{2,66},{66,2},{3,67},{67,3},{4,68},{68... | collective-permute-start | bytes 786440 | tf_op jit(solution)/shard_map/ppermute | solution.py:310
  4.5 1.7 %collective-permute-start.1 = (bf16[1,16,64,128]{3,2,1,0:T(8,128)(2,1)S(1)}, bf16[1,16,64,128]{3,2,1,0:T(8,128)(2,1)S(1)}, u32[]{:S(2)}, u32[]{:S(2)}) collective-permute-start(bf16[1,16,64,128]{3,2,1,0:T(8,128)(2,1)S(1)} %get-tuple-element.33), channel_id=1, source_target_pairs={{0,64},{64,0},{1,65},{65,1},{2,66},{66,2},{3,67},{67,3},{4,68},{68... | collective-permute-start | bytes 786440 | tf_op jit(solution)/shard_map/ppermute | solution.py:310
  4.6 1.8 %collective-permute-start.2 = (bf16[1,16,64,128]{3,2,1,0:T(8,128)(2,1)S(1)}, bf16[1,16,64,128]{3,2,1,0:T(8,128)(2,1)S(1)}, u32[]{:S(2)}, u32[]{:S(2)}) collective-permute-start(bf16[1,16,64,128]{3,2,1,0:T(8,128)(2,1)S(1)} %get-tuple-element.34), channel_id=1, source_target_pairs={{0,64},{64,0},{1,65},{65,1},{2,66},{66,2},{3,67},{67,3},{4,68},{68... | collective-permute-start | bytes 786440 | tf_op jit(solution)/shard_map/ppermute | solution.py:310
  58.6 4.7 %collective-permute-start.3 = (bf16[16,2,64,128]{3,2,1,0:T(8,128)(2,1)S(1)}, bf16[16,2,64,128]{3,2,1,0:T(8,128)(2,1)S(1)}, u32[]{:S(2)}, u32[]{:S(2)}) collective-permute-start(bf16[16,2,64,128]{3,2,1,0:T(8,128)(2,1)S(1)} %get-tuple-element.62.refs_1_), channel_id=1, source_target_pairs={{0,64},{64,0},{1,65},{65,1},{2,66},{66,2},{3,67},{67,3},{4,68},{68... | collective-permute-start | bytes 1572872 | tf_op jit(solution)/shard_map/ppermute | solution.py:310
  61.7 2.3 %collective-permute-start.4 = (bf16[16,2,64,128]{3,2,1,0:T(8,128)(2,1)S(1)}, bf16[16,2,64,128]{3,2,1,0:T(8,128)(2,1)S(1)}, u32[]{:S(2)}, u32[]{:S(2)}) collective-permute-start(bf16[16,2,64,128]{3,2,1,0:T(8,128)(2,1)S(1)} %get-tuple-element.61.refs_2_), channel_id=1, source_target_pairs={{0,64},{64,0},{1,65},{65,1},{2,66},{66,2},{3,67},{67,3},{4,68},{68... | collective-permute-start | bytes 1572872 | tf_op jit(solution)/shard_map/ppermute | solution.py:310
  61.9 26.3 %collective-permute-start.6 = (bf16[2,1,16,2,64,128]{5,4,3,2,1,0:T(8,128)(2,1)S(1)}, bf16[2,1,16,2,64,128]{5,4,3,2,1,0:T(8,128)(2,1)S(1)}, u32[]{:S(2)}, u32[]{:S(2)}) collective-permute-start(bf16[2,1,16,2,64,128]{5,4,3,2,1,0:T(8,128)(2,1)S(1)} %slice.30), channel_id=1, source_target_pairs={{0,128},{128,0},{1,129},{129,1},{2,130},{130,2},{3,131},{131,3},{4... | collective-permute-start | bytes 3145736 | tf_op jit(solution)/shard_map/ppermute | solution.py:332
  62.4 8.3 %collective-permute-start.5 = (bf16[16,64,128]{2,1,0:T(8,128)(2,1)S(1)}, bf16[16,64,128]{2,1,0:T(8,128)(2,1)S(1)}, u32[]{:S(2)}, u32[]{:S(2)}) collective-permute-start(bf16[16,64,128]{2,1,0:T(8,128)(2,1)S(1)} %get-tuple-element.59), channel_id=1, source_target_pairs={{0,16},{16,0},{1,17},{17,1},{2,18},{18,2},{3,19},{19,3},{4,20},{20... | collective-permute-start | bytes 786440 | tf_op jit(solution)/shard_map/ppermute | solution.py:333
  67.2 9.9 %collective-permute-start.8 = (bf16[16,64,128]{2,1,0:T(8,128)(2,1)S(1)}, bf16[16,64,128]{2,1,0:T(8,128)(2,1)S(1)}, u32[]{:S(2)}, u32[]{:S(2)}) collective-permute-start(bf16[16,64,128]{2,1,0:T(8,128)(2,1)S(1)} %get-tuple-element.47), channel_id=1, source_target_pairs={{0,16},{16,0},{1,17},{17,1},{2,18},{18,2},{3,19},{19,3},{4,20},{20... | collective-permute-start | bytes 786440 | tf_op jit(solution)/shard_map/ppermute | solution.py:338
  75.7 7.4 %collective-permute-start.7 = (bf16[17,64,128]{2,1,0:T(8,128)(2,1)S(1)}, bf16[17,64,128]{2,1,0:T(8,128)(2,1)S(1)}, u32[]{:S(2)}, u32[]{:S(2)}) collective-permute-start(bf16[17,64,128]{2,1,0:T(8,128)(2,1)S(1)} %attend.7), channel_id=1, source_target_pairs={{0,16},{16,0},{1,17},{17,1},{2,18},{18,2},{3,19},{19,3},{4,20},{20... | collective-permute-start | bytes 835592 | tf_op jit(solution)/shard_map/ppermute | solution.py:342
  77.1 39.0 %slice-start = ((s8[8388608]{0:T(1024)(128)(4,1)}), s8[4194304]{0:T(1024)(128)(4,1)S(1)}, s32[]{:S(2)}) async-start(s8[8388608]{0:T(1024)(128)(4,1)} %bitcast.25), calls=%async_computation.2 | async-start | bytes 8388608
  82.1 7.3 %collective-permute-start.9 = (bf16[17,64,128]{2,1,0:T(8,128)(2,1)S(1)}, bf16[17,64,128]{2,1,0:T(8,128)(2,1)S(1)}, u32[]{:S(2)}, u32[]{:S(2)}) collective-permute-start(bf16[17,64,128]{2,1,0:T(8,128)(2,1)S(1)} %attend.8), channel_id=1, source_target_pairs={{0,16},{16,0},{1,17},{17,1},{2,18},{18,2},{3,19},{19,3},{4,20},{20... | collective-permute-start | bytes 835592 | tf_op jit(solution)/shard_map/ppermute | solution.py:345
  88.2 27.9 %slice-start.1 = ((s8[8388608]{0:T(1024)(128)(4,1)}), s8[4194304]{0:T(1024)(128)(4,1)S(1)}, s32[]{:S(2)}) async-start(s8[8388608]{0:T(1024)(128)(4,1)} %bitcast.25), calls=%async_computation.3 | async-start | bytes 8388608
  111.3 4.8 %copy-start = (bf16[1,128,2048]{2,1,0:T(8,128)(2,1)S(1)}, bf16[1,128,2048]{2,1,0:T(8,128)(2,1)}, u32[]{:S(2)}) copy-start(bf16[1,128,2048]{2,1,0:T(8,128)(2,1)} %param.6) | copy-start | bytes 1572868
  111.3 4.8 %copy-start.1 = (bf16[1,2048]{1,0:T(2,128)(2,1)S(1)}, bf16[1,2048]{1,0:T(2,128)(2,1)}, u32[]{:S(2)}) copy-start(bf16[1,2048]{1,0:T(2,128)(2,1)} %g_ref.1) | copy-start | bytes 12292
  111.3 4.7 %collective-permute-start.10 = (bf16[1,16,64,128]{3,2,1,0:T(8,128)(2,1)S(1)}, bf16[1,16,64,128]{3,2,1,0:T(8,128)(2,1)S(1)}, u32[]{:S(2)}, u32[]{:S(2)}) collective-permute-start(bf16[1,16,64,128]{3,2,1,0:T(8,128)(2,1)S(1)} %add_send.1), channel_id=1, source_target_pairs={{0,64},{64,0},{1,65},{65,1},{2,66},{66,2},{3,67},{67,3},{4,68},{68... | collective-permute-start | bytes 786440 | tf_op jit(solution)/shard_map/ppermute | solution.py:356

commit v7 on v6

--- a/solution.py
+++ b/solution.py
@@ -38,12 +38,12 @@
     return moves
 
 
-def pack_send_kernel(q_ref, k_ref, v_ref, sq_ref, sk_ref, sv_ref, held, sems):
+def pack_send_kernel(q_ref, k_ref, v_ref, o_ref, held, sems):
     moves = fetch_half(1 - lax.axis_index("c"), (q_ref, k_ref, v_ref), held, sems)
-    for j, out in enumerate((sq_ref, sk_ref, sv_ref)):
+    for j in range(3):
         moves[j].wait()
-        for h in range(out.shape[1]):
-            out[0, h] = held[j, :, h * HD : (h + 1) * HD]
+        for h in range(o_ref.shape[1]):
+            o_ref[j, h] = held[j, :, h * HD : (h + 1) * HD]
 
 
 def pack_keep_kernel(q_ref, k_ref, v_ref, o_ref, held, sems):
@@ -68,25 +68,23 @@
     )(*(pltpu.with_memory_space_constraint(x, pltpu.HBM) for x in (q, k, v)))
 
 
-def place_kernel(a_ref, q_ref, k_ref, v_ref, o_ref):
-    _, parts, heads = a_ref.shape[:3]
+def place_kernel(a_ref, got_ref, o_ref):
     you = 1 - lax.axis_index("c")
-    for j, ref in enumerate((q_ref, k_ref, v_ref)):
-        for r in range(parts):
-            for h in range(heads):
-                o_ref[you, r, h, j] = ref[r, h]
+    for j in range(got_ref.shape[0]):
+        for h in range(got_ref.shape[1]):
+            o_ref[you, 0, h, j] = got_ref[j, h]
 
 
 def place(mine, got):
     return pl.pallas_call(
         place_kernel,
-        in_specs=whole(4),
+        in_specs=whole(2),
         out_specs=pl.BlockSpec(memory_space=pltpu.VMEM),
         out_shape=jax.ShapeDtypeStruct(mine.shape, BF),
         input_output_aliases={0: 0},
         compiler_params=params(),
         name="place",
-    )(mine, *got)
+    )(mine, got)
 
 
 def gather_kv(kv_refs, k_all, v_all):
@@ -154,7 +152,7 @@
 def attend(q, kv, first, travels, kb=2048):
     src, rows, _ = q.shape
     nq = src * rows
-    qb = nq // 2
+    qb = nq if nq <= 512 else nq // 2
     total = sum(a.shape[0] * a.shape[2] for a in kv) if first else kv[0].shape[0]
     out_shape = [jax.ShapeDtypeStruct((src + travels, rows, HD), BF if travels else F32)]
     if not travels:
@@ -303,7 +301,7 @@
 
 
 SWAP = [(0, 1), (1, 0)]
-CHUNKS = 2
+CHUNKS = 1
 
 
 def swap(chunks, axis):
@@ -317,8 +315,8 @@
     rows = tok // 2
     n = 2 * HEADS
 
-    away = pack(pack_send_kernel, [(1, HEADS, rows, HD)] * 3, q, k, v)
-    came = swap(away, "c")
+    (away,) = pack(pack_send_kernel, [(3, HEADS, rows, HD)], q, k, v)
+    came = lax.ppermute(away, "c", SWAP)
     (mine,) = pack(pack_keep_kernel, [(2, 1, HEADS, 3, rows, HD)], q, k, v)
     mine = place(mine, came)
     got = lax.all_to_all(mine.reshape(n, 3 * rows, HD), seq, split_axis=0, concat_axis=0, tiled=True)

time: 119 us -> 118 us (level)
    ppermute x5 -> x1, starting transfers between devices: 7.07 us -> 3.13 us  [swap(): return [lax.ppermute(x, axis, SWAP) for x in chunks]]
    ppermute x0 -> x1, starting transfers between devices: none -> 3.33 us  [local(): came = lax.ppermute(away, 'c', SWAP)]
  transfers between devices with their start and end apart: 11 -> 8, of which waited for: 6 -> 5; matrix products, arithmetic and copies ran while one was open for 0% -> 0% of each run, Pallas kernels for 20% -> 20%
where the time goes in v7:
time: 118 us
  blocking collectives  73.2 us (62%)
  Pallas kernels  27.6 us (23%)
  starting transfers between devices  13.5 us (11%)
  waiting for transfers between devices  2.91 us (2%)
    all_to_all x1, blocking collectives, local(): lax.all_to_all(mine.reshape(n, 3 * rows, HD), seq, split_axis=0, concat_a...  52 us
    all_to_all x1, blocking collectives, local(): back = lax.all_to_all(o, seq, split_axis=0, concat_axis=0, tiled=True)  21.2 us
    pallas_call x5, Pallas kernels, attend(): pl.pallas_call(functools.partial(attend_kernel, first=first, travels=trav...  20.6 us
    ppermute x1, starting transfers between devices, local(): came = lax.ppermute(send, 'c', SWAP)  3.62 us
    ppermute x1, starting transfers between devices, local(): came = lax.ppermute(away, 'c', SWAP)  3.33 us
    ppermute x1, starting transfers between devices, swap(): return [lax.ppermute(x, axis, SWAP) for x in chunks]  3.13 us
  transfers between devices with their start and end apart: 8, of which 5 were waited for; matrix products, arithmetic and copies ran while one was open for 0% of the time, Pallas kernels for 20%

profile of v7, /device:TPU:1, one launch (start us, length us, event | category | flops | bytes accessed | tf_op | source)
XLA Modules:
  0.0 117.6 jit_solution(1353736785616935140)
XLA Ops:
  0.0 1.2 %pack.3 = bf16[3,16,64,128]{3,2,1,0:T(8,128)(2,1)S(1)} custom-call(bf16[128,2048]{1,0:T(8,128)(2,1)} %bitcast.34, bf16[128,2048]{1,0:T(8,128)(2,1)} %bitcast.36, bf16[128,2048]{1,0:T(8,128)(2,1)} %bitcast.38), custom_call_target="tpu_custom_call" | custom-call | tf_op jit(solution)/shard_map/pack/pallas_call | solution.py:60
  1.2 3.3 %collective-permute-start = (bf16[3,16,64,128]{3,2,1,0:T(8,128)(2,1)S(1)}, bf16[3,16,64,128]{3,2,1,0:T(8,128)(2,1)S(1)}, u32[]{:S(2)}, u32[]{:S(2)}) collective-permute-start(bf16[3,16,64,128]{3,2,1,0:T(8,128)(2,1)S(1)} %pack.3), channel_id=1, source_target_pairs={{0,64},{64,0},{1,65},{65,1},{2,66},{66,2},{3,67},{67,3},{4,68},{68... | collective-permute-start | bytes 2359304 | tf_op jit(solution)/shard_map/ppermute | solution.py:319
  4.5 1.2 %pack.2.a_ref = bf16[2,1,16,3,64,128]{5,4,3,2,1,0:T(8,128)(2,1)S(1)} custom-call(bf16[128,2048]{1,0:T(8,128)(2,1)} %bitcast.35, bf16[128,2048]{1,0:T(8,128)(2,1)} %bitcast.37, bf16[128,2048]{1,0:T(8,128)(2,1)} %bitcast.39), custom_call_target="tpu_custom_call" | custom-call | tf_op jit(solution)/shard_map/pack/pallas_call | solution.py:60
  5.7 0.7 collective-permute-done.got_ref
  6.4 0.1 place.1.a_ref
  6.5 52.0 %all_to_all.10 = bf16[32,192,128]{2,1,0:T(8,128)(2,1)S(1)} all-to-all(bf16[32,192,128]{2,1,0:T(8,128)(2,1)S(1)} %bitcast.24), channel_id=1, replica_groups=mesh['xl'=2,'c'=2,'yv'=2,'yr'=2,'z'=8,'xh'=2] {'yv','z','xh'}, dimensions={0} | all-to-all | bytes 3145728 | tf_op jit(solution)/shard_map/all_to_all | solution.py:322
  58.5 0.1 slice.31.refs_1_
  58.6 3.1 %collective-permute-start.1 = (bf16[32,2,64,128]{3,2,1,0:T(8,128)(2,1)S(1)}, bf16[32,2,64,128]{3,2,1,0:T(8,128)(2,1)S(1)}, u32[]{:S(2)}, u32[]{:S(2)}) collective-permute-start(bf16[32,2,64,128]{3,2,1,0:T(8,128)(2,1)S(1)} %slice.31.refs_1_), channel_id=1, source_target_pairs={{0,64},{64,0},{1,65},{65,1},{2,66},{66,2},{3,67},{67,3},{4,68},{68... | collective-permute-start | bytes 3145736 | tf_op jit(solution)/shard_map/ppermute | solution.py:308
  61.7 0.1 slice.26
  61.8 0.4 collective-permute-start.3
  62.3 0.5 collective-permute-start.2
  62.8 1.2 %collective-permute-done.1.refs_2_ = bf16[32,2,64,128]{3,2,1,0:T(8,128)(2,1)S(1)} collective-permute-done((bf16[32,2,64,128]{3,2,1,0:T(8,128)(2,1)S(1)}, bf16[32,2,64,128]{3,2,1,0:T(8,128)(2,1)S(1)}, u32[]{:S(2)}, u32[]{:S(2)}) %collective-permute-start.1) | collective-permute-done | bytes 1048608 | tf_op jit(solution)/shard_map/ppermute | solution.py:308
  64.0 3.0 %attend.5 = (f32[8,64,128]{2,1,0:T(8,128)S(1)}, f32[4,128]{1,0:T(4,128)S(1)}, bf16[4096,128]{1,0:T(8,128)(2,1)S(1)}, bf16[4096,256]{1,0:T(8,128)(2,1)S(1)}) custom-call(bf16[8,64,128]{2,1,0:T(8,128)(2,1)S(1)} %get-tuple-element.55.refs_0_, bf16[32,2,64,128]{3,2,1,0:T(8,128)(2,1)S(1)} %slice.31.refs_1_, ...), custom_call_target="tpu_custom_call" | custom-call | tf_op jit(solution)/shard_map/attend/pallas_call | solution.py:165
  67.0 0.7 collective-permute-start.5
  67.7 2.6 %attend.6 = (f32[8,64,128]{2,1,0:T(8,128)S(1)}, f32[4,128]{1,0:T(4,128)S(1)}) custom-call(bf16[8,64,128]{2,1,0:T(8,128)(2,1)S(1)} %get-tuple-element.33.refs_0_, bf16[4096,128]{1,0:T(8,128)(2,1)S(1)} %get-tuple-element.34.refs_1_, bf16[4096,256]{1,0:T(8,128)(2,1)S(1)} %get-tuple-element.35.refs_2_), custom_call_target="tpu_custom_call" | custom-call | tf_op jit(solution)/shard_map/attend/pallas_call | solution.py:165
  70.3 0.0 collective-permute-done.2.refs_0_
  70.3 5.0 %attend.7 = bf16[17,64,128]{2,1,0:T(8,128)(2,1)S(1)} custom-call(bf16[16,64,128]{2,1,0:T(8,128)(2,1)S(1)} %collective-permute-done.2.refs_0_, bf16[4096,128]{1,0:T(8,128)(2,1)S(1)} %get-tuple-element.34.refs_1_, bf16[4096,256]{1,0:T(8,128)(2,1)S(1)} %get-tuple-element.35.refs_2_), custom_call_target="tpu_custom_call" | custom-call | tf_op jit(solution)/shard_map/attend/pallas_call | solution.py:165
  75.3 1.4 %collective-permute-start.4 = (bf16[17,64,128]{2,1,0:T(8,128)(2,1)S(1)}, bf16[17,64,128]{2,1,0:T(8,128)(2,1)S(1)}, u32[]{:S(2)}, u32[]{:S(2)}) collective-permute-start(bf16[17,64,128]{2,1,0:T(8,128)(2,1)S(1)} %attend.7), channel_id=1, source_target_pairs={{0,16},{16,0},{1,17},{17,1},{2,18},{18,2},{3,19},{19,3},{4,20},{20... | collective-permute-start | bytes 835592 | tf_op jit(solution)/shard_map/ppermute | solution.py:340
  76.7 0.0 collective-permute-done.5.refs_0_
  76.7 0.0 slice-start
  76.7 5.0 %attend.8 = bf16[17,64,128]{2,1,0:T(8,128)(2,1)S(1)} custom-call(bf16[16,64,128]{2,1,0:T(8,128)(2,1)S(1)} %collective-permute-done.5.refs_0_, bf16[4096,128]{1,0:T(8,128)(2,1)S(1)} %get-tuple-element.34.refs_1_, bf16[4096,256]{1,0:T(8,128)(2,1)S(1)} %get-tuple-element.35.refs_2_), custom_call_target="tpu_custom_call" | custom-call | tf_op jit(solution)/shard_map/attend/pallas_call | solution.py:165
  81.7 0.5 collective-permute-start.6
  82.2 0.1 collective-permute-done.4.refs_6_
  82.3 5.0 %attend.9 = (f32[16,64,128]{2,1,0:T(8,128)S(1)}, f32[8,128]{1,0:T(8,128)S(1)}) custom-call(bf16[16,64,128]{2,1,0:T(8,128)(2,1)S(1)} %slice_bitcast_fusion.refs_0_, bf16[4096,128]{1,0:T(8,128)(2,1)S(1)} %get-tuple-element.34.refs_1_, bf16[4096,256]{1,0:T(8,128)(2,1)S(1)} %get-tuple-element.35.refs_2_), custom_call_target="tpu_custom_call" | custom-call | tf_op jit(solution)/shard_map/attend/pallas_call | solution.py:165
  87.3 0.0 collective-permute-done.3.b_ref
  87.3 0.0 slice-start.1
  87.4 0.9 cross.2.c_ref
  88.3 0.6 collective-permute-done.6.refs_7_
  88.9 0.4 merge.1
  89.3 21.2 %all_to_all.11 = bf16[32,64,128]{2,1,0:T(8,128)(2,1)S(1)} all-to-all(bf16[32,64,128]{2,1,0:T(8,128)(2,1)S(1)} %merge.1), channel_id=1, replica_groups=mesh['xl'=2,'c'=2,'yv'=2,'yr'=2,'z'=8,'xh'=2] {'yv','z','xh'}, dimensions={0} | all-to-all | bytes 1048576 | tf_op jit(solution)/shard_map/all_to_all | solution.py:350
  110.5 0.1 add_send.1
  110.6 0.0 copy-start
  110.6 0.0 copy-start.1
  110.6 3.6 %collective-permute-start.7 = (bf16[1,16,64,128]{3,2,1,0:T(8,128)(2,1)S(1)}, bf16[1,16,64,128]{3,2,1,0:T(8,128)(2,1)S(1)}, u32[]{:S(2)}, u32[]{:S(2)}) collective-permute-start(bf16[1,16,64,128]{3,2,1,0:T(8,128)(2,1)S(1)} %add_send.1), channel_id=1, source_target_pairs={{0,64},{64,0},{1,65},{65,1},{2,66},{66,2},{3,67},{67,3},{4,68},{68... | collective-permute-start | bytes 786440 | tf_op jit(solution)/shard_map/ppermute | solution.py:354
  114.2 1.0 cross.3.keep_ref
  115.2 0.2 collective-permute-done.7.came_ref
  115.4 0.0 slice-done
  115.4 0.0 slice-done.1
  115.4 0.0 copy-done
  115.4 0.0 copy-done.1
  115.4 2.2 %project.1 = bf16[128,2048]{1,0:T(8,128)(2,1)} custom-call(bf16[1,16,64,128]{3,2,1,0:T(8,128)(2,1)S(1)} %cross.3.keep_ref, bf16[1,16,64,128]{3,2,1,0:T(8,128)(2,1)S(1)} %collective-permute-done.7.came_ref, bf16[2048,2048]{1,0:T(8,128)(2,1)S(1)} %bitcast.26, bf16[128,2048]{1,0:T(8,128)(2,1)S(1)} %bitcast.29, bf16[1,2048]{1,0:T(2,128)(2,1)S(1)} %copy-done.1), custom_call_target="tpu_custom_call" | custom-call | tf_op jit(solution)/shard_map/project/pallas_call | solution.py:292
  (4 shorter events, 0.1 us)
Async XLA Ops:
  1.2 5.2 %collective-permute-start = (bf16[3,16,64,128]{3,2,1,0:T(8,128)(2,1)S(1)}, bf16[3,16,64,128]{3,2,1,0:T(8,128)(2,1)S(1)}, u32[]{:S(2)}, u32[]{:S(2)}) collective-permute-start(bf16[3,16,64,128]{3,2,1,0:T(8,128)(2,1)S(1)} %pack.3), channel_id=1, source_target_pairs={{0,64},{64,0},{1,65},{65,1},{2,66},{66,2},{3,67},{67,3},{4,68},{68... | collective-permute-start | bytes 2359304 | tf_op jit(solution)/shard_map/ppermute | solution.py:319
  58.6 5.4 %collective-permute-start.1 = (bf16[32,2,64,128]{3,2,1,0:T(8,128)(2,1)S(1)}, bf16[32,2,64,128]{3,2,1,0:T(8,128)(2,1)S(1)}, u32[]{:S(2)}, u32[]{:S(2)}) collective-permute-start(bf16[32,2,64,128]{3,2,1,0:T(8,128)(2,1)S(1)} %slice.31.refs_1_), channel_id=1, source_target_pairs={{0,64},{64,0},{1,65},{65,1},{2,66},{66,2},{3,67},{67,3},{4,68},{68... | collective-permute-start | bytes 3145736 | tf_op jit(solution)/shard_map/ppermute | solution.py:308
  61.8 25.5 %collective-permute-start.3 = (bf16[2,1,16,2,64,128]{5,4,3,2,1,0:T(8,128)(2,1)S(1)}, bf16[2,1,16,2,64,128]{5,4,3,2,1,0:T(8,128)(2,1)S(1)}, u32[]{:S(2)}, u32[]{:S(2)}) collective-permute-start(bf16[2,1,16,2,64,128]{5,4,3,2,1,0:T(8,128)(2,1)S(1)} %slice.26), channel_id=1, source_target_pairs={{0,128},{128,0},{1,129},{129,1},{2,130},{130,2},{3,131},{131,3},{4... | collective-permute-start | bytes 3145736 | tf_op jit(solution)/shard_map/ppermute | solution.py:330
  62.3 8.0 %collective-permute-start.2 = (bf16[16,64,128]{2,1,0:T(8,128)(2,1)S(1)}, bf16[16,64,128]{2,1,0:T(8,128)(2,1)S(1)}, u32[]{:S(2)}, u32[]{:S(2)}) collective-permute-start(bf16[16,64,128]{2,1,0:T(8,128)(2,1)S(1)} %get-tuple-element.53), channel_id=1, source_target_pairs={{0,16},{16,0},{1,17},{17,1},{2,18},{18,2},{3,19},{19,3},{4,20},{20... | collective-permute-start | bytes 786440 | tf_op jit(solution)/shard_map/ppermute | solution.py:331
  67.0 9.7 %collective-permute-start.5 = (bf16[16,64,128]{2,1,0:T(8,128)(2,1)S(1)}, bf16[16,64,128]{2,1,0:T(8,128)(2,1)S(1)}, u32[]{:S(2)}, u32[]{:S(2)}) collective-permute-start(bf16[16,64,128]{2,1,0:T(8,128)(2,1)S(1)} %get-tuple-element.41), channel_id=1, source_target_pairs={{0,16},{16,0},{1,17},{17,1},{2,18},{18,2},{3,19},{19,3},{4,20},{20... | collective-permute-start | bytes 786440 | tf_op jit(solution)/shard_map/ppermute | solution.py:336
  75.3 7.0 %collective-permute-start.4 = (bf16[17,64,128]{2,1,0:T(8,128)(2,1)S(1)}, bf16[17,64,128]{2,1,0:T(8,128)(2,1)S(1)}, u32[]{:S(2)}, u32[]{:S(2)}) collective-permute-start(bf16[17,64,128]{2,1,0:T(8,128)(2,1)S(1)} %attend.7), channel_id=1, source_target_pairs={{0,16},{16,0},{1,17},{17,1},{2,18},{18,2},{3,19},{19,3},{4,20},{20... | collective-permute-start | bytes 835592 | tf_op jit(solution)/shard_map/ppermute | solution.py:340
  76.7 38.7 %slice-start = ((s8[8388608]{0:T(1024)(128)(4,1)}), s8[4194304]{0:T(1024)(128)(4,1)S(1)}, s32[]{:S(2)}) async-start(s8[8388608]{0:T(1024)(128)(4,1)} %bitcast.25), calls=%async_computation.2 | async-start | bytes 8388608
  81.7 7.2 %collective-permute-start.6 = (bf16[17,64,128]{2,1,0:T(8,128)(2,1)S(1)}, bf16[17,64,128]{2,1,0:T(8,128)(2,1)S(1)}, u32[]{:S(2)}, u32[]{:S(2)}) collective-permute-start(bf16[17,64,128]{2,1,0:T(8,128)(2,1)S(1)} %attend.8), channel_id=1, source_target_pairs={{0,16},{16,0},{1,17},{17,1},{2,18},{18,2},{3,19},{19,3},{4,20},{20... | collective-permute-start | bytes 835592 | tf_op jit(solution)/shard_map/ppermute | solution.py:343
  87.3 28.0 %slice-start.1 = ((s8[8388608]{0:T(1024)(128)(4,1)}), s8[4194304]{0:T(1024)(128)(4,1)S(1)}, s32[]{:S(2)}) async-start(s8[8388608]{0:T(1024)(128)(4,1)} %bitcast.25), calls=%async_computation.3 | async-start | bytes 8388608
  110.6 4.8 %copy-start = (bf16[1,128,2048]{2,1,0:T(8,128)(2,1)S(1)}, bf16[1,128,2048]{2,1,0:T(8,128)(2,1)}, u32[]{:S(2)}) copy-start(bf16[1,128,2048]{2,1,0:T(8,128)(2,1)} %param.6) | copy-start | bytes 1572868
  110.6 4.8 %copy-start.1 = (bf16[1,2048]{1,0:T(2,128)(2,1)S(1)}, bf16[1,2048]{1,0:T(2,128)(2,1)}, u32[]{:S(2)}) copy-start(bf16[1,2048]{1,0:T(2,128)(2,1)} %g_ref.1) | copy-start | bytes 12292
  110.6 4.8 %collective-permute-start.7 = (bf16[1,16,64,128]{3,2,1,0:T(8,128)(2,1)S(1)}, bf16[1,16,64,128]{3,2,1,0:T(8,128)(2,1)S(1)}, u32[]{:S(2)}, u32[]{:S(2)}) collective-permute-start(bf16[1,16,64,128]{3,2,1,0:T(8,128)(2,1)S(1)} %add_send.1), channel_id=1, source_target_pairs={{0,64},{64,0},{1,65},{65,1},{2,66},{66,2},{3,67},{67,3},{4,68},{68... | collective-permute-start | bytes 786440 | tf_op jit(solution)/shard_map/ppermute | solution.py:354

commit v8 on v7

--- a/solution.py
+++ b/solution.py
@@ -341,9 +341,9 @@
     q_in, mo1 = lax.optimization_barrier((mate_q2, mo1))
     (mo2,) = attend(q_in, kv, False, True)
     back2 = lax.ppermute(mo2, "yr", SWAP)
-    q_in, back1, mo2 = lax.optimization_barrier((qs[2], back1, mo2))
+    q_in, mo2 = lax.optimization_barrier((qs[2], mo2))
     o3, l3 = attend(q_in, kv, False, False)
-    other, o3 = lax.optimization_barrier((other, o3))
+    other, back1, o3 = lax.optimization_barrier((other, back1, o3))
     cross_send = cross(mine, other, None, True)
     back2, cross_send = lax.optimization_barrier((back2, cross_send))
     o = merge([(o1, l1), (o2, l2), (o3, l3)], [back1, back2])

time: 118 us -> 117 us (level)
  transfers between devices with their start and end apart: 8 -> 8, of which waited for: 5 -> 4; matrix products, arithmetic and copies ran while one was open for 0% -> 0% of each run, Pallas kernels for 20% -> 20%
where the time goes in v8:
time: 117 us
  blocking collectives  72.7 us (62%)
  Pallas kernels  27.6 us (24%)
  starting transfers between devices  13.8 us (12%)
  waiting for transfers between devices  2.89 us (2%)
    all_to_all x1, blocking collectives, local(): lax.all_to_all(mine.reshape(n, 3 * rows, HD), seq, split_axis=0, concat_a...  52 us
    all_to_all x1, blocking collectives, local(): back = lax.all_to_all(o, seq, split_axis=0, concat_axis=0, tiled=True)  20.6 us
    pallas_call x5, Pallas kernels, attend(): pl.pallas_call(functools.partial(attend_kernel, first=first, travels=trav...  20.6 us
    ppermute x1, starting transfers between devices, local(): came = lax.ppermute(send, 'c', SWAP)  3.89 us
    ppermute x1, starting transfers between devices, local(): came = lax.ppermute(away, 'c', SWAP)  3.33 us
    ppermute x1, starting transfers between devices, swap(): return [lax.ppermute(x, axis, SWAP) for x in chunks]  3.13 us
    pallas_call x2, Pallas kernels, pack(): pl.pallas_call(kernel, in_specs=[pl.BlockSpec(memory_space=pltpu.HBM)] *...  2.36 us
  transfers between devices with their start and end apart: 8, of which 4 were waited for; matrix products, arithmetic and copies ran while one was open for 0% of the time, Pallas kernels for 20%

profile of v8, /device:TPU:1, one launch (start us, length us, event | category | flops | bytes accessed | tf_op | source)
XLA Modules:
  0.0 117.3 jit_solution(7267067910469640127)
XLA Ops:
  0.0 1.2 %pack.3 = bf16[3,16,64,128]{3,2,1,0:T(8,128)(2,1)S(1)} custom-call(bf16[128,2048]{1,0:T(8,128)(2,1)} %bitcast.34, bf16[128,2048]{1,0:T(8,128)(2,1)} %bitcast.36, bf16[128,2048]{1,0:T(8,128)(2,1)} %bitcast.38), custom_call_target="tpu_custom_call" | custom-call | tf_op jit(solution)/shard_map/pack/pallas_call | solution.py:60
  1.2 3.3 %collective-permute-start = (bf16[3,16,64,128]{3,2,1,0:T(8,128)(2,1)S(1)}, bf16[3,16,64,128]{3,2,1,0:T(8,128)(2,1)S(1)}, u32[]{:S(2)}, u32[]{:S(2)}) collective-permute-start(bf16[3,16,64,128]{3,2,1,0:T(8,128)(2,1)S(1)} %pack.3), channel_id=1, source_target_pairs={{0,64},{64,0},{1,65},{65,1},{2,66},{66,2},{3,67},{67,3},{4,68},{68... | collective-permute-start | bytes 2359304 | tf_op jit(solution)/shard_map/ppermute | solution.py:319
  4.5 1.2 %pack.2.a_ref = bf16[2,1,16,3,64,128]{5,4,3,2,1,0:T(8,128)(2,1)S(1)} custom-call(bf16[128,2048]{1,0:T(8,128)(2,1)} %bitcast.35, bf16[128,2048]{1,0:T(8,128)(2,1)} %bitcast.37, bf16[128,2048]{1,0:T(8,128)(2,1)} %bitcast.39), custom_call_target="tpu_custom_call" | custom-call | tf_op jit(solution)/shard_map/pack/pallas_call | solution.py:60
  5.7 0.7 collective-permute-done.got_ref
  6.4 0.1 place.1.a_ref
  6.5 52.0 %all_to_all.10 = bf16[32,192,128]{2,1,0:T(8,128)(2,1)S(1)} all-to-all(bf16[32,192,128]{2,1,0:T(8,128)(2,1)S(1)} %bitcast.24), channel_id=1, replica_groups=mesh['xl'=2,'c'=2,'yv'=2,'yr'=2,'z'=8,'xh'=2] {'yv','z','xh'}, dimensions={0} | all-to-all | bytes 3145728 | tf_op jit(solution)/shard_map/all_to_all | solution.py:322
  58.5 0.1 slice.31.refs_1_
  58.6 3.1 %collective-permute-start.1 = (bf16[32,2,64,128]{3,2,1,0:T(8,128)(2,1)S(1)}, bf16[32,2,64,128]{3,2,1,0:T(8,128)(2,1)S(1)}, u32[]{:S(2)}, u32[]{:S(2)}) collective-permute-start(bf16[32,2,64,128]{3,2,1,0:T(8,128)(2,1)S(1)} %slice.31.refs_1_), channel_id=1, source_target_pairs={{0,64},{64,0},{1,65},{65,1},{2,66},{66,2},{3,67},{67,3},{4,68},{68... | collective-permute-start | bytes 3145736 | tf_op jit(solution)/shard_map/ppermute | solution.py:308
  61.7 0.1 slice.26
  61.8 0.4 collective-permute-start.3
  62.3 0.5 collective-permute-start.2
  62.8 1.2 %collective-permute-done.1.refs_2_ = bf16[32,2,64,128]{3,2,1,0:T(8,128)(2,1)S(1)} collective-permute-done((bf16[32,2,64,128]{3,2,1,0:T(8,128)(2,1)S(1)}, bf16[32,2,64,128]{3,2,1,0:T(8,128)(2,1)S(1)}, u32[]{:S(2)}, u32[]{:S(2)}) %collective-permute-start.1) | collective-permute-done | bytes 1048608 | tf_op jit(solution)/shard_map/ppermute | solution.py:308
  64.0 3.0 %attend.5 = (f32[8,64,128]{2,1,0:T(8,128)S(1)}, f32[4,128]{1,0:T(4,128)S(1)}, bf16[4096,128]{1,0:T(8,128)(2,1)S(1)}, bf16[4096,256]{1,0:T(8,128)(2,1)S(1)}) custom-call(bf16[8,64,128]{2,1,0:T(8,128)(2,1)S(1)} %get-tuple-element.55.refs_0_, bf16[32,2,64,128]{3,2,1,0:T(8,128)(2,1)S(1)} %slice.31.refs_1_, ...), custom_call_target="tpu_custom_call" | custom-call | tf_op jit(solution)/shard_map/attend/pallas_call | solution.py:165
  67.0 0.7 collective-permute-start.5
  67.7 2.6 %attend.6 = (f32[8,64,128]{2,1,0:T(8,128)S(1)}, f32[4,128]{1,0:T(4,128)S(1)}) custom-call(bf16[8,64,128]{2,1,0:T(8,128)(2,1)S(1)} %get-tuple-element.33.refs_0_, bf16[4096,128]{1,0:T(8,128)(2,1)S(1)} %get-tuple-element.34.refs_1_, bf16[4096,256]{1,0:T(8,128)(2,1)S(1)} %get-tuple-element.35.refs_2_), custom_call_target="tpu_custom_call" | custom-call | tf_op jit(solution)/shard_map/attend/pallas_call | solution.py:165
  70.3 0.0 collective-permute-done.2.refs_0_
  70.3 5.0 %attend.7 = bf16[17,64,128]{2,1,0:T(8,128)(2,1)S(1)} custom-call(bf16[16,64,128]{2,1,0:T(8,128)(2,1)S(1)} %collective-permute-done.2.refs_0_, bf16[4096,128]{1,0:T(8,128)(2,1)S(1)} %get-tuple-element.34.refs_1_, bf16[4096,256]{1,0:T(8,128)(2,1)S(1)} %get-tuple-element.35.refs_2_), custom_call_target="tpu_custom_call" | custom-call | tf_op jit(solution)/shard_map/attend/pallas_call | solution.py:165
  75.3 1.4 %collective-permute-start.4 = (bf16[17,64,128]{2,1,0:T(8,128)(2,1)S(1)}, bf16[17,64,128]{2,1,0:T(8,128)(2,1)S(1)}, u32[]{:S(2)}, u32[]{:S(2)}) collective-permute-start(bf16[17,64,128]{2,1,0:T(8,128)(2,1)S(1)} %attend.7), channel_id=1, source_target_pairs={{0,16},{16,0},{1,17},{17,1},{2,18},{18,2},{3,19},{19,3},{4,20},{20... | collective-permute-start | bytes 835592 | tf_op jit(solution)/shard_map/ppermute | solution.py:340
  76.7 0.0 collective-permute-done.5.refs_0_
  76.7 0.0 slice-start
  76.7 5.0 %attend.8 = bf16[17,64,128]{2,1,0:T(8,128)(2,1)S(1)} custom-call(bf16[16,64,128]{2,1,0:T(8,128)(2,1)S(1)} %collective-permute-done.5.refs_0_, bf16[4096,128]{1,0:T(8,128)(2,1)S(1)} %get-tuple-element.34.refs_1_, bf16[4096,256]{1,0:T(8,128)(2,1)S(1)} %get-tuple-element.35.refs_2_), custom_call_target="tpu_custom_call" | custom-call | tf_op jit(solution)/shard_map/attend/pallas_call | solution.py:165
  81.7 0.5 collective-permute-start.6
  82.2 5.0 %attend.9 = (f32[16,64,128]{2,1,0:T(8,128)S(1)}, f32[8,128]{1,0:T(8,128)S(1)}) custom-call(bf16[16,64,128]{2,1,0:T(8,128)(2,1)S(1)} %slice_bitcast_fusion.refs_0_, bf16[4096,128]{1,0:T(8,128)(2,1)S(1)} %get-tuple-element.34.refs_1_, bf16[4096,256]{1,0:T(8,128)(2,1)S(1)} %get-tuple-element.35.refs_2_), custom_call_target="tpu_custom_call" | custom-call | tf_op jit(solution)/shard_map/attend/pallas_call | solution.py:165
  87.2 0.0 collective-permute-done.3.b_ref
  87.2 0.0 collective-permute-done.4.refs_6_
  87.2 0.0 slice-start.1
  87.3 0.9 cross.2.c_ref
  88.2 0.7 collective-permute-done.6.refs_7_
  88.9 0.4 merge.1
  89.3 20.6 %all_to_all.11 = bf16[32,64,128]{2,1,0:T(8,128)(2,1)S(1)} all-to-all(bf16[32,64,128]{2,1,0:T(8,128)(2,1)S(1)} %merge.1), channel_id=1, replica_groups=mesh['xl'=2,'c'=2,'yv'=2,'yr'=2,'z'=8,'xh'=2] {'yv','z','xh'}, dimensions={0} | all-to-all | bytes 1048576 | tf_op jit(solution)/shard_map/all_to_all | solution.py:350
  109.9 0.1 add_send.1
  110.0 0.0 copy-start
  110.0 0.0 copy-start.1
  110.0 3.9 %collective-permute-start.7 = (bf16[1,16,64,128]{3,2,1,0:T(8,128)(2,1)S(1)}, bf16[1,16,64,128]{3,2,1,0:T(8,128)(2,1)S(1)}, u32[]{:S(2)}, u32[]{:S(2)}) collective-permute-start(bf16[1,16,64,128]{3,2,1,0:T(8,128)(2,1)S(1)} %add_send.1), channel_id=1, source_target_pairs={{0,64},{64,0},{1,65},{65,1},{2,66},{66,2},{3,67},{67,3},{4,68},{68... | collective-permute-start | bytes 786440 | tf_op jit(solution)/shard_map/ppermute | solution.py:354
  113.9 1.0 cross.3.keep_ref
  114.9 0.2 collective-permute-done.7.came_ref
  115.0 0.0 slice-done
  115.1 0.0 slice-done.1
  115.1 0.0 copy-done
  115.1 0.0 copy-done.1
  115.1 2.2 %project.1 = bf16[128,2048]{1,0:T(8,128)(2,1)} custom-call(bf16[1,16,64,128]{3,2,1,0:T(8,128)(2,1)S(1)} %cross.3.keep_ref, bf16[1,16,64,128]{3,2,1,0:T(8,128)(2,1)S(1)} %collective-permute-done.7.came_ref, bf16[2048,2048]{1,0:T(8,128)(2,1)S(1)} %bitcast.26, bf16[128,2048]{1,0:T(8,128)(2,1)S(1)} %bitcast.29, bf16[1,2048]{1,0:T(2,128)(2,1)S(1)} %copy-done.1), custom_call_target="tpu_custom_call" | custom-call | tf_op jit(solution)/shard_map/project/pallas_call | solution.py:292
  (4 shorter events, 0.1 us)
Async XLA Ops:
  1.2 5.2 %collective-permute-start = (bf16[3,16,64,128]{3,2,1,0:T(8,128)(2,1)S(1)}, bf16[3,16,64,128]{3,2,1,0:T(8,128)(2,1)S(1)}, u32[]{:S(2)}, u32[]{:S(2)}) collective-permute-start(bf16[3,16,64,128]{3,2,1,0:T(8,128)(2,1)S(1)} %pack.3), channel_id=1, source_target_pairs={{0,64},{64,0},{1,65},{65,1},{2,66},{66,2},{3,67},{67,3},{4,68},{68... | collective-permute-start | bytes 2359304 | tf_op jit(solution)/shard_map/ppermute | solution.py:319
  58.6 5.4 %collective-permute-start.1 = (bf16[32,2,64,128]{3,2,1,0:T(8,128)(2,1)S(1)}, bf16[32,2,64,128]{3,2,1,0:T(8,128)(2,1)S(1)}, u32[]{:S(2)}, u32[]{:S(2)}) collective-permute-start(bf16[32,2,64,128]{3,2,1,0:T(8,128)(2,1)S(1)} %slice.31.refs_1_), channel_id=1, source_target_pairs={{0,64},{64,0},{1,65},{65,1},{2,66},{66,2},{3,67},{67,3},{4,68},{68... | collective-permute-start | bytes 3145736 | tf_op jit(solution)/shard_map/ppermute | solution.py:308
  61.8 25.4 %collective-permute-start.3 = (bf16[2,1,16,2,64,128]{5,4,3,2,1,0:T(8,128)(2,1)S(1)}, bf16[2,1,16,2,64,128]{5,4,3,2,1,0:T(8,128)(2,1)S(1)}, u32[]{:S(2)}, u32[]{:S(2)}) collective-permute-start(bf16[2,1,16,2,64,128]{5,4,3,2,1,0:T(8,128)(2,1)S(1)} %slice.26), channel_id=1, source_target_pairs={{0,128},{128,0},{1,129},{129,1},{2,130},{130,2},{3,131},{131,3},{4... | collective-permute-start | bytes 3145736 | tf_op jit(solution)/shard_map/ppermute | solution.py:330
  62.3 8.0 %collective-permute-start.2 = (bf16[16,64,128]{2,1,0:T(8,128)(2,1)S(1)}, bf16[16,64,128]{2,1,0:T(8,128)(2,1)S(1)}, u32[]{:S(2)}, u32[]{:S(2)}) collective-permute-start(bf16[16,64,128]{2,1,0:T(8,128)(2,1)S(1)} %get-tuple-element.53), channel_id=1, source_target_pairs={{0,16},{16,0},{1,17},{17,1},{2,18},{18,2},{3,19},{19,3},{4,20},{20... | collective-permute-start | bytes 786440 | tf_op jit(solution)/shard_map/ppermute | solution.py:331
  67.0 9.7 %collective-permute-start.5 = (bf16[16,64,128]{2,1,0:T(8,128)(2,1)S(1)}, bf16[16,64,128]{2,1,0:T(8,128)(2,1)S(1)}, u32[]{:S(2)}, u32[]{:S(2)}) collective-permute-start(bf16[16,64,128]{2,1,0:T(8,128)(2,1)S(1)} %get-tuple-element.41), channel_id=1, source_target_pairs={{0,16},{16,0},{1,17},{17,1},{2,18},{18,2},{3,19},{19,3},{4,20},{20... | collective-permute-start | bytes 786440 | tf_op jit(solution)/shard_map/ppermute | solution.py:336
  75.3 11.9 %collective-permute-start.4 = (bf16[17,64,128]{2,1,0:T(8,128)(2,1)S(1)}, bf16[17,64,128]{2,1,0:T(8,128)(2,1)S(1)}, u32[]{:S(2)}, u32[]{:S(2)}) collective-permute-start(bf16[17,64,128]{2,1,0:T(8,128)(2,1)S(1)} %attend.7), channel_id=1, source_target_pairs={{0,16},{16,0},{1,17},{17,1},{2,18},{18,2},{3,19},{19,3},{4,20},{20... | collective-permute-start | bytes 835592 | tf_op jit(solution)/shard_map/ppermute | solution.py:340
  76.7 38.4 %slice-start = ((s8[8388608]{0:T(1024)(128)(4,1)}), s8[4194304]{0:T(1024)(128)(4,1)S(1)}, s32[]{:S(2)}) async-start(s8[8388608]{0:T(1024)(128)(4,1)} %bitcast.25), calls=%async_computation.2 | async-start | bytes 8388608
  81.7 7.2 %collective-permute-start.6 = (bf16[17,64,128]{2,1,0:T(8,128)(2,1)S(1)}, bf16[17,64,128]{2,1,0:T(8,128)(2,1)S(1)}, u32[]{:S(2)}, u32[]{:S(2)}) collective-permute-start(bf16[17,64,128]{2,1,0:T(8,128)(2,1)S(1)} %attend.8), channel_id=1, source_target_pairs={{0,16},{16,0},{1,17},{17,1},{2,18},{18,2},{3,19},{19,3},{4,20},{20... | collective-permute-start | bytes 835592 | tf_op jit(solution)/shard_map/ppermute | solution.py:343
  87.2 27.8 %slice-start.1 = ((s8[8388608]{0:T(1024)(128)(4,1)}), s8[4194304]{0:T(1024)(128)(4,1)S(1)}, s32[]{:S(2)}) async-start(s8[8388608]{0:T(1024)(128)(4,1)} %bitcast.25), calls=%async_computation.3 | async-start | bytes 8388608
  110.0 5.1 %copy-start = (bf16[1,128,2048]{2,1,0:T(8,128)(2,1)S(1)}, bf16[1,128,2048]{2,1,0:T(8,128)(2,1)}, u32[]{:S(2)}) copy-start(bf16[1,128,2048]{2,1,0:T(8,128)(2,1)} %param.6) | copy-start | bytes 1572868
  110.0 5.1 %copy-start.1 = (bf16[1,2048]{1,0:T(2,128)(2,1)S(1)}, bf16[1,2048]{1,0:T(2,128)(2,1)}, u32[]{:S(2)}) copy-start(bf16[1,2048]{1,0:T(2,128)(2,1)} %g_ref.1) | copy-start | bytes 12292
  110.0 5.1 %collective-permute-start.7 = (bf16[1,16,64,128]{3,2,1,0:T(8,128)(2,1)S(1)}, bf16[1,16,64,128]{3,2,1,0:T(8,128)(2,1)S(1)}, u32[]{:S(2)}, u32[]{:S(2)}) collective-permute-start(bf16[1,16,64,128]{3,2,1,0:T(8,128)(2,1)S(1)} %add_send.1), channel_id=1, source_target_pairs={{0,64},{64,0},{1,65},{65,1},{2,66},{66,2},{3,67},{67,3},{4,68},{68... | collective-permute-start | bytes 786440 | tf_op jit(solution)/shard_map/ppermute | solution.py:354
